TPU v7x, 32 devices: a whole 2x2x4 slice. The times are simulated.
32 devices in a mesh: row: 8 (over z, y), col: 4 (over x, core).
Axes of the slice: x: 2, y: 2, z: 4, core: 2. Of those that a mesh axis runs over, the one named last changes fastest.
Arguments:
- image_tokens: bfloat16 [51200, 768], P(('row', 'col')), may hold values from -9 to 9
- image_norm_gain: float32 [2, 768], replicated, may hold values from 0.5 to 1.5
- image_norm_bias: float32 [2, 768], replicated, may hold values from -1.75 to 1.75
- image_qkv: bfloat16 [768, 2304], P('col'), may hold values from -0.21875 to 0.21875
- image_out: bfloat16 [768, 768], P('col'), may hold values from -0.625 to 0.625
- image_up: bfloat16 [768, 3072], P('col'), may hold values from -0.21875 to 0.21875
- image_down: bfloat16 [3072, 768], P('col'), may hold values from -0.15625 to 0.15625
- text_tokens: bfloat16 [16384, 768], P(('row', 'col')), may hold values from -6 to 6
- text_lengths: int32 [1024], P(('row', 'col')), may hold values from 4 to 16, as said below
- norm1_gain: float32 [768], replicated, may hold values from 0.5 to 1.5
- norm1_bias: float32 [768], replicated, may hold values from -1.75 to 1.75
- norm2_gain: float32 [768], replicated, may hold values from 0.5 to 1.5
- norm2_bias: float32 [768], replicated, may hold values from -1.75 to 1.75
- text_qkv: bfloat16 [768, 2304], replicated, may hold values from -0.21875 to 0.21875
- text_out: bfloat16 [768, 768], replicated, may hold values from -0.625 to 0.625
- text_up: bfloat16 [768, 3072], replicated, may hold values from -0.21875 to 0.21875
- text_down: bfloat16 [3072, 768], replicated, may hold values from -0.15625 to 0.15625
- text_proj: bfloat16 [768, 768], replicated, may hold values from -0.21875 to 0.21875
Outputs:
- mean_loss: float32 [], replicated
- text_hidden: bfloat16 [16384, 768], P(('row', 'col'))
- text_input_grad: bfloat16 [16384, 768], P(('row', 'col'))
- grad_norm1_gain: float32 [768], replicated
- grad_norm1_bias: float32 [768], replicated
- grad_norm2_gain: float32 [768], replicated
- grad_norm2_bias: float32 [768], replicated
- grad_qkv: float32 [768, 2304], P('row', 'col')
- grad_out: float32 [768, 768], P('row', 'col')
- grad_up: float32 [768, 3072], P('row', 'col')
- grad_down: float32 [3072, 768], P('row', 'col')
- grad_proj: float32 [768, 768], P('row', 'col')
Inputs may be any that keep to these rules, and one draw needn't show every extreme that they name: Caption n's true tokens are its first text_lengths[n] slots; some caption has 16 and some has 4.
All inputs are finite; a program needn't handle non-finite values.
Results may differ from a plain program's by a relative error of at most 0.015.
Values may be sent and summed in bfloat16 or wider, within the bound.
A program may use at most 256 MiB of HBM per device.

v0:
```python
import jax
import jax.numpy as jnp
from jax import lax
from jax.sharding import PartitionSpec as P

HEADS = 12
IMG_TOK = 50


norm_eps = 1e-06
logit_scale = 50.0
masked_score = -1e30


def merged(x, axis, combine):
    everything = lax.all_gather(x, axis)
    initial = everything[0]

    def lap(k, so_far):
        return combine(so_far, everything[k])

    return lax.fori_loop(1, lax.axis_size(axis), lap, initial)


def layer_norm(row_data, gain_vec, bias_vec):
    row_mean = jnp.mean(row_data, axis=-1, keepdims=True)
    centered = row_data - row_mean
    variance = jnp.mean(centered * centered, axis=-1, keepdims=True)
    return centered * lax.rsqrt(variance + norm_eps) * gain_vec + bias_vec


def unit_rows(row_data):
    return row_data * lax.rsqrt(jnp.sum(row_data * row_data, axis=-1, keepdims=True) + norm_eps)


def exact_gelu(pre_act):
    return jax.nn.gelu(pre_act, approximate=False)


def split_heads(united_qkv, groups, length):
    model_width = united_qkv.shape[1] // 3
    head_parts = []
    for part_index in range(3):
        piece_bf = united_qkv[:, part_index * model_width : (part_index + 1) * model_width].astype(
            jnp.bfloat16
        )
        head_parts.append(piece_bf.reshape(groups, length, HEADS, model_width // HEADS))
    return head_parts


def head_scores(query_heads, key_heads, valid_keys):
    factor = query_heads.shape[-1] ** (-0.5)
    scores = (
        jnp.einsum("gqhe,gkhe->ghqk", query_heads, key_heads, preferred_element_type=jnp.float32)
        * factor
    )
    return jnp.where(valid_keys[:, None, None, :], scores, masked_score)


def attend(query_heads, key_heads, value_heads, valid_keys):
    scores = head_scores(query_heads, key_heads, valid_keys)
    totals = jax.nn.logsumexp(scores, axis=-1, keepdims=True)
    prob_low = jnp.exp(scores - totals).astype(jnp.bfloat16)
    mixed_heads = jnp.einsum(
        "ghqk,gkhe->gqhe", prob_low, value_heads, preferred_element_type=jnp.float32
    )
    return (mixed_heads.astype(jnp.bfloat16), totals)


def embed_images(image_tokens, norm_gains, norm_biases, w_qkv, w_out, w_up, w_down):
    model_width = image_tokens.shape[1]
    images = image_tokens.shape[0] // IMG_TOK
    hidden_in = image_tokens.astype(jnp.float32)
    normed1 = layer_norm(hidden_in, norm_gains[0], norm_biases[0]).astype(jnp.bfloat16)
    united_qkv = jnp.dot(normed1, w_qkv, preferred_element_type=jnp.float32)
    query_heads, key_heads, value_heads = split_heads(united_qkv, images, IMG_TOK)
    valid_keys = jnp.ones((images, IMG_TOK), dtype=bool)
    mixed_heads, _ = attend(query_heads, key_heads, value_heads, valid_keys)
    hidden_mid = hidden_in + jnp.dot(
        mixed_heads.reshape(-1, model_width), w_out, preferred_element_type=jnp.float32
    )
    normed2 = layer_norm(hidden_mid, norm_gains[1], norm_biases[1]).astype(jnp.bfloat16)
    inner_act = exact_gelu(jnp.dot(normed2, w_up, preferred_element_type=jnp.float32)).astype(
        jnp.bfloat16
    )
    hidden_out = hidden_mid + jnp.dot(inner_act, w_down, preferred_element_type=jnp.float32)
    pooled = jnp.mean(hidden_out.reshape(images, IMG_TOK, model_width), axis=1)
    return unit_rows(pooled).astype(jnp.bfloat16)


def merge_totals(former, latter):
    return jnp.logaddexp(former, latter)


def grid_blocks(matrix, row_parts, col_parts):
    height, breadth = matrix.shape
    shaped = matrix.reshape(row_parts, height // row_parts, col_parts, breadth // col_parts)
    return shaped.transpose(0, 2, 1, 3).reshape(
        row_parts * col_parts, height // row_parts, breadth // col_parts
    )


def body(
    image_tokens,
    image_norm_gain,
    image_norm_bias,
    image_qkv,
    image_out,
    image_up,
    image_down,
    text_tokens,
    text_lengths,
    norm1_gain,
    norm1_bias,
    norm2_gain,
    norm2_bias,
    text_qkv,
    text_out,
    text_up,
    text_down,
    text_proj,
):
    model_width = text_tokens.shape[1]
    captions = text_lengths.shape[0]
    length = text_tokens.shape[0] // captions
    row_count = lax.axis_size("row")
    col_count = lax.axis_size("col")
    full_qkv, full_out, full_up, full_down = (
        lax.all_gather(image_qkv, "col", axis=0, tiled=True),
        lax.all_gather(image_out, "col", axis=0, tiled=True),
        lax.all_gather(image_up, "col", axis=0, tiled=True),
        lax.all_gather(image_down, "col", axis=0, tiled=True),
    )
    image_embed = embed_images(
        image_tokens, image_norm_gain, image_norm_bias, full_qkv, full_out, full_up, full_down
    )
    image_rows = lax.all_gather(image_embed, "col", axis=0, tiled=True)
    positions = lax.broadcasted_iota(jnp.int32, (captions, length), 1)
    valid_keys = positions < text_lengths[:, None]
    pool_weight = valid_keys.astype(jnp.float32) / text_lengths[:, None].astype(jnp.float32)
    hidden_in = text_tokens.astype(jnp.float32)
    normed1 = layer_norm(hidden_in, norm1_gain, norm1_bias).astype(jnp.bfloat16)
    united_qkv = jnp.dot(normed1, text_qkv, preferred_element_type=jnp.float32)
    query_heads, key_heads, value_heads = split_heads(united_qkv, captions, length)
    mixed_heads, totals = attend(query_heads, key_heads, value_heads, valid_keys)
    mixed_rows = mixed_heads.reshape(-1, model_width)
    hidden_mid = hidden_in + jnp.dot(mixed_rows, text_out, preferred_element_type=jnp.float32)
    normed2 = layer_norm(hidden_mid, norm2_gain, norm2_bias).astype(jnp.bfloat16)
    pre_act = jnp.dot(normed2, text_up, preferred_element_type=jnp.float32)
    inner_act = exact_gelu(pre_act).astype(jnp.bfloat16)
    state_out = hidden_mid + jnp.dot(inner_act, text_down, preferred_element_type=jnp.float32)
    text_hidden = state_out.astype(jnp.bfloat16)
    pooled = jnp.sum(
        state_out.reshape(captions, length, model_width) * pool_weight[:, :, None], axis=1
    ).astype(jnp.bfloat16)
    projected = jnp.dot(pooled, text_proj, preferred_element_type=jnp.float32)
    text_unit, unit_back = jax.vjp(unit_rows, projected)
    text_embed = text_unit.astype(jnp.bfloat16)
    text_cols = lax.all_gather(text_embed, "row", axis=0, tiled=True)
    similarity = logit_scale * jnp.einsum(
        "id,jd->ij", image_rows, text_cols, preferred_element_type=jnp.float32
    )
    row_lse = merged(jax.nn.logsumexp(similarity, axis=1), "col", merge_totals)
    col_lse = merged(jax.nn.logsumexp(similarity, axis=0), "row", merge_totals)
    own_rows = lax.dynamic_slice_in_dim(row_lse, lax.axis_index("col") * captions, captions)
    own_cols = lax.dynamic_slice_in_dim(col_lse, lax.axis_index("row") * captions, captions)
    image_own = image_embed.astype(jnp.float32)
    positives = logit_scale * jnp.sum(image_own * text_embed.astype(jnp.float32), axis=1)
    loss_part = 0.5 * jnp.sum(own_rows + own_cols - 2.0 * positives)
    sim_grad = (
        0.5 * (jnp.exp(similarity - row_lse[:, None]) + jnp.exp(similarity - col_lse[None, :]))
    ).astype(jnp.bfloat16)
    embed_grad = (
        lax.psum_scatter(
            logit_scale
            * jnp.einsum("ij,id->jd", sim_grad, image_rows, preferred_element_type=jnp.float32),
            "row",
            scatter_dimension=0,
            tiled=True,
        )
        - logit_scale * image_own
    )
    proj_grad = unit_back(embed_grad)[0].astype(jnp.bfloat16)
    grad_proj = jnp.einsum("nd,ne->de", pooled, proj_grad, preferred_element_type=jnp.float32)
    pooled_grad = jnp.einsum("ne,de->nd", proj_grad, text_proj, preferred_element_type=jnp.float32)
    state_grad = (pool_weight[:, :, None] * pooled_grad[:, None, :]).reshape(-1, model_width)
    branch_grad = state_grad.astype(jnp.bfloat16)
    grad_down = jnp.einsum("tf,td->fd", inner_act, branch_grad, preferred_element_type=jnp.float32)
    inner_grad = jnp.einsum("td,fd->tf", branch_grad, text_down, preferred_element_type=jnp.float32)
    _, gelu_back = jax.vjp(exact_gelu, pre_act)
    pre_grad = gelu_back(inner_grad)[0].astype(jnp.bfloat16)
    grad_up = jnp.einsum("td,tf->df", normed2, pre_grad, preferred_element_type=jnp.float32)
    normed2_grad = jnp.einsum("tf,df->td", pre_grad, text_up, preferred_element_type=jnp.float32)
    _, norm2_back = jax.vjp(layer_norm, hidden_mid, norm2_gain, norm2_bias)
    mid_part, gain2_grad, bias2_grad = norm2_back(normed2_grad)
    mid_grad = state_grad + mid_part
    out_grad = mid_grad.astype(jnp.bfloat16)
    grad_out = jnp.einsum("td,te->de", mixed_rows, out_grad, preferred_element_type=jnp.float32)
    mixed_grad = jnp.einsum("te,de->td", out_grad, text_out, preferred_element_type=jnp.float32)
    mixed_grad = mixed_grad.astype(jnp.bfloat16).reshape(captions, length, HEADS, -1)
    scores = head_scores(query_heads, key_heads, valid_keys)
    prob_full = jnp.exp(scores - totals)
    prob_grad = jnp.einsum(
        "gqhe,gkhe->ghqk", mixed_grad, value_heads, preferred_element_type=jnp.float32
    )
    score_grad = (
        prob_full * (prob_grad - jnp.sum(prob_grad * prob_full, axis=-1, keepdims=True))
    ).astype(jnp.bfloat16)
    factor = query_heads.shape[-1] ** (-0.5)
    query_grad = (
        jnp.einsum("ghqk,gkhe->gqhe", score_grad, key_heads, preferred_element_type=jnp.float32)
        * factor
    )
    key_grad = (
        jnp.einsum("ghqk,gqhe->gkhe", score_grad, query_heads, preferred_element_type=jnp.float32)
        * factor
    )
    value_grad = jnp.einsum(
        "ghqk,gqhe->gkhe",
        prob_full.astype(jnp.bfloat16),
        mixed_grad,
        preferred_element_type=jnp.float32,
    )
    heads_grad = jnp.concatenate(
        [
            query_grad.reshape(-1, model_width),
            key_grad.reshape(-1, model_width),
            value_grad.reshape(-1, model_width),
        ],
        axis=1,
    ).astype(jnp.bfloat16)
    grad_qkv = jnp.einsum("td,te->de", normed1, heads_grad, preferred_element_type=jnp.float32)
    normed1_grad = jnp.einsum("te,de->td", heads_grad, text_qkv, preferred_element_type=jnp.float32)
    _, norm1_back = jax.vjp(layer_norm, hidden_in, norm1_gain, norm1_bias)
    input_part, gain1_grad, bias1_grad = norm1_back(normed1_grad)
    text_input_grad = (mid_grad + input_part).astype(jnp.bfloat16)
    weight_grads = (grad_qkv, grad_out, grad_up, grad_down, grad_proj)
    blocked = tuple((grid_blocks(matrix, row_count, col_count) for matrix in weight_grads))
    summed = lax.psum_scatter(blocked, ("row", "col"), scatter_dimension=0, tiled=True)
    shards = tuple((block_sum[0] for block_sum in summed))
    loss_total, gain1_sum, bias1_sum, gain2_sum, bias2_sum = lax.psum(
        (loss_part, gain1_grad, bias1_grad, gain2_grad, bias2_grad), ("row", "col")
    )
    mean_loss = loss_total / (captions * row_count * col_count)
    return (
        mean_loss,
        text_hidden,
        text_input_grad,
        gain1_sum,
        bias1_sum,
        gain2_sum,
        bias2_sum,
        shards[0],
        shards[1],
        shards[2],
        shards[3],
        shards[4],
    )


def solution(mesh):
    in_specs = (
        P(("row", "col"), None),
        P(),
        P(),
        P("col", None),
        P("col", None),
        P("col", None),
        P("col", None),
        P(("row", "col"), None),
        P(("row", "col")),
        P(),
        P(),
        P(),
        P(),
        P(),
        P(),
        P(),
        P(),
        P(),
    )
    out_specs = (
        P(),
        P(("row", "col"), None),
        P(("row", "col"), None),
        P(),
        P(),
        P(),
        P(),
        P("row", "col"),
        P("row", "col"),
        P("row", "col"),
        P("row", "col"),
        P("row", "col"),
    )
    return jax.shard_map(body, mesh=mesh, in_specs=in_specs, out_specs=out_specs, check_vma=False)
```

profile of v0, /device:TPU:0, one launch (start us, length us, event | category | flops | bytes accessed | tf_op | source)
XLA Modules:
  0.0 1053.0 jit_solution(7241844781892209419)
XLA Ops:
  40.7 3.8 fusion.86
  46.4 4.3 reshape.366
  55.0 17.5 %fusion.15 = (f32[512,3072]{1,0:T(8,128)S(1)}, f32[512,3072]{1,0:T(8,128)S(1)}) fusion(bf16[768,3072]{1,0:T(8,128)(2,1)} %param.37, f32[512,768]{1,0:T(8,128)S(1)} %get-tuple-element.235, f32[768]{0:T(1024)S(1)} %copy-done.59, f32[768]{0:T(1024)S(1)} %copy-done.53, f32[512]{0:T(512)S(1)} %fusion.113, f32[512]{0:T(512)S(1)} %broadcast_multiply_fusion.2), kind=kOutput, calls=%fused_computation.37 | convolution fusion | flops 2515402752 | bytes 18884608 | tf_op jit(solution)/shard_map/dot_general | solution.py:149
  72.7 4.5 multiply_reduce_fusion.5
  78.6 34.7 %all_gather.31 = bf16[256,768]{1,0:T(8,128)(2,1)} all-gather(bf16[32,768]{1,0:T(8,128)(2,1)S(1)} %multiply_convert_fusion.8), channel_id=1, replica_groups=mesh['row'=8,'col'=4] {'row'}, dimensions={0}, use_global_device_ids=true | all-gather | bytes 442368 | tf_op jit(solution)/shard_map/all_gather | solution.py:159
  113.9 9.4 convolution_convert_fusion
  126.5 8.5 reshape.393
  135.0 8.5 reshape.394
  143.5 13.2 %multiply_reduce_fusion = (f32[32,12,50]{2,1,0:T(8,128)}, f32[32,12,50,50]{2,3,1,0:T(8,128)}) fusion(bf16[32,50,12,64]{3,2,1,0:T(8,128)(2,1)} %reshape.394, bf16[32,50,12,64]{3,2,1,0:T(8,128)(2,1)} %reshape.393), kind=kOutput, calls=%fused_computation.31 | convolution fusion | flops 124780800 | bytes 8832000 | tf_op jit(solution)/shard_map/gqhe,gkhe->ghqk/dot_general | solution.py:54
  157.6 7.5 exponential_reduce_fusion
  165.8 8.6 reshape.392
  174.5 9.4 convert_bitcast_fusion
  183.9 9.4 copy.115
  193.3 11.4 %reshape.361 = bf16[1600,768]{0,1:T(8,128)(2,1)} reshape(bf16[32,50,12,64]{1,0,3,2:T(8,128)(2,1)} %copy.115) | data formatting | bytes 4915200 | tf_op jit(solution)/shard_map/reshape | solution.py:80
  204.7 5.1 fusion.165
  212.8 53.9 %fusion.211 = bf16[1600,3072]{1,0:T(8,128)(2,1)} fusion(bf16[768,3072]{1,0:T(8,128)(2,1)} %all-gather.11.cloned.1.call-done, f32[1600,768]{1,0:T(8,128)} %copy-done.13, f32[768]{0:T(1024)} %get-tuple-element.205, f32[768]{0:T(1024)} %get-tuple-element.252, f32[1600]{0:T(1024)S(1)} %add_rsqrt_fusion, ...), kind=kOutput, calls=%fused_computation.10.clone.clone.clone.clone.1 | convolution fusion | flops 7875379200 | bytes 19483136 | tf_op jit(solution)/shard_map/dot_general | solution.py:83
  266.7 14.1 %fusion.51 = f32[1600,768]{1,0:T(8,128)} fusion(f32[1600,768]{1,0:T(8,128)} %copy-done.13, bf16[3072,768]{1,0:T(8,128)(2,1)} %all-gather.13.cloned.1.call-done, bf16[1600,3072]{1,0:T(8,128)(2,1)} %fusion.211), kind=kOutput, calls=%fused_computation.91 | convolution fusion | flops 7550976000 | bytes 24379392 | tf_op jit(solution)/shard_map/dot_general | solution.py:86
  280.8 5.4 reshape.362
  292.0 5.6 all_gather.30
  300.5 20.5 %all-gather.1 = f32[8,1,256]{2,1,0:T(1,128)S(1)} all-gather(f32[1,1,256]{2,1,0:T(1,128)S(1)} %fusion.115), channel_id=1, replica_groups=mesh['row'=8,'col'=4] {'row'}, dimensions={0}, use_global_device_ids=true | all-gather | bytes 9216 | tf_op jit(solution)/shard_map/all_gather | solution.py:16
  322.1 5.0 all-gather
  331.4 13.7 %while.31 = (s32[]{:T(128)}, f32[256]{0:T(256)}, f32[8,256]{1,0:T(8,128)}, s32[]{:T(128)}, s32[]{:T(128)}, /*index=5*/s32[]{:T(128)}) while((s32[]{:T(128)}, f32[256]{0:T(256)}, f32[8,256]{1,0:T(8,128)}, s32[]{:T(128)}, s32[]{:T(128)}, /*index=5*/s32[]{:T(128)}) %tuple.126), condition=%wide.region_23.24_spmd, body=%wide.region_22.23_spmd.sunk | while | flops 2053 | bytes 5235 | solution.py:22
  350.5 56.9 %reduce-scatter.7.cloned.1.call-done = f32[32,768]{1,0:T(8,128)} async-done(((f32[256,768]{1,0:T(8,128)}), f32[32,768]{1,0:T(8,128)}) %reduce-scatter.7.cloned.1.call-update) | async-done | bytes 98320 | tf_op jit(solution)/shard_map/reduce_scatter | solution.py:174
  415.9 4.9 reshape.378
  420.8 4.1 copy.136
  426.1 9.0 add_convert_fusion
  435.2 7.2 multiply_reduce_fusion.3
  447.7 4.0 fusion.167
  455.0 4.0 reshape.368
  459.0 3.8 fusion.87
  464.7 3.9 reshape.371
  468.6 5.0 multiply_reduce_fusion.2
  478.7 3.9 reshape.370
  487.5 4.3 reshape.369
  496.9 6.4 fusion.153
  503.2 10.4 reshape.372
  513.6 7.4 copy.130
  521.6 8.9 fusion.157
  530.5 12.6 %reshape.375 = f32[8,96,4,768]{3,2,1,0:T(4,128)} reshape(f32[768,3072]{1,0:T(8,128)} %fusion.157) | data formatting | bytes 18874368 | tf_op jit(solution)/shard_map/reshape | solution.py:97
  543.1 9.1 copy.133
  552.3 15.5 %fusion.18 = bf16[3072,512]{0,1:T(8,128)(2,1)} fusion(f32[512,3072]{1,0:T(8,128)} %copy-done.3), kind=kLoop, calls=%fused_computation.40 | loop fusion | flops 102236160 | bytes 9437184 | tf_op jit(solution)/shard_map/convert_element_type | solution.py:150
  567.9 4.7 copy.148
  574.8 8.4 fusion.168
  585.9 4.7 fusion.159
  591.9 40.8 %all-reduce = (f32[]{:T(128)}, f32[768]{0:T(1024)}, f32[768]{0:T(1024)}, f32[768]{0:T(1024)}, f32[768]{0:T(1024)}) all-reduce(f32[]{:T(128)S(6)} %mul.413, f32[768]{0:T(1024)} %get-tuple-element.192, f32[768]{0:T(1024)} %get-tuple-element.195, f32[768]{0:T(1024)} %get-tuple-element.190, ...), channel_id=1, replica_groups=mesh['row'=8,'col'=4] {'row','col'}, use_global_device_ids=true, to_apply=%region_26.27 | all-reduce | flops 3073 | bytes 24584 | tf_op jit(solution)/shard_map/psum | solution.py:241
  637.5 124.2 %reduce-scatter.9.cloned.1.call-done = f32[1,96,576]{2,1,0:T(8,128)} async-done(((f32[32,96,576]{2,1,0:T(8,128)}), f32[1,96,576]{2,1,0:T(8,128)}) %reduce-scatter.9.cloned.1.call-update) | async-done | bytes 221200 | tf_op jit(solution)/shard_map/reduce_scatter | solution.py:239
  761.7 141.5 %reduce-scatter.13.cloned.1.call-done = f32[1,96,768]{2,1,0:T(8,128)} async-done(((f32[32,96,768]{2,1,0:T(8,128)}), f32[1,96,768]{2,1,0:T(8,128)}) %reduce-scatter.13.cloned.1.call-update) | async-done | bytes 294928 | tf_op jit(solution)/shard_map/reduce_scatter | solution.py:239
  903.2 141.7 %reduce-scatter.15.cloned.1.call-done = f32[1,384,192]{1,2,0:T(8,128)} async-done(((f32[32,384,192]{1,2,0:T(8,128)}), f32[1,384,192]{1,2,0:T(8,128)}) %reduce-scatter.15.cloned.1.call-update) | async-done | bytes 294928 | tf_op jit(solution)/shard_map/reduce_scatter | solution.py:239
  (250 shorter events, 131.7 us)
Async XLA Ops:
  7.2 11.3 %copy-start = (bf16[768,2304]{1,0:T(8,128)(2,1)S(1)}, bf16[768,2304]{1,0:T(8,128)(2,1)}, u32[]{:S(2)}) copy-start(bf16[768,2304]{1,0:T(8,128)(2,1)} %param.35) | copy-start | bytes 10616836
  7.2 11.3 %copy-start.43 = (f32[768]{0:T(1024)S(1)}, f32[768]{0:T(1024)}, u32[]{:S(2)}) copy-start(f32[768]{0:T(1024)} %param.31) | copy-start | bytes 9220
  7.2 106.7 %all-gather.7.cloned.1.call-start = ((), (), s32[]{:S(2)}) async-start(), calls=%async_computation.6 | async-start | bytes 4423680 | tf_op jit(solution)/shard_map/all_gather | solution.py:129
  7.9 196.8 %all-gather.9.cloned.1.call-start = ((), (), s32[]{:S(2)}) async-start(), calls=%async_computation.7 | async-start | bytes 1474560 | tf_op jit(solution)/shard_map/all_gather | solution.py:130
  8.7 204.1 %all-gather.11.cloned.1.call-start = ((), (), s32[]{:S(2)}) async-start(), calls=%async_computation.8 | async-start | bytes 5898240 | tf_op jit(solution)/shard_map/all_gather | solution.py:131
  9.4 257.3 %all-gather.13.cloned.1.call-start = ((), (), s32[]{:S(2)}) async-start(), calls=%async_computation.9 | async-start | bytes 5898240 | tf_op jit(solution)/shard_map/all_gather | solution.py:132
  10.0 397.3 %reduce-scatter.7.cloned.1.call-start = ((), (), s32[]{:S(2)}) async-start(), calls=%async_computation.10 | async-start | bytes 884736 | tf_op jit(solution)/shard_map/reduce_scatter | solution.py:174
  10.8 29.9 %copy-start.26 = (pred[32,16]{1,0:T(8,128)(4,1)}, pred[32,16]{1,0:T(8,128)(4,1)S(1)}, u32[]{:S(2)}) copy-start(pred[32,16]{1,0:T(8,128)(4,1)S(1)} %iota_compare_fusion) | copy-start | bytes 1540
  12.0 5.4 copy-start.8
  12.0 6.5 copy-start.58
  46.4 8.5 copy-start.55
  46.4 8.6 copy-start.53
  50.8 21.9 %slice-start = ((s8[4718592]{0:T(1024)(128)(4,1)}), s8[4194304]{0:T(1024)(128)(4,1)S(1)}, s32[]{:S(2)}) async-start(s8[4718592]{0:T(1024)(128)(4,1)} %bitcast.207), calls=%async_computation.16 | async-start | bytes 8388608
  53.7 18.9 %copy-start.4 = (f32[512,768]{1,0:T(8,128)}, f32[512,768]{1,0:T(8,128)S(1)}, u32[]{:S(2)}) copy-start(f32[512,768]{1,0:T(8,128)S(1)} %get-tuple-element.235) | copy-start | bytes 4718596
  53.8 18.8 %copy-start.36 = (f32[512]{0:T(512)}, f32[512]{0:T(512)S(1)}, u32[]{:S(2)}) copy-start(f32[512]{0:T(512)S(1)} %broadcast_multiply_fusion.2) | copy-start | bytes 6148
  54.9 17.7 %copy-start.46 = (f32[512]{0:T(512)}, f32[512]{0:T(512)S(1)}, u32[]{:S(2)}) copy-start(f32[512]{0:T(512)S(1)} %fusion.113) | copy-start | bytes 6148
  55.0 17.6 %copy-start.24 = (f32[32,16]{1,0:T(8,128)}, f32[32,16]{1,0:T(8,128)S(1)}, u32[]{:S(2)}) copy-start(f32[32,16]{1,0:T(8,128)S(1)} %convert_divide_fusion) | copy-start | bytes 6148
  55.0 17.6 %slice-start.1 = ((s8[4718592]{0:T(1024)(128)(4,1)}), s8[524288]{0:T(1024)(128)(4,1)S(1)}, s32[]{:S(2)}) async-start(s8[4718592]{0:T(1024)(128)(4,1)} %bitcast.207), calls=%async_computation.17 | async-start | bytes 1048576
  72.6 4.8 copy-start.12
  72.7 4.7 copy-start.14
  72.7 40.6 %copy-start.49 = (f32[2,768]{1,0:T(2,128)S(1)}, f32[2,768]{1,0:T(2,128)}, u32[]{:S(2)}) copy-start(f32[2,768]{1,0:T(2,128)} %param.24) | copy-start | bytes 18436
  72.7 40.6 %copy-start.50 = (f32[2,768]{1,0:T(2,128)S(1)}, f32[2,768]{1,0:T(2,128)}, u32[]{:S(2)}) copy-start(f32[2,768]{1,0:T(2,128)} %param.23) | copy-start | bytes 18436
  77.9 35.4 %copy-start.56 = (f32[32]{0:T(128)}, f32[32]{0:T(128)S(1)}, u32[]{:S(2)}) copy-start(f32[32]{0:T(128)S(1)} %get-tuple-element.244) | copy-start | bytes 388
  77.9 35.4 %copy-start.51 = (f32[32]{0:T(128)}, f32[32]{0:T(128)S(1)}, u32[]{:S(2)}) copy-start(f32[32]{0:T(128)S(1)} %add_rsqrt_fusion.2) | copy-start | bytes 388
  157.6 7.5 copy-start.17
  286.2 61.3 %copy-start.25 = (f32[32,16]{1,0:T(8,128)S(1)}, f32[32,16]{1,0:T(8,128)}, u32[]{:S(2)}) copy-start(f32[32,16]{1,0:T(8,128)} %copy-done.24) | copy-start | bytes 6148
  347.5 290.0 %reduce-scatter.17.cloned.1.call-start = ((), (), s32[]{:S(2)}) async-start(), calls=%async_computation.15 | async-start | bytes 3244032 | tf_op jit(solution)/shard_map/reduce_scatter | solution.py:239
  424.9 212.5 %reduce-scatter.11.cloned.1.call-start = ((), (), s32[]{:S(2)}) async-start(), calls=%async_computation.12 | async-start | bytes 3244032 | tf_op jit(solution)/shard_map/reduce_scatter | solution.py:239
  426.0 9.1 copy-start.16
  426.1 9.1 copy-start.5
  426.1 9.1 copy-start.37
  426.1 9.1 copy-start.47
  426.1 9.1 copy-start.54
  435.1 7.2 copy-start.60
  435.2 7.2 copy-start.42
  435.2 9.0 copy-start.20
  443.0 8.7 copy-start.38
  451.7 7.3 copy-start.27
  451.7 310.0 %reduce-scatter.9.cloned.1.call-start = ((), (), s32[]{:S(2)}) async-start(), calls=%async_computation.11 | async-start | bytes 8110080 | tf_op jit(solution)/shard_map/reduce_scatter | solution.py:239
  468.6 5.0 copy-start.2
  468.6 5.0 copy-start.15
  485.5 11.3 %copy-start.31 = (f32[512]{0:T(512)S(1)}, f32[512]{0:T(512)}, u32[]{:S(2)}) copy-start(f32[512]{0:T(512)} %copy-done.30) | copy-start | bytes 6148
  485.6 11.3 %copy-start.34 = (f32[512]{0:T(512)S(1)}, f32[512]{0:T(512)}, u32[]{:S(2)}) copy-start(f32[512]{0:T(512)} %copy-done.33) | copy-start | bytes 6148
  521.0 382.2 %reduce-scatter.13.cloned.1.call-start = ((), (), s32[]{:S(2)}) async-start(), calls=%async_computation.13 | async-start | bytes 9732096 | tf_op jit(solution)/shard_map/reduce_scatter | solution.py:239
  552.3 492.6 %reduce-scatter.15.cloned.1.call-start = ((), (), s32[]{:S(2)}) async-start(), calls=%async_computation.14 | async-start | bytes 9732096 | tf_op jit(solution)/shard_map/reduce_scatter | solution.py:239
  585.8 4.7 copy-start.9
  585.8 4.7 copy-start.35
  585.9 4.7 copy-start.44
  (25 other events, 46.8 us)
Sparse Core Ops, SparseCore 0:
  9.6 33.4 all-gather.6
  44.7 17.4 all-gather.8
  63.7 37.4 all-gather.10
  102.6 37.4 all-gather.12
  347.6 59.7 reduce-scatter.6
  425.1 100.4 reduce-scatter.16
  532.4 100.5 reduce-scatter.10
  640.2 121.4 reduce-scatter.8
  768.2 134.9 reduce-scatter.12
  910.5 134.3 reduce-scatter.14
where the time goes:
time: 1070 us; the launch traced here: 1050 us
  waiting for transfers between devices  467 us (44%)
  matrix products  213 us (20%)
  local copies, waits for them, and re-layouts  180 us (17%)
  blocking collectives  107 us (10%)
  other arithmetic  68.4 us (6%)
  between operations  17.7 us (2%)
    reduce_scatter x5, waiting for transfers between devices, body(): lax.psum_scatter(blocked, ('row', 'col'), scatter_dimension=0, tiled=True)  407 us
    reduce_scatter x1, waiting for transfers between devices, body(): lax.psum_scatter(logit_scale * jnp.einsum('ij,id->jd', sim_grad, image_ro...  56.9 us
    dot_general x1, matrix products, embed_images(): jnp.dot(normed2, w_up, preferred_element_type=jnp.float32)  53.9 us
    psum x1, blocking collectives, body(): lax.psum((loss_part, gain1_grad, bias1_grad, gain2_grad, bias2_grad), ('r...  40.8 us
    reshape x6, local copies, waits for them, and re-layouts, split_heads(): piece_bf.reshape(groups, length, HEADS, model_width // HEADS)  36.8 us
    all_gather x1, blocking collectives, body(): text_cols = lax.all_gather(text_embed, 'row', axis=0, tiled=True)  34.7 us
    reshape x3, local copies, waits for them, and re-layouts, grid_blocks(): matrix.reshape(row_parts, height // row_parts, col_parts, breadth // col_...  27.8 us
    all_gather x2, blocking collectives, merged(): everything = lax.all_gather(x, axis)  25.5 us
  transfers between devices with their start and end apart: 10, of which 4 were waited for; matrix products, arithmetic and copies ran while one was open for 36% of the time, Pallas kernels for 0%

commit v1 on v0

v1 whole, which is shorter than its diff:
```python
import functools
import math

import jax
import jax.numpy as jnp
from jax import lax
from jax.experimental import pallas as pl
from jax.experimental.pallas import tpu as pltpu
from jax.sharding import PartitionSpec as P

HEADS = 12
IMG_TOK = 50
norm_eps = 1e-06
logit_scale = 50.0
masked_score = -1e30
log2e = math.log2(math.e)
f32 = jnp.float32
bf16 = jnp.bfloat16
VMEM_LIMIT = 60 * 2**20


def dot_nn(a, b):
    return lax.dot_general(a, b, (((1,), (0,)), ((), ())), preferred_element_type=f32)


def dot_nt(a, b):
    return lax.dot_general(a, b, (((1,), (1,)), ((), ())), preferred_element_type=f32)


def dot_tn(a, b):
    return lax.dot_general(a, b, (((0,), (0,)), ((), ())), preferred_element_type=f32)


def split_low(x):
    high = x.astype(bf16)
    return high, (x - high.astype(f32)).astype(bf16)


def normed(x):
    centered = x - jnp.mean(x, axis=-1, keepdims=True)
    spread = lax.rsqrt(jnp.mean(centered * centered, axis=-1, keepdims=True) + norm_eps)
    return centered * spread, spread


def layer_norm(x, gain, bias):
    return normed(x)[0] * gain + bias


def normal_tail(x):
    size = jnp.abs(x)
    t = 1.0 / (1.0 + (0.3275911 * math.sqrt(0.5)) * size)
    bell = jnp.exp2((-0.5 * log2e) * (x * x))
    series = 0.5 * 1.061405429
    for factor in (-1.453152027, 1.421413741, -0.284496736, 0.254829592):
        series = series * t + 0.5 * factor
    return size, bell, series * t * bell


def gelu(x):
    size, _, tail = normal_tail(x)
    return jnp.maximum(x, 0.0) - size * tail


def gelu_and_slope(x):
    size, bell, tail = normal_tail(x)
    value = jnp.maximum(x, 0.0) - size * tail
    below = jnp.where(x >= 0.0, 1.0 - tail, tail)
    return value, below + x * (bell * (1.0 / math.sqrt(2.0 * math.pi)))


def lane_halves(width):
    lane = lax.broadcasted_iota(jnp.int32, (1, width), 1)
    first = (lane < width // 2).astype(f32)
    return first.astype(bf16), (1.0 - first).astype(bf16)


def stack_heads(x, first, second):
    return jnp.concatenate([x * first, x * second], axis=0)


def join_heads(stacked):
    rows, width = stacked.shape[0] // 2, stacked.shape[1]
    lane = lax.broadcasted_iota(jnp.int32, (rows, width), 1)
    return jnp.where(lane < width // 2, stacked[:rows], stacked[rows:])


def soft_weights(query, key, bias, factor):
    scores = dot_nt(query, key) * (factor * log2e) + bias
    weights = jnp.exp2(scores - jnp.max(scores, axis=-1, keepdims=True))
    return weights, 1.0 / jnp.sum(weights, axis=-1, keepdims=True)


def text_bias(key_bias_ref, block, rows, length):
    near = lax.broadcasted_iota(jnp.int32, (rows, rows), 0) // length
    far = lax.broadcasted_iota(jnp.int32, (rows, rows), 1) // length
    columns = pl.ds(pl.multiple_of(block * rows, rows), rows)
    bias = jnp.where(near == far, key_bias_ref[:, columns], masked_score)
    return jnp.concatenate([bias, bias], axis=0)


def member(len_ref, captions, tokens):
    length = tokens // captions
    token = lax.broadcasted_iota(jnp.int32, (captions, tokens), 1)
    caption = lax.broadcasted_iota(jnp.int32, (captions, tokens), 0)
    return ((token // length == caption) & (token % length < len_ref[...])).astype(f32)


def spread_rows(x, length):
    rows, width = x.shape
    return jnp.broadcast_to(x[:, None, :], (rows, length, width)).reshape(rows * length, width)


def text_forward_kernel(
    tok_ref, len_ref, key_bias_ref, gain1, bias1, gain2, bias2, qkv_hbm, out_hbm, up_hbm, down_hbm, proj_hbm,
    hidden_ref, embed_ref, projected_ref, pooled_ref, inner_sum_ref, heads_ref, mixed_ref, mid_ref, slope_ref,
    w_qkv, w_out, w_up, w_down, w_proj, norm_ref, inner_ref, sems,
):
    tokens, width = tok_ref.shape
    captions = len_ref.shape[0]
    length = tokens // captions
    wide = w_up.shape[1]
    pairs = ((qkv_hbm, w_qkv), (out_hbm, w_out), (up_hbm, w_up), (down_hbm, w_down), (proj_hbm, w_proj))
    loads = [pltpu.make_async_copy(s, d, sems.at[i]) for i, (s, d) in enumerate(pairs)]
    for load in loads:
        load.start()

    band = 128

    @pl.loop(0, tokens // band)
    def _(i):
        rows = pl.ds(pl.multiple_of(i * band, band), band)
        norm_ref[rows, :] = layer_norm(tok_ref[rows, :].astype(f32), gain1[...], bias1[...]).astype(bf16)

    loads[0].wait()

    @pl.loop(0, 3 * width // 256)
    def _(j):
        columns = pl.ds(pl.multiple_of(j * 256, 256), 256)
        heads_ref[:, columns] = dot_nn(norm_ref[...], w_qkv[:, columns]).astype(bf16)

    first, second = lane_halves(128)
    factor = (width // HEADS) ** -0.5

    @pl.loop(0, tokens // band)
    def _(block):
        rows = pl.ds(pl.multiple_of(block * band, band), band)
        bias = text_bias(key_bias_ref, block, band, length)
        for pair in range(width // 128):
            at = pair * 128
            query = stack_heads(heads_ref[rows, at : at + 128], first, second)
            weights, scale = soft_weights(query, heads_ref[rows, width + at : width + at + 128], bias, factor)
            value = heads_ref[rows, 2 * width + at : 2 * width + at + 128]
            mixed = dot_nn(weights.astype(bf16), value) * scale
            mixed_ref[rows, at : at + 128] = join_heads(mixed).astype(bf16)

    loads[1].wait()

    @pl.loop(0, tokens // band)
    def _(i):
        rows = pl.ds(pl.multiple_of(i * band, band), band)
        mid = tok_ref[rows, :].astype(f32) + dot_nn(mixed_ref[rows, :], w_out[...])
        mid_ref[rows, :] = mid
        norm_ref[rows, :] = layer_norm(mid, gain2[...], bias2[...]).astype(bf16)

    loads[2].wait()
    chosen = member(len_ref, captions, tokens)
    chosen_low = chosen.astype(bf16)
    place = lax.broadcasted_iota(jnp.int32, (captions, length, 1), 1)
    valid = (place < len_ref[...].reshape(captions, 1, 1)).astype(f32).reshape(tokens, 1)

    @pl.loop(0, wide // 256)
    def _(j):
        columns = pl.ds(pl.multiple_of(j * 256, 256), 256)
        value, slope = gelu_and_slope(dot_nn(norm_ref[...], w_up[:, columns]))
        value = value.astype(bf16)
        inner_ref[:, columns] = value
        slope_ref[:, columns] = (slope * valid).astype(bf16)
        inner_sum_ref[:, columns] = dot_nn(chosen_low, value).astype(bf16)

    loads[3].wait()
    inverse = 1.0 / len_ref[...].astype(f32)

    @pl.loop(0, width // 256)
    def _(j):
        columns = pl.ds(pl.multiple_of(j * 256, 256), 256)
        state = mid_ref[:, columns] + dot_nn(inner_ref[...], w_down[:, columns])
        hidden_ref[:, columns] = state.astype(bf16)
        high, low = split_low(state)
        pooled_ref[:, columns] = ((dot_nn(chosen_low, high) + dot_nn(chosen_low, low)) * inverse).astype(bf16)

    loads[4].wait()
    projected = dot_nn(pooled_ref[...], w_proj[...])
    projected_ref[...] = projected
    embed_ref[...] = (
        projected * lax.rsqrt(jnp.sum(projected * projected, axis=-1, keepdims=True) + norm_eps)
    ).astype(bf16)


def text_backward_kernel(
    tok_ref, len_ref, key_bias_ref, gain1, bias1, gain2, bias2, embed_grad_ref, projected_ref,
    heads_ref, mixed_ref, mid_ref, slope_ref, qkv_hbm, out_hbm, up_hbm, down_hbm, proj_hbm,
    proj_grad_ref, branch_ref, up_grad_ref, out_grad_ref, qkv_grad_ref, input_grad_ref, norm_grad_ref,
    w_qkv, w_out, w_up, w_down, w_proj, norm_ref, pre_grad_ref, wide_ref, mid_grad_ref, low_grad_ref,
    mixed_grad_ref, heads_grad_ref, sems,
):
    tokens, width = tok_ref.shape
    captions = len_ref.shape[0]
    length = tokens // captions
    wide = w_up.shape[1]
    col_parts = up_grad_ref.shape[0]
    pairs = ((proj_hbm, w_proj), (down_hbm, w_down), (up_hbm, w_up), (out_hbm, w_out), (qkv_hbm, w_qkv))
    loads = [pltpu.make_async_copy(s, d, sems.at[i]) for i, (s, d) in enumerate(pairs)]
    for load in loads:
        load.start()
    band = 128

    @pl.loop(0, tokens // band)
    def _(i):
        rows = pl.ds(pl.multiple_of(i * band, band), band)
        norm_ref[rows, :] = layer_norm(mid_ref[rows, :], gain2[...], bias2[...]).astype(bf16)

    projected = projected_ref[...]
    embed_grad = embed_grad_ref[...]
    r = lax.rsqrt(jnp.sum(projected * projected, axis=-1, keepdims=True) + norm_eps)
    along = jnp.sum(projected * embed_grad, axis=-1, keepdims=True)
    proj_grad = (r * embed_grad - (r * r * r) * projected * along).astype(bf16)
    proj_grad_ref[...] = proj_grad
    loads[0].wait()
    state_grad = dot_nt(proj_grad, w_proj[...]) * (1.0 / len_ref[...].astype(f32))
    branch = state_grad.astype(bf16)
    branch_ref[...] = branch
    loads[1].wait()
    loads[2].wait()

    for part in range(col_parts):
        step = wide // col_parts

        @pl.loop(0, step // 256)
        def _(j):
            columns = pl.ds(pl.multiple_of(part * step + j * 256, 256), 256)
            inner_grad = dot_nt(branch, w_down[columns, :])
            pre_grad = (spread_rows(inner_grad, length) * slope_ref[:, columns].astype(f32)).astype(bf16)
            pre_grad_ref[:, columns] = pre_grad
            local = pl.ds(pl.multiple_of(j * 256, 256), 256)
            up_grad_ref[part, :, local] = dot_tn(norm_ref[...], pre_grad).astype(bf16)

    place = lax.broadcasted_iota(jnp.int32, (captions, length, 1), 1)
    valid = (place < len_ref[...].reshape(captions, 1, 1)).astype(f32).reshape(tokens, 1)

    @pl.loop(0, width // 256)
    def _(j):
        columns = pl.ds(pl.multiple_of(j * 256, 256), 256)
        wide_ref[:, columns] = dot_nt(pre_grad_ref[...], w_up[columns, :])

    mid_grad_ref[...] = spread_rows(state_grad, length) * valid
    norm_grad_ref[...] = jnp.zeros_like(norm_grad_ref)

    @pl.loop(0, tokens // band)
    def _(i):
        rows = pl.ds(pl.multiple_of(i * band, band), band)
        unit, spread = normed(mid_ref[rows, :])
        outer = wide_ref[rows, :]
        norm_grad_ref[2:3, :] += jnp.sum(outer * unit, axis=0, keepdims=True)
        norm_grad_ref[3:4, :] += jnp.sum(outer, axis=0, keepdims=True)
        outer = outer * gain2[...]
        inner = outer - jnp.mean(outer, axis=-1, keepdims=True)
        inner = inner - unit * jnp.mean(outer * unit, axis=-1, keepdims=True)
        mid_grad = mid_grad_ref[rows, :] + spread * inner
        mid_grad_ref[rows, :] = mid_grad
        low_grad_ref[rows, :] = mid_grad.astype(bf16)

    loads[3].wait()
    step = width // col_parts
    for part in range(col_parts):
        out_grad_ref[part] = dot_tn(
            mixed_ref[...], low_grad_ref[:, part * step : (part + 1) * step]
        ).astype(bf16)

    @pl.loop(0, tokens // band)
    def _(i):
        rows = pl.ds(pl.multiple_of(i * band, band), band)
        mixed_grad_ref[rows, :] = dot_nt(low_grad_ref[rows, :], w_out[...]).astype(bf16)
        norm_ref[rows, :] = layer_norm(tok_ref[rows, :].astype(f32), gain1[...], bias1[...]).astype(bf16)

    first, second = lane_halves(128)
    factor = (width // HEADS) ** -0.5

    @pl.loop(0, tokens // band)
    def _(block):
        rows = pl.ds(pl.multiple_of(block * band, band), band)
        bias = text_bias(key_bias_ref, block, band, length)
        for pair in range(width // 128):
            at = pair * 128
            query = stack_heads(heads_ref[rows, at : at + 128], first, second)
            key = heads_ref[rows, width + at : width + at + 128]
            value = heads_ref[rows, 2 * width + at : 2 * width + at + 128]
            grad = stack_heads(mixed_grad_ref[rows, at : at + 128], first, second)
            weights, scale = soft_weights(query, key, bias, factor)
            probs = weights * scale
            prob_grad = dot_nt(grad, value)
            total = jnp.sum(prob_grad * probs, axis=-1, keepdims=True)
            score_grad = (probs * (prob_grad - total)).astype(bf16)
            query_grad = join_heads(dot_nn(score_grad, key)) * factor
            heads_grad_ref[rows, at : at + 128] = query_grad.astype(bf16)
            key_grad = dot_tn(score_grad, query) * factor
            heads_grad_ref[rows, width + at : width + at + 128] = key_grad.astype(bf16)
            value_grad = dot_tn(probs.astype(bf16), grad)
            heads_grad_ref[rows, 2 * width + at : 2 * width + at + 128] = value_grad.astype(bf16)

    step = 3 * width // col_parts
    for part in range(col_parts):
        qkv_grad_ref[part] = dot_tn(
            norm_ref[...], heads_grad_ref[:, part * step : (part + 1) * step]
        ).astype(bf16)
    loads[4].wait()

    @pl.loop(0, width // 256)
    def _(j):
        columns = pl.ds(pl.multiple_of(j * 256, 256), 256)
        wide_ref[:, columns] = dot_nt(heads_grad_ref[...], w_qkv[columns, :])

    @pl.loop(0, tokens // band)
    def _(i):
        rows = pl.ds(pl.multiple_of(i * band, band), band)
        unit, spread = normed(tok_ref[rows, :].astype(f32))
        outer = wide_ref[rows, :]
        norm_grad_ref[0:1, :] += jnp.sum(outer * unit, axis=0, keepdims=True)
        norm_grad_ref[1:2, :] += jnp.sum(outer, axis=0, keepdims=True)
        outer = outer * gain1[...]
        inner = outer - jnp.mean(outer, axis=-1, keepdims=True)
        inner = inner - unit * jnp.mean(outer * unit, axis=-1, keepdims=True)
        input_grad_ref[rows, :] = (mid_grad_ref[rows, :] + spread * inner).astype(bf16)


def group_mean(images, rows):
    token = lax.broadcasted_iota(jnp.int32, (images, rows), 1)
    image = lax.broadcasted_iota(jnp.int32, (images, rows), 0)
    inside = (token >= image * IMG_TOK) & (token < (image + 1) * IMG_TOK)
    return inside.astype(f32).astype(bf16)


def load_parts(parts, target, sems, col, col_count):
    depth = target.shape[0] // col_count
    copies = []
    for k, part in enumerate(parts):
        place = pl.multiple_of((col ^ k) * depth, depth)
        copies.append(pltpu.make_async_copy(part, target.at[pl.ds(place, depth)], sems.at[k]))
    return copies


def image_mix_kernel(
    col_count, tok_ref, gain_ref, bias_ref, *refs,
):
    qkv_parts, out_parts = refs[:col_count], refs[col_count : 2 * col_count]
    normed_ref, mean_ref, w_qkv, w_out, norm_ref, heads_ref, mixed_ref, sems = refs[2 * col_count :]
    rows, width = tok_ref.shape
    images = rows // IMG_TOK
    step = pl.program_id(0)
    col = lax.axis_index("col")

    @pl.when(step == 0)
    def _():
        copies = load_parts(qkv_parts, w_qkv, sems.at[0], col, col_count)
        copies += load_parts(out_parts, w_out, sems.at[1], col, col_count)
        for copy in copies:
            copy.start()
        for copy in copies:
            copy.wait()

    norm_ref[...] = layer_norm(tok_ref[...].astype(f32), gain_ref[0:1, :], bias_ref[0:1, :]).astype(bf16)

    @pl.loop(0, 3 * width // 256)
    def _(j):
        columns = pl.ds(pl.multiple_of(j * 256, 256), 256)
        heads_ref[:, columns] = dot_nn(norm_ref[...], w_qkv[:, columns]).astype(bf16)

    first, second = lane_halves(128)
    factor = (width // HEADS) ** -0.5
    window = 112
    for pair in range(images // 2):
        start, low = pair * 2 * IMG_TOK, (pair * 2 * IMG_TOK) // 16 * 16
        near = lax.broadcasted_iota(jnp.int32, (window, window), 0) + low
        far = lax.broadcasted_iota(jnp.int32, (window, window), 1) + low
        same = (near >= start) & (near < start + 2 * IMG_TOK) & (far >= start) & (far < start + 2 * IMG_TOK)
        same = same & ((near >= start + IMG_TOK) == (far >= start + IMG_TOK))
        bias = jnp.where(same, 0.0, masked_score)
        bias = jnp.concatenate([bias, bias], axis=0)
        keep = lax.broadcasted_iota(jnp.int32, (16, 128), 0) + low < start
        span = slice(low, low + window)

        @pl.loop(0, width // 128)
        def _(two):
            at = pl.multiple_of(two * 128, 128)
            query = stack_heads(heads_ref[span, pl.ds(at, 128)], first, second)
            weights, scale = soft_weights(query, heads_ref[span, pl.ds(width + at, 128)], bias, factor)
            value = heads_ref[span, pl.ds(2 * width + at, 128)]
            mixed = join_heads(dot_nn(weights.astype(bf16), value) * scale)
            if low == start:
                mixed_ref[span, pl.ds(at, 128)] = mixed.astype(bf16)
            else:
                former = mixed_ref[low : low + 16, pl.ds(at, 128)].astype(f32)
                mixed_ref[low : low + 16, pl.ds(at, 128)] = jnp.where(keep, former, mixed[:16]).astype(bf16)
                mixed_ref[low + 16 : low + window, pl.ds(at, 128)] = mixed[16:].astype(bf16)

    mid = tok_ref[...].astype(f32) + dot_nn(mixed_ref[...], w_out[...])
    normed_ref[...] = layer_norm(mid, gain_ref[1:2, :], bias_ref[1:2, :]).astype(bf16)
    high, low = split_low(mid)
    select = group_mean(images, rows)
    mean_ref[...] = (dot_nn(select, high) + dot_nn(select, low)) * (1.0 / IMG_TOK)


def image_embed_kernel(col_count, normed_ref, mean_ref, *refs):
    up_parts, down_parts = refs[:col_count], refs[col_count : 2 * col_count]
    embed_ref, w_up, w_down, sum_ref, sems = refs[2 * col_count :]
    rows, width = normed_ref.shape
    images = rows // IMG_TOK
    wide = w_up.shape[1]
    step = pl.program_id(0)
    col = lax.axis_index("col")
    downs = load_parts(down_parts, w_down, sems.at[1], col, col_count)

    @pl.when(step == 0)
    def _():
        ups = load_parts(up_parts, w_up, sems.at[0], col, col_count)
        for copy in ups + downs:
            copy.start()
        for copy in ups:
            copy.wait()

    select = group_mean(images, rows)

    @pl.loop(0, wide // 256)
    def _(j):
        columns = pl.ds(pl.multiple_of(j * 256, 256), 256)
        inner = gelu(dot_nn(normed_ref[...], w_up[:, columns])).astype(bf16)
        sum_ref[pl.ds(pl.multiple_of(step * images, images), images), columns] = dot_nn(select, inner)

    @pl.when(step == pl.num_programs(0) - 1)
    def _():
        for copy in downs:
            copy.wait()
        high, low = split_low(sum_ref[...] * (1.0 / IMG_TOK))
        pooled = mean_ref[...] + dot_nn(high, w_down[...]) + dot_nn(low, w_down[...])
        embed_ref[...] = (
            pooled * lax.rsqrt(jnp.sum(pooled * pooled, axis=-1, keepdims=True) + norm_eps)
        ).astype(bf16)


def whole(shape):
    return pl.BlockSpec(shape, lambda *_: (0,) * len(shape))


in_vmem = pl.BlockSpec(memory_space=pltpu.VMEM)
anywhere = pl.BlockSpec(memory_space=pl.ANY)


def plain(kernel, outs, ins, scratch, name, **settings):
    return pl.pallas_call(
        kernel,
        out_shape=outs,
        in_specs=ins,
        out_specs=[in_vmem] * len(outs),
        scratch_shapes=scratch,
        compiler_params=pltpu.CompilerParams(vmem_limit_bytes=VMEM_LIMIT, **settings),
        name=name,
    )


def array(shape, dtype):
    return jax.ShapeDtypeStruct(shape, dtype)


def partners(x, col_count):
    order = [(i, i ^ 2) for i in range(col_count)]
    near = [(i, i ^ 1) for i in range(col_count)]
    far = lax.ppermute(x, "col", order)
    return [x, lax.ppermute(x, "col", near), far, lax.ppermute(far, "col", near)]


def body(
    image_tokens, image_norm_gain, image_norm_bias, image_qkv, image_out, image_up, image_down,
    text_tokens, text_lengths, norm1_gain, norm1_bias, norm2_gain, norm2_bias,
    text_qkv, text_out, text_up, text_down, text_proj,
):
    tokens, width = text_tokens.shape
    captions = text_lengths.shape[0]
    length = tokens // captions
    wide = text_up.shape[1]
    row_count, col_count = lax.axis_size("row"), lax.axis_size("col")
    row, col = lax.axis_index("row"), lax.axis_index("col")
    pair_total = captions * row_count * col_count
    image_rows, images = image_tokens.shape[0], image_tokens.shape[0] // IMG_TOK

    qkv_parts = partners(image_qkv, col_count)
    out_parts = partners(image_out, col_count)
    up_parts = partners(image_up, col_count)
    down_parts = partners(image_down, col_count)

    lengths = text_lengths.reshape(captions, 1)
    place = lax.broadcasted_iota(jnp.int32, (captions, length), 1)
    key_bias = jnp.where(place < lengths, 0.0, masked_score).reshape(1, tokens)
    vectors = [v.reshape(1, width) for v in (norm1_gain, norm1_bias, norm2_gain, norm2_bias)]
    weights = (text_qkv, text_out, text_up, text_down, text_proj)
    weight_scratch = [pltpu.VMEM(w.shape, bf16) for w in weights]

    (hidden, text_embed, projected, pooled, inner_sum, heads, mixed, mid, slope) = plain(
        text_forward_kernel,
        (
            array((tokens, width), bf16),
            array((captions, width), bf16),
            array((captions, width), f32),
            array((captions, width), bf16),
            array((captions, wide), bf16),
            array((tokens, 3 * width), bf16),
            array((tokens, width), bf16),
            array((tokens, width), f32),
            array((tokens, wide), bf16),
        ),
        [in_vmem] * 7 + [anywhere] * 5,
        weight_scratch
        + [pltpu.VMEM((tokens, width), bf16), pltpu.VMEM((tokens, wide), bf16), pltpu.SemaphoreType.DMA((5,))],
        "text_forward",
    )(text_tokens, lengths, key_bias, *vectors, *weights)

    groups = 4
    group_rows, group_images = image_rows // groups, images // groups
    parts = [anywhere] * (2 * col_count)
    image_tokens, text_embed = lax.optimization_barrier((image_tokens, text_embed))
    image_normed, image_mean = pl.pallas_call(
        functools.partial(image_mix_kernel, col_count),
        grid=(groups,),
        out_shape=(array((image_rows, width), bf16), array((images, width), f32)),
        in_specs=[
            pl.BlockSpec((group_rows, width), lambda i: (i, 0)),
            whole(image_norm_gain.shape),
            whole(image_norm_bias.shape),
        ]
        + parts,
        out_specs=(
            pl.BlockSpec((group_rows, width), lambda i: (i, 0)),
            pl.BlockSpec((group_images, width), lambda i: (i, 0)),
        ),
        scratch_shapes=[
            pltpu.VMEM((width, 3 * width), bf16),
            pltpu.VMEM((width, width), bf16),
            pltpu.VMEM((group_rows, width), bf16),
            pltpu.VMEM((group_rows, 3 * width), bf16),
            pltpu.VMEM((group_rows, width), bf16),
            pltpu.SemaphoreType.DMA((2, col_count)),
        ],
        compiler_params=pltpu.CompilerParams(vmem_limit_bytes=VMEM_LIMIT),
        name="image_mix",
    )(image_tokens, image_norm_gain, image_norm_bias, *qkv_parts, *out_parts)
    image_embed = pl.pallas_call(
        functools.partial(image_embed_kernel, col_count),
        grid=(groups,),
        out_shape=array((images, width), bf16),
        in_specs=[pl.BlockSpec((group_rows, width), lambda i: (i, 0)), whole((images, width))] + parts,
        out_specs=whole((images, width)),
        scratch_shapes=[
            pltpu.VMEM((width, wide), bf16),
            pltpu.VMEM((wide, width), bf16),
            pltpu.VMEM((images, wide), f32),
            pltpu.SemaphoreType.DMA((2, col_count)),
        ],
        compiler_params=pltpu.CompilerParams(vmem_limit_bytes=VMEM_LIMIT),
        name="image_embed",
    )(image_normed, image_mean, *up_parts, *down_parts)

    both = ("row", "col")
    image_all = lax.all_gather(image_embed, both, axis=0, tiled=True)
    sims = logit_scale * dot_nt(image_all, text_embed)
    lifted = jnp.exp(sims)
    row_sums = lax.psum(jnp.sum(lifted, axis=1), both)
    col_sums = jnp.sum(lifted, axis=0)
    sim_grad = (0.5 * (lifted / row_sums[:, None] + lifted / col_sums[None, :])).astype(bf16)
    image_own = image_embed.astype(f32)
    embed_grad = logit_scale * (dot_tn(sim_grad, image_all) - image_own)
    positives = logit_scale * jnp.sum(image_own * text_embed.astype(f32), axis=1)
    loss_part = 0.5 * jnp.sum(jnp.log(col_sums) - 2.0 * positives)

    (proj_grad, branch, up_grad, out_grad, qkv_grad, input_grad, norm_grads) = plain(
        text_backward_kernel,
        (
            array((captions, width), bf16),
            array((captions, width), bf16),
            array((col_count, width, wide // col_count), bf16),
            array((col_count, width, width // col_count), bf16),
            array((col_count, width, 3 * width // col_count), bf16),
            array((tokens, width), bf16),
            array((8, width), f32),
        ),
        [in_vmem] * 13 + [anywhere] * 5,
        weight_scratch
        + [
            pltpu.VMEM((tokens, width), bf16),
            pltpu.VMEM((tokens, wide), bf16),
            pltpu.VMEM((tokens, width), f32),
            pltpu.VMEM((tokens, width), f32),
            pltpu.VMEM((tokens, width), bf16),
            pltpu.VMEM((tokens, width), bf16),
            pltpu.VMEM((tokens, 3 * width), bf16),
            pltpu.SemaphoreType.DMA((5,)),
        ],
        "text_backward",
    )(
        text_tokens, lengths, key_bias, *vectors, embed_grad, projected, heads, mixed, mid, slope, *weights,
    )

    def scattered(matrix):
        blocks = matrix.reshape(col_count * row_count, width // row_count, matrix.shape[2])
        return lax.psum_scatter(blocks, ("col", "row"), scatter_dimension=0, tiled=True)[0].astype(f32)

    def by_row(x):
        x = lax.all_to_all(x, "row", split_axis=1, concat_axis=0, tiled=True)
        return lax.all_gather(x, "col", axis=0, tiled=True)

    def by_col(x):
        x = lax.all_gather(x, "row", axis=0, tiled=True)
        return lax.all_to_all(x, "col", split_axis=1, concat_axis=0, tiled=True)

    grad_down = dot_tn(by_row(inner_sum), by_col(branch))
    grad_proj = dot_tn(by_row(pooled), by_col(proj_grad))
    loss_total, norm_total = lax.psum((loss_part, norm_grads), both)
    mean_loss = (loss_total + 0.5 * jnp.sum(jnp.log(row_sums))) / pair_total
    return (
        mean_loss, hidden, input_grad, norm_total[0], norm_total[1], norm_total[2], norm_total[3],
        scattered(qkv_grad), scattered(out_grad), scattered(up_grad), grad_down, grad_proj,
    )


def solution(mesh):
    split = P(("row", "col"), None)
    grid = P("row", "col")
    in_specs = (
        split, P(), P(), P("col", None), P("col", None), P("col", None), P("col", None), split, P(("row", "col")),
    ) + (P(),) * 9
    out_specs = (P(), split, split, P(), P(), P(), P(), grid, grid, grid, grid, grid)
    return jax.shard_map(body, mesh=mesh, in_specs=in_specs, out_specs=out_specs, check_vma=False)
```

time: 1070 us -> 702 us (0.66); the launches traced: 1050 us -> 701 us
  matrix products: 213 us -> 5.28 us
  Pallas kernels: 0 us -> 176 us
  waiting for transfers between devices: 467 us -> 298 us
  local copies, waits for them, and re-layouts: 180 us -> 12.7 us
  other arithmetic: 68.4 us -> 6.76 us
  blocking collectives: 107 us -> 162 us
  starting transfers between devices: 0.4 us -> 23.1 us
    reduce_scatter x6 -> x3, waiting for transfers between devices: 464 us -> 159 us  [scattered(): lax.psum_scatter(blocks, ('col', 'row'), scatter_dimension=0, tiled=True)[0]]
    dot_general x29 -> x4, matrix products: 213 us -> 5.28 us  [the longest x3 3.07 us: dot_tn(): lax.dot_general(a, b, (((0,), (0,)), ((), ())), preferred_element_type=f32)]
    pallas_call x0 -> x4, Pallas kernels: none -> 176 us  [the longest x1 59.4 us: body(): pl.pallas_call(functools.partial(image_mix_kernel, col_count), grid=(grou...]
    reshape x16 -> x5, local copies, waits for them, and re-layouts: 102 us -> 6.4 us  [the longest x4 5.07 us: body(): v.reshape(1, width)]
    ppermute x0 -> x12, waiting for transfers between devices: none -> 74.5 us  [the longest x4 72.9 us: partners(): far = lax.ppermute(x, 'col', order)]
    all_gather x4 -> x1, waiting for transfers between devices: 0.03 us -> 56.6 us  [body(): image_all = lax.all_gather(image_embed, both, axis=0, tiled=True)]
    psum x1 -> x2, blocking collectives: 40.8 us -> 79.6 us  [the longest x1 40.5 us: body(): loss_total, norm_total = lax.psum((loss_part, norm_grads), both)]
    reduce_sum x15 -> x3, other arithmetic: 25 us -> 1.33 us  [the longest x1 0.61 us: body(): loss_part = 0.5 * jnp.sum(jnp.log(col_sums) - 2.0 * positives)]
  transfers between devices with their start and end apart: 10 -> 20, of which waited for: 4 -> 6; matrix products, arithmetic and copies ran while one was open for 36% -> 3% of each run, Pallas kernels for 0% -> 13%
where the time goes in v1:
time: 702 us; the launch traced here: 701 us
  waiting for transfers between devices  298 us (42%)
  Pallas kernels  176 us (25%)
  blocking collectives  162 us (23%)
  starting transfers between devices  23.1 us (3%)
  between operations  17.1 us (2%)
  local copies, waits for them, and re-layouts  12.7 us (2%)
    reduce_scatter x3, waiting for transfers between devices, scattered(): lax.psum_scatter(blocks, ('col', 'row'), scatter_dimension=0, tiled=True)[0]  159 us
    ppermute x4, waiting for transfers between devices, partners(): far = lax.ppermute(x, 'col', order)  72.9 us
    all_gather x2, blocking collectives, by_col(): x = lax.all_gather(x, 'row', axis=0, tiled=True)  63.6 us
    pallas_call x1, Pallas kernels, body(): pl.pallas_call(functools.partial(image_mix_kernel, col_count), grid=(grou...  59.4 us
    all_gather x1, waiting for transfers between devices, body(): image_all = lax.all_gather(image_embed, both, axis=0, tiled=True)  56.6 us
    pallas_call x1, Pallas kernels, body(): plain(text_backward_kernel, (array((captions, width), bf16), array((capti...  48.1 us
    psum x1, blocking collectives, body(): loss_total, norm_total = lax.psum((loss_part, norm_grads), both)  40.5 us
    psum x1, blocking collectives, body(): row_sums = lax.psum(jnp.sum(lifted, axis=1), both)  39.1 us
  transfers between devices with their start and end apart: 20, of which 6 were waited for; matrix products, arithmetic and copies ran while one was open for 3% of the time, Pallas kernels for 13%

profile of v1, /device:TPU:0, one launch (start us, length us, event | category | flops | bytes accessed | tf_op | source)
XLA Modules:
  0.0 700.8 jit_solution(5122837906358941250)
XLA Ops:
  7.2 3.0 collective-permute-start.7
  10.3 0.5 collective-permute-start
  10.8 1.9 collective-permute-start.1
  12.8 1.3 collective-permute-start.4
  14.0 72.9 %collective-permute-done.4.refs_6_ = bf16[192,768]{1,0:T(8,128)(2,1)S(1)} collective-permute-done((bf16[192,768]{1,0:T(8,128)(2,1)}, bf16[192,768]{1,0:T(8,128)(2,1)S(1)}, u32[]{:S(2)}, u32[]{:S(2)}) %collective-permute-start.4) | collective-permute-done | bytes 294944 | tf_op jit(solution)/shard_map/ppermute | solution.py:476
  87.0 1.6 collective-permute-done.5.refs_7_
  90.2 1.3 copy.32.len_ref
  91.5 0.7 fusion.6
  92.3 0.7 select_n.15.key_bias_ref
  92.9 1.3 reshape.99.gain1
  94.2 1.3 reshape.100.bias1
  95.4 1.3 reshape.101.gain2
  96.7 1.3 reshape.102.bias2
  98.0 30.7 %text_forward.1 = (bf16[512,768]{1,0:T(8,128)(2,1)}, bf16[32,768]{1,0:T(8,128)(2,1)}, f32[32,768]{1,0:T(8,128)}, bf16[32,768]{1,0:T(8,128)(2,1)}, bf16[32,3072]{...) custom-call(bf16[512,768]{1,0:T(8,128)(2,1)} %tok_ref.4, ...), custom_call_target="tpu_custom_call" | custom-call | tf_op jit(solution)/shard_map/text_forward/pallas_call | solution.py:506
  128.7 59.4 %image_mix.1 = (bf16[1600,768]{1,0:T(8,128)(2,1)}, f32[32,768]{1,0:T(8,128)}) custom-call(bf16[1600,768]{1,0:T(8,128)(2,1)} %tok_ref.3, f32[2,768]{1,0:T(2,128)} %gain_ref.1, f32[2,768]{1,0:T(2,128)} %bias_ref.1, bf16[192,2304]{1,0:T(8,128)(2,1)} %refs_0_.2, bf16[192,2304]{1,0:T(8,128)(2,1)} %copy-done.4, bf16[192,2304]{1,0:T(8,128)(2,1)} %collective-permute-done.1.refs_2_, ...), custom_call_target="tpu_custom_call" | custom-call | tf_op jit(solution)/shard_map/image_mix/pallas_call | solution.py:529
  188.1 1.0 copy-done.3
  189.1 38.0 %image_embed.1 = bf16[32,768]{1,0:T(8,128)(2,1)} custom-call(bf16[1600,768]{1,0:T(8,128)(2,1)} %get-tuple-element.34.normed_ref, f32[32,768]{1,0:T(8,128)} %get-tuple-element.35.mean_ref, bf16[192,3072]{1,0:T(8,128)(2,1)} %refs_0_.3, bf16[192,3072]{1,0:T(8,128)(2,1)} %copy-done.3, bf16[192,3072]{1,0:T(8,128)(2,1)} %copy-done.1, ...), custom_call_target="tpu_custom_call" | custom-call | tf_op jit(solution)/shard_map/image_embed/pallas_call | solution.py:554
  227.1 56.6 %all-gather.2.cloned.1.call-done = bf16[1024,768]{1,0:T(8,128)(2,1)} async-done(((bf16[32,768]{1,0:T(8,128)(2,1)}), bf16[1024,768]{1,0:T(8,128)(2,1)}) %all-gather.2.cloned.1.call-update) | async-done | bytes 1572880 | tf_op jit(solution)/shard_map/all_gather | solution.py:571
  283.7 2.2 fusion.8
  285.9 39.1 %psum.22 = f32[1024]{0:T(1024)S(1)} all-reduce(f32[1024]{0:T(1024)S(1)} %get-tuple-element.52), channel_id=1, replica_groups=mesh['row'=8,'col'=4] {'row','col'}, use_global_device_ids=true, to_apply=%region_5.6 | all-reduce | flops 1024 | bytes 8192 | tf_op jit(solution)/shard_map/psum | solution.py:574
  325.1 1.1 fusion.1.embed_grad_ref
  326.1 48.1 %text_backward.1 = (bf16[32,768]{1,0:T(8,128)(2,1)}, bf16[32,768]{1,0:T(8,128)(2,1)}, bf16[4,768,768]{2,1,0:T(8,128)(2,1)}, bf16[4,768,192]{2,1,0:T(8,128)(2,1)}...) custom-call(bf16[512,768]{1,0:T(8,128)(2,1)} %tok_ref.4, s32[32,1]{1,0:T(8,128)} %copy.32.len_ref, ...), custom_call_target="tpu_custom_call" | custom-call | tf_op jit(solution)/shard_map/text_backward/pallas_call | solution.py:582
  374.3 0.7 reduce-scatter.4.cloned.1.call-update
  375.1 0.5 reduce-scatter.8.cloned.1.call-update
  376.0 0.6 copy.37
  376.6 4.6 all-to-all-start.2
  381.2 0.7 copy.44
  381.9 6.2 all-to-all-done.2
  388.1 3.4 all-to-all-start
  391.5 5.8 all_gather.18
  397.3 32.4 %all_gather.17 = bf16[256,768]{1,0:T(8,128)(2,1)S(1)} all-gather(bf16[32,768]{1,0:T(8,128)(2,1)S(1)} %copy-done.13), channel_id=1, replica_groups=mesh['row'=8,'col'=4] {'row'}, dimensions={0}, use_global_device_ids=true | all-gather | bytes 442368 | tf_op jit(solution)/shard_map/all_gather | solution.py:619
  429.7 0.9 copy.35
  430.6 3.5 all-to-all-start.1
  434.1 13.2 %all_gather.16 = bf16[1024,384]{1,0:T(8,128)(2,1)S(1)} all-gather(bf16[256,384]{1,0:T(8,128)(2,1)S(1)} %bitcast.45), channel_id=1, replica_groups=mesh['row'=8,'col'=4] {'col'}, dimensions={0}, use_global_device_ids=true | all-gather | bytes 983040 | tf_op jit(solution)/shard_map/all_gather | solution.py:616
  447.4 31.2 %all_gather.19 = bf16[256,768]{1,0:T(8,128)(2,1)S(1)} all-gather(bf16[32,768]{1,0:T(8,128)(2,1)S(1)} %copy-done.12), channel_id=1, replica_groups=mesh['row'=8,'col'=4] {'row'}, dimensions={0}, use_global_device_ids=true | all-gather | bytes 442368 | tf_op jit(solution)/shard_map/all_gather | solution.py:619
  478.6 0.9 copy.38
  479.5 3.5 all-to-all-start.3
  483.0 0.6 subtract_reduce_fusion
  484.3 40.5 %all-reduce = (f32[]{:T(128)}, f32[8,768]{1,0:T(8,128)S(1)}) all-reduce(f32[]{:T(128)S(6)} %mul.40, f32[8,768]{1,0:T(8,128)S(1)} %copy-done.14), channel_id=1, replica_groups=mesh['row'=8,'col'=4] {'row','col'}, use_global_device_ids=true, to_apply=%region_3.4 | all-reduce | flops 6145 | bytes 49160 | tf_op jit(solution)/shard_map/psum | solution.py:624
  524.8 0.6 log_reduce_fusion
  526.7 0.6 slice_reduce_fusion
  527.4 0.9 fusion.9
  528.3 1.1 fusion.10
  529.4 1.4 bitcast_convert_fusion.2
  530.9 49.3 %reduce-scatter.4.cloned.1.call-done = bf16[1,96,576]{2,1,0:T(8,128)(2,1)} async-done(((bf16[32,96,576]{2,1,0:T(8,128)(2,1)}), bf16[1,96,576]{2,1,0:T(8,128)(2,1)}) %reduce-scatter.4.cloned.1.call-update) | async-done | bytes 110608 | tf_op jit(solution)/shard_map/reduce_scatter | solution.py:612
  580.2 1.6 bitcast_convert_fusion.1
  581.8 109.7 %reduce-scatter.8.cloned.1.call-done = bf16[1,96,768]{2,1,0:T(8,128)(2,1)} async-done(((bf16[32,96,768]{2,1,0:T(8,128)(2,1)}), bf16[1,96,768]{2,1,0:T(8,128)(2,1)}) %reduce-scatter.8.cloned.1.call-update) | async-done | bytes 147472 | tf_op jit(solution)/shard_map/reduce_scatter | solution.py:612
  691.5 1.6 bitcast_convert_fusion
  (61 shorter events, 2.6 us)
Async XLA Ops:
  7.2 276.5 %all-gather.2.cloned.1.call-start = ((), (), s32[]{:S(2)}) async-start(), calls=%async_computation.7 | async-start | bytes 1622016 | tf_op jit(solution)/shard_map/all_gather | solution.py:571
  7.2 81.9 %collective-permute-start.7 = (bf16[192,3072]{1,0:T(8,128)(2,1)}, bf16[192,3072]{1,0:T(8,128)(2,1)S(1)}, u32[]{:S(2)}, u32[]{:S(2)}) collective-permute-start(bf16[192,3072]{1,0:T(8,128)(2,1)} %refs_0_.3), channel_id=1, source_target_pairs={{0,2},{1,3},{2,0},{3,1},{4,6},{5,7},{6,4},{7,5},{8,10},{9,11},{10,... | collective-permute-start | bytes 3538952 | tf_op jit(solution)/shard_map/ppermute | solution.py:476
  10.2 79.0 %collective-permute-start.10 = (bf16[768,768]{1,0:T(8,128)(2,1)}, bf16[768,768]{1,0:T(8,128)(2,1)S(1)}, u32[]{:S(2)}, u32[]{:S(2)}) collective-permute-start(bf16[768,768]{1,0:T(8,128)(2,1)} %refs_4_.3), channel_id=1, source_target_pairs={{0,2},{1,3},{2,0},{3,1},{4,6},{5,7},{6,4},{7,5},{8,10},{9,11},{10,... | collective-permute-start | bytes 3538952 | tf_op jit(solution)/shard_map/ppermute | solution.py:476
  10.3 2.5 collective-permute-start.3
  10.3 78.4 %collective-permute-start = (bf16[192,2304]{1,0:T(8,128)(2,1)}, bf16[192,2304]{1,0:T(8,128)(2,1)S(1)}, u32[]{:S(2)}, u32[]{:S(2)}) collective-permute-start(bf16[192,2304]{1,0:T(8,128)(2,1)} %refs_0_.2), channel_id=1, source_target_pairs={{0,1},{1,0},{2,3},{3,2},{4,5},{5,4},{6,7},{7,6},{8,9},{9,8},{10,11... | collective-permute-start | bytes 2654216 | tf_op jit(solution)/shard_map/ppermute | solution.py:477
  10.8 79.2 %collective-permute-start.1 = (bf16[192,2304]{1,0:T(8,128)(2,1)}, bf16[192,2304]{1,0:T(8,128)(2,1)}, u32[]{:S(2)}, u32[]{:S(2)}) collective-permute-start(bf16[192,2304]{1,0:T(8,128)(2,1)} %refs_0_.2), channel_id=1, source_target_pairs={{0,2},{1,3},{2,0},{3,1},{4,6},{5,7},{6,4},{7,5},{8,10},{9,11},{10,... | collective-permute-start | bytes 2654216 | tf_op jit(solution)/shard_map/ppermute | solution.py:476
  12.8 77.2 %copy-start.6 = (bf16[192,768]{1,0:T(8,128)(2,1)}, bf16[192,768]{1,0:T(8,128)(2,1)S(1)}, u32[]{:S(2)}) copy-start(bf16[192,768]{1,0:T(8,128)(2,1)S(1)} %collective-permute-done.3.refs_5_) | copy-start | bytes 884740
  12.8 74.2 %collective-permute-start.4 = (bf16[192,768]{1,0:T(8,128)(2,1)}, bf16[192,768]{1,0:T(8,128)(2,1)S(1)}, u32[]{:S(2)}, u32[]{:S(2)}) collective-permute-start(bf16[192,768]{1,0:T(8,128)(2,1)} %refs_4_.2), channel_id=1, source_target_pairs={{0,2},{1,3},{2,0},{3,1},{4,6},{5,7},{6,4},{7,5},{8,10},{9,11},{10,... | collective-permute-start | bytes 884744 | tf_op jit(solution)/shard_map/ppermute | solution.py:476
  87.0 3.0 copy-start.7
  87.0 1.6 collective-permute-start.5
  88.6 1.6 copy-start.8
  88.6 99.5 %collective-permute-start.6 = (bf16[192,3072]{1,0:T(8,128)(2,1)}, bf16[192,3072]{1,0:T(8,128)(2,1)S(1)}, u32[]{:S(2)}, u32[]{:S(2)}) collective-permute-start(bf16[192,3072]{1,0:T(8,128)(2,1)} %refs_0_.3), channel_id=1, source_target_pairs={{0,1},{1,0},{2,3},{3,2},{4,5},{5,4},{6,7},{7,6},{8,9},{9,8},{10,11... | collective-permute-start | bytes 3538952 | tf_op jit(solution)/shard_map/ppermute | solution.py:477
  88.7 0.9 copy-start.4
  88.7 99.4 %collective-permute-start.9 = (bf16[768,768]{1,0:T(8,128)(2,1)}, bf16[768,768]{1,0:T(8,128)(2,1)}, u32[]{:S(2)}, u32[]{:S(2)}) collective-permute-start(bf16[768,768]{1,0:T(8,128)(2,1)} %refs_4_.3), channel_id=1, source_target_pairs={{0,1},{1,0},{2,3},{3,2},{4,5},{5,4},{6,7},{7,6},{8,9},{9,8},{10,11... | collective-permute-start | bytes 3538952 | tf_op jit(solution)/shard_map/ppermute | solution.py:477
  89.1 39.6 %copy-start.1 = (bf16[192,3072]{1,0:T(8,128)(2,1)}, bf16[192,3072]{1,0:T(8,128)(2,1)S(1)}, u32[]{:S(2)}) copy-start(bf16[192,3072]{1,0:T(8,128)(2,1)S(1)} %collective-permute-done.7.refs_2_) | copy-start | bytes 3538948
  89.1 99.0 %collective-permute-start.8 = (bf16[192,3072]{1,0:T(8,128)(2,1)S(1)}, bf16[192,3072]{1,0:T(8,128)(2,1)}, u32[]{:S(2)}, u32[]{:S(2)}) collective-permute-start(bf16[192,3072]{1,0:T(8,128)(2,1)S(1)} %collective-permute-done.7.refs_2_), channel_id=1, source_target_pairs={{0,1},{1,0},{2,3},{3,2},{4,5},{5,4},{6,7},{7,6},{8,9},{9,8},{10,11... | collective-permute-start | bytes 3538952 | tf_op jit(solution)/shard_map/ppermute | solution.py:477
  89.6 39.0 %copy-start.2 = (bf16[768,768]{1,0:T(8,128)(2,1)}, bf16[768,768]{1,0:T(8,128)(2,1)S(1)}, u32[]{:S(2)}) copy-start(bf16[768,768]{1,0:T(8,128)(2,1)S(1)} %collective-permute-done.10.refs_6_) | copy-start | bytes 3538948
  89.6 98.5 %collective-permute-start.11 = (bf16[768,768]{1,0:T(8,128)(2,1)S(1)}, bf16[768,768]{1,0:T(8,128)(2,1)}, u32[]{:S(2)}, u32[]{:S(2)}) collective-permute-start(bf16[768,768]{1,0:T(8,128)(2,1)S(1)} %collective-permute-done.10.refs_6_), channel_id=1, source_target_pairs={{0,1},{1,0},{2,3},{3,2},{4,5},{5,4},{6,7},{7,6},{8,9},{9,8},{10,11... | collective-permute-start | bytes 3538952 | tf_op jit(solution)/shard_map/ppermute | solution.py:477
  90.0 38.7 %collective-permute-start.2 = (bf16[192,2304]{1,0:T(8,128)(2,1)}, bf16[192,2304]{1,0:T(8,128)(2,1)}, u32[]{:S(2)}, u32[]{:S(2)}) collective-permute-start(bf16[192,2304]{1,0:T(8,128)(2,1)} %collective-permute-done.1.refs_2_), channel_id=1, source_target_pairs={{0,1},{1,0},{2,3},{3,2},{4,5},{5,4},{6,7},{7,6},{8,9},{9,8},{10,11... | collective-permute-start | bytes 2654216 | tf_op jit(solution)/shard_map/ppermute | solution.py:477
  188.1 1.0 copy-start.3
  189.1 94.7 %copy-start.10 = (bf16[32,768]{1,0:T(8,128)(2,1)S(1)}, bf16[32,768]{1,0:T(8,128)(2,1)}, u32[]{:S(2)}) copy-start(bf16[32,768]{1,0:T(8,128)(2,1)} %get-tuple-element.36) | copy-start | bytes 147460
  227.1 98.0 %copy-start.5 = (bf16[32,768]{1,0:T(8,128)(2,1)S(1)}, bf16[32,768]{1,0:T(8,128)(2,1)}, u32[]{:S(2)}) copy-start(bf16[32,768]{1,0:T(8,128)(2,1)} %image_embed.1) | copy-start | bytes 147460
  227.1 302.3 %reduce-scatter.6.cloned.1.call-start = ((), (), s32[]{:S(2)}) async-start(), calls=%async_computation.9 | async-start | bytes 1622016 | tf_op jit(solution)/shard_map/reduce_scatter | solution.py:612
  283.7 41.3 %copy-start = (bf16[1024,768]{1,0:T(8,128)(2,1)S(1)}, bf16[1024,768]{1,0:T(8,128)(2,1)}, u32[]{:S(2)}) copy-start(bf16[1024,768]{1,0:T(8,128)(2,1)} %all-gather.2.cloned.1.call-done) | copy-start | bytes 4718596
  374.2 205.9 %reduce-scatter.4.cloned.1.call-start = ((), (), s32[]{:S(2)}) async-start(), calls=%async_computation.8 | async-start | bytes 4055040 | tf_op jit(solution)/shard_map/reduce_scatter | solution.py:612
  375.0 316.6 %reduce-scatter.8.cloned.1.call-start = ((), (), s32[]{:S(2)}) async-start(), calls=%async_computation.10 | async-start | bytes 4866048 | tf_op jit(solution)/shard_map/reduce_scatter | solution.py:612
  375.0 0.8 copy-start.11
  375.0 6.1 copy-start.9
  375.0 22.2 %copy-start.13 = (bf16[32,768]{1,0:T(8,128)(2,1)S(1)}, bf16[32,768]{1,0:T(8,128)(2,1)}, u32[]{:S(2)}) copy-start(bf16[32,768]{1,0:T(8,128)(2,1)} %get-tuple-element.49) | copy-start | bytes 147460
  376.6 11.5 %all-to-all-start.2 = ((bf16[32,8,96]{2,0,1:T(8,128)(2,1)}), bf16[32,8,96]{2,0,1:T(8,128)(2,1)S(1)}, u32[]{:S(2)}, u32[]{:S(2)}) async-start(bf16[32,8,96]{2,0,1:T(8,128)(2,1)} %copy.37), calls=%async_computation.5 | async-start | bytes 131072 | tf_op jit(solution)/shard_map/all_to_all | solution.py:615
  388.1 42.6 %all-to-all-start = ((bf16[32,8,384]{2,0,1:T(8,128)(2,1)}), bf16[32,8,384]{2,0,1:T(8,128)(2,1)S(1)}, u32[]{:S(2)}, u32[]{:S(2)}) async-start(bf16[32,8,384]{2,0,1:T(8,128)(2,1)} %bitcast.37), calls=%async_computation.3 | async-start | bytes 393216 | tf_op jit(solution)/shard_map/all_to_all | solution.py:615
  397.3 50.2 %copy-start.12 = (bf16[32,768]{1,0:T(8,128)(2,1)S(1)}, bf16[32,768]{1,0:T(8,128)(2,1)}, u32[]{:S(2)}) copy-start(bf16[32,768]{1,0:T(8,128)(2,1)} %get-tuple-element.51) | copy-start | bytes 147460
  430.6 48.9 %all-to-all-start.1 = ((bf16[256,4,192]{0,2,1:T(8,128)(2,1)}), bf16[256,4,192]{0,2,1:T(8,128)(2,1)S(1)}, u32[]{:S(2)}, u32[]{:S(2)}) async-start(bf16[256,4,192]{0,2,1:T(8,128)(2,1)} %bitcast.9), calls=%async_computation.4 | async-start | bytes 786432 | tf_op jit(solution)/shard_map/all_to_all | solution.py:620
  434.1 50.2 %copy-start.14 = (f32[8,768]{1,0:T(8,128)S(1)}, f32[8,768]{1,0:T(8,128)}, u32[]{:S(2)}) copy-start(f32[8,768]{1,0:T(8,128)} %get-tuple-element.44) | copy-start | bytes 73732
  479.5 47.8 %all-to-all-start.3 = ((bf16[256,4,192]{0,2,1:T(8,128)(2,1)}), bf16[256,4,192]{0,2,1:T(8,128)(2,1)S(1)}, u32[]{:S(2)}, u32[]{:S(2)}) async-start(bf16[256,4,192]{0,2,1:T(8,128)(2,1)} %bitcast.13), calls=%async_computation.6 | async-start | bytes 786432 | tf_op jit(solution)/shard_map/all_to_all | solution.py:620
Sparse Core Ops, SparseCore 0:
  227.2 56.4 all-gather.1
  374.4 97.4 reduce-scatter.5
  477.3 102.8 reduce-scatter.3
  585.5 105.9 reduce-scatter.7

commit v2 on v1

--- a/solution.py
+++ b/solution.py
@@ -17,6 +17,7 @@
 f32 = jnp.float32
 bf16 = jnp.bfloat16
 VMEM_LIMIT = 60 * 2**20
+MESH = pl.DeviceIdType.MESH
 
 
 def dot_nn(a, b):
@@ -196,140 +197,408 @@
     ).astype(bf16)
 
 
-def text_backward_kernel(
-    tok_ref, len_ref, key_bias_ref, gain1, bias1, gain2, bias2, embed_grad_ref, projected_ref,
-    heads_ref, mixed_ref, mid_ref, slope_ref, qkv_hbm, out_hbm, up_hbm, down_hbm, proj_hbm,
-    proj_grad_ref, branch_ref, up_grad_ref, out_grad_ref, qkv_grad_ref, input_grad_ref, norm_grad_ref,
-    w_qkv, w_out, w_up, w_down, w_proj, norm_ref, pre_grad_ref, wide_ref, mid_grad_ref, low_grad_ref,
-    mixed_grad_ref, heads_grad_ref, sems,
-):
-    tokens, width = tok_ref.shape
-    captions = len_ref.shape[0]
-    length = tokens // captions
-    wide = w_up.shape[1]
-    col_parts = up_grad_ref.shape[0]
-    pairs = ((proj_hbm, w_proj), (down_hbm, w_down), (up_hbm, w_up), (out_hbm, w_out), (qkv_hbm, w_qkv))
+def load_weights(pairs, sems):
     loads = [pltpu.make_async_copy(s, d, sems.at[i]) for i, (s, d) in enumerate(pairs)]
     for load in loads:
         load.start()
+    return loads
+
+
+def spans(count, size):
+    return lambda i: pl.ds(pl.multiple_of(i * size, size), size)
+
+
+def norm_backward(outer, unit, spread, gain):
+    outer = outer * gain
+    inner = outer - jnp.mean(outer, axis=-1, keepdims=True)
+    return spread * (inner - unit * jnp.mean(outer * unit, axis=-1, keepdims=True))
+
+
+class TextBackward:
     band = 128
 
-    @pl.loop(0, tokens // band)
-    def _(i):
-        rows = pl.ds(pl.multiple_of(i * band, band), band)
-        norm_ref[rows, :] = layer_norm(mid_ref[rows, :], gain2[...], bias2[...]).astype(bf16)
-
-    projected = projected_ref[...]
-    embed_grad = embed_grad_ref[...]
-    r = lax.rsqrt(jnp.sum(projected * projected, axis=-1, keepdims=True) + norm_eps)
-    along = jnp.sum(projected * embed_grad, axis=-1, keepdims=True)
-    proj_grad = (r * embed_grad - (r * r * r) * projected * along).astype(bf16)
-    proj_grad_ref[...] = proj_grad
-    loads[0].wait()
-    state_grad = dot_nt(proj_grad, w_proj[...]) * (1.0 / len_ref[...].astype(f32))
-    branch = state_grad.astype(bf16)
-    branch_ref[...] = branch
-    loads[1].wait()
-    loads[2].wait()
-
-    for part in range(col_parts):
-        step = wide // col_parts
-
-        @pl.loop(0, step // 256)
+    def __init__(self, names, refs):
+        for name, ref in zip(names, refs, strict=True):
+            setattr(self, name, ref)
+        self.tokens, self.width = self.tok.shape
+        self.captions = self.lens.shape[0]
+        self.length = self.tokens // self.captions
+        self.wide = self.w_up.shape[1]
+        pairs = (
+            (self.proj_hbm, self.w_proj), (self.down_hbm, self.w_down), (self.up_hbm, self.w_up),
+            (self.out_hbm, self.w_out), (self.qkv_hbm, self.w_qkv),
+        )
+        self.loads = load_weights(pairs, self.sems)
+
+    def rows(self, i):
+        return pl.ds(pl.multiple_of(i * self.band, self.band), self.band)
+
+    def bands(self, step):
+        pl.loop(0, self.tokens // self.band)(lambda i: step(self.rows(i)))
+
+    def project(self):
+        def renorm(rows):
+            self.norm[rows, :] = layer_norm(self.mid[rows, :], self.gain2[...], self.bias2[...]).astype(bf16)
+
+        self.bands(renorm)
+        projected = self.projected[...]
+        embed_grad = self.embed_grad[...]
+        r = lax.rsqrt(jnp.sum(projected * projected, axis=-1, keepdims=True) + norm_eps)
+        along = jnp.sum(projected * embed_grad, axis=-1, keepdims=True)
+        proj_grad = (r * embed_grad - (r * r * r) * projected * along).astype(bf16)
+        self.loads[0].wait()
+        state_grad = dot_nt(proj_grad, self.w_proj[...]) * (1.0 / self.lens[...].astype(f32))
+        self.branch[...] = state_grad.astype(bf16)
+        place = lax.broadcasted_iota(jnp.int32, (self.captions, self.length, 1), 1)
+        valid = (place < self.lens[...].reshape(self.captions, 1, 1)).astype(f32).reshape(self.tokens, 1)
+        self.mid_grad[...] = spread_rows(state_grad, self.length) * valid
+        return proj_grad, self.branch[...]
+
+    def inner(self, col_parts, store_up):
+        self.loads[1].wait()
+        branch = self.branch[...]
+        step = self.wide // col_parts
+        for part in range(col_parts):
+
+            @pl.loop(0, step // 256)
+            def _(j):
+                columns = pl.ds(pl.multiple_of(part * step + j * 256, 256), 256)
+                inner_grad = dot_nt(branch, self.w_down[columns, :])
+                pre_grad = spread_rows(inner_grad, self.length) * self.slope[:, columns].astype(f32)
+                pre_grad = pre_grad.astype(bf16)
+                self.pre_grad[:, columns] = pre_grad
+                local = pl.ds(pl.multiple_of(j * 256, 256), 256)
+                store_up(part, local, dot_tn(self.norm[...], pre_grad).astype(bf16))
+
+    def middle(self):
+        self.loads[2].wait()
+
+        @pl.loop(0, self.width // 256)
         def _(j):
-            columns = pl.ds(pl.multiple_of(part * step + j * 256, 256), 256)
-            inner_grad = dot_nt(branch, w_down[columns, :])
-            pre_grad = (spread_rows(inner_grad, length) * slope_ref[:, columns].astype(f32)).astype(bf16)
-            pre_grad_ref[:, columns] = pre_grad
-            local = pl.ds(pl.multiple_of(j * 256, 256), 256)
-            up_grad_ref[part, :, local] = dot_tn(norm_ref[...], pre_grad).astype(bf16)
-
-    place = lax.broadcasted_iota(jnp.int32, (captions, length, 1), 1)
-    valid = (place < len_ref[...].reshape(captions, 1, 1)).astype(f32).reshape(tokens, 1)
-
-    @pl.loop(0, width // 256)
-    def _(j):
-        columns = pl.ds(pl.multiple_of(j * 256, 256), 256)
-        wide_ref[:, columns] = dot_nt(pre_grad_ref[...], w_up[columns, :])
-
-    mid_grad_ref[...] = spread_rows(state_grad, length) * valid
-    norm_grad_ref[...] = jnp.zeros_like(norm_grad_ref)
-
-    @pl.loop(0, tokens // band)
-    def _(i):
-        rows = pl.ds(pl.multiple_of(i * band, band), band)
-        unit, spread = normed(mid_ref[rows, :])
-        outer = wide_ref[rows, :]
-        norm_grad_ref[2:3, :] += jnp.sum(outer * unit, axis=0, keepdims=True)
-        norm_grad_ref[3:4, :] += jnp.sum(outer, axis=0, keepdims=True)
-        outer = outer * gain2[...]
-        inner = outer - jnp.mean(outer, axis=-1, keepdims=True)
-        inner = inner - unit * jnp.mean(outer * unit, axis=-1, keepdims=True)
-        mid_grad = mid_grad_ref[rows, :] + spread * inner
-        mid_grad_ref[rows, :] = mid_grad
-        low_grad_ref[rows, :] = mid_grad.astype(bf16)
-
-    loads[3].wait()
-    step = width // col_parts
-    for part in range(col_parts):
-        out_grad_ref[part] = dot_tn(
-            mixed_ref[...], low_grad_ref[:, part * step : (part + 1) * step]
-        ).astype(bf16)
-
-    @pl.loop(0, tokens // band)
-    def _(i):
-        rows = pl.ds(pl.multiple_of(i * band, band), band)
-        mixed_grad_ref[rows, :] = dot_nt(low_grad_ref[rows, :], w_out[...]).astype(bf16)
-        norm_ref[rows, :] = layer_norm(tok_ref[rows, :].astype(f32), gain1[...], bias1[...]).astype(bf16)
-
-    first, second = lane_halves(128)
-    factor = (width // HEADS) ** -0.5
-
-    @pl.loop(0, tokens // band)
-    def _(block):
-        rows = pl.ds(pl.multiple_of(block * band, band), band)
-        bias = text_bias(key_bias_ref, block, band, length)
-        for pair in range(width // 128):
-            at = pair * 128
-            query = stack_heads(heads_ref[rows, at : at + 128], first, second)
-            key = heads_ref[rows, width + at : width + at + 128]
-            value = heads_ref[rows, 2 * width + at : 2 * width + at + 128]
-            grad = stack_heads(mixed_grad_ref[rows, at : at + 128], first, second)
-            weights, scale = soft_weights(query, key, bias, factor)
-            probs = weights * scale
-            prob_grad = dot_nt(grad, value)
-            total = jnp.sum(prob_grad * probs, axis=-1, keepdims=True)
-            score_grad = (probs * (prob_grad - total)).astype(bf16)
-            query_grad = join_heads(dot_nn(score_grad, key)) * factor
-            heads_grad_ref[rows, at : at + 128] = query_grad.astype(bf16)
-            key_grad = dot_tn(score_grad, query) * factor
-            heads_grad_ref[rows, width + at : width + at + 128] = key_grad.astype(bf16)
-            value_grad = dot_tn(probs.astype(bf16), grad)
-            heads_grad_ref[rows, 2 * width + at : 2 * width + at + 128] = value_grad.astype(bf16)
-
-    step = 3 * width // col_parts
-    for part in range(col_parts):
-        qkv_grad_ref[part] = dot_tn(
-            norm_ref[...], heads_grad_ref[:, part * step : (part + 1) * step]
-        ).astype(bf16)
-    loads[4].wait()
-
-    @pl.loop(0, width // 256)
-    def _(j):
-        columns = pl.ds(pl.multiple_of(j * 256, 256), 256)
-        wide_ref[:, columns] = dot_nt(heads_grad_ref[...], w_qkv[columns, :])
-
-    @pl.loop(0, tokens // band)
-    def _(i):
-        rows = pl.ds(pl.multiple_of(i * band, band), band)
-        unit, spread = normed(tok_ref[rows, :].astype(f32))
-        outer = wide_ref[rows, :]
-        norm_grad_ref[0:1, :] += jnp.sum(outer * unit, axis=0, keepdims=True)
-        norm_grad_ref[1:2, :] += jnp.sum(outer, axis=0, keepdims=True)
-        outer = outer * gain1[...]
-        inner = outer - jnp.mean(outer, axis=-1, keepdims=True)
-        inner = inner - unit * jnp.mean(outer * unit, axis=-1, keepdims=True)
-        input_grad_ref[rows, :] = (mid_grad_ref[rows, :] + spread * inner).astype(bf16)
+            columns = pl.ds(pl.multiple_of(j * 256, 256), 256)
+            self.outer[:, columns] = dot_nt(self.pre_grad[...], self.w_up[columns, :])
+
+        self.norm_grad[...] = jnp.zeros_like(self.norm_grad)
+
+        def through_norm(rows):
+            unit, spread = normed(self.mid[rows, :])
+            outer = self.outer[rows, :]
+            self.norm_grad[2:3, :] += jnp.sum(outer * unit, axis=0, keepdims=True)
+            self.norm_grad[3:4, :] += jnp.sum(outer, axis=0, keepdims=True)
+            mid_grad = self.mid_grad[rows, :] + norm_backward(outer, unit, spread, self.gain2[...])
+            self.mid_grad[rows, :] = mid_grad
+            self.low_grad[rows, :] = mid_grad.astype(bf16)
+
+        self.bands(through_norm)
+
+    def output(self, col_parts, store_out):
+        step = self.width // col_parts
+        for part in range(col_parts):
+            store_out(part, dot_tn(self.mixed[...], self.low_grad[:, part * step : (part + 1) * step]).astype(bf16))
+        self.loads[3].wait()
+
+        def through_out(rows):
+            self.mixed_grad[rows, :] = dot_nt(self.low_grad[rows, :], self.w_out[...]).astype(bf16)
+            norm = layer_norm(self.tok[rows, :].astype(f32), self.gain1[...], self.bias1[...])
+            self.norm[rows, :] = norm.astype(bf16)
+
+        self.bands(through_out)
+
+    def attention(self):
+        first, second = lane_halves(128)
+        width = self.width
+        factor = (width // HEADS) ** -0.5
+
+        @pl.loop(0, self.tokens // self.band)
+        def _(block):
+            rows = self.rows(block)
+            bias = text_bias(self.key_bias, block, self.band, self.length)
+            for pair in range(width // 128):
+                at = pair * 128
+                query = stack_heads(self.heads[rows, at : at + 128], first, second)
+                key = self.heads[rows, width + at : width + at + 128]
+                value = self.heads[rows, 2 * width + at : 2 * width + at + 128]
+                grad = stack_heads(self.mixed_grad[rows, at : at + 128], first, second)
+                weights, scale = soft_weights(query, key, bias, factor)
+                probs = weights * scale
+                prob_grad = dot_nt(grad, value)
+                total = jnp.sum(prob_grad * probs, axis=-1, keepdims=True)
+                score_grad = (probs * (prob_grad - total)).astype(bf16)
+                query_grad = join_heads(dot_nn(score_grad, key)) * factor
+                self.heads_grad[rows, at : at + 128] = query_grad.astype(bf16)
+                key_grad = dot_tn(score_grad, query) * factor
+                self.heads_grad[rows, width + at : width + at + 128] = key_grad.astype(bf16)
+                value_grad = dot_tn(probs.astype(bf16), grad)
+                self.heads_grad[rows, 2 * width + at : 2 * width + at + 128] = value_grad.astype(bf16)
+
+    def heads_weights(self, col_parts, store_qkv):
+        step = 3 * self.width // col_parts
+        for part in range(col_parts):
+            store_qkv(
+                part, dot_tn(self.norm[...], self.heads_grad[:, part * step : (part + 1) * step]).astype(bf16)
+            )
+
+    def input(self):
+        self.loads[4].wait()
+
+        @pl.loop(0, self.width // 256)
+        def _(j):
+            columns = pl.ds(pl.multiple_of(j * 256, 256), 256)
+            self.outer[:, columns] = dot_nt(self.heads_grad[...], self.w_qkv[columns, :])
+
+        def through_norm(rows):
+            unit, spread = normed(self.tok[rows, :].astype(f32))
+            outer = self.outer[rows, :]
+            self.norm_grad[0:1, :] += jnp.sum(outer * unit, axis=0, keepdims=True)
+            self.norm_grad[1:2, :] += jnp.sum(outer, axis=0, keepdims=True)
+            inner = norm_backward(outer, unit, spread, self.gain1[...])
+            self.input_grad[rows, :] = (self.mid_grad[rows, :] + inner).astype(bf16)
+
+        self.bands(through_norm)
+
+
+backward_ins = (
+    "tok", "lens", "key_bias", "gain1", "bias1", "gain2", "bias2", "embed_grad", "projected", "heads",
+    "mixed", "mid", "slope", "qkv_hbm", "out_hbm", "up_hbm", "down_hbm", "proj_hbm",
+)
+backward_scratch = (
+    "w_qkv", "w_out", "w_up", "w_down", "w_proj", "norm", "pre_grad", "outer", "mid_grad", "low_grad",
+    "mixed_grad", "heads_grad", "sems",
+)
+scatter_names = (
+    "held", "near", "x1", "y1", "x2", "y2", "far", "sends", "recvs",
+)
+exchange_names = (
+    "own", "all", "sends", "recvs",
+)
+
+
+def text_backward_kernel(*refs):
+    outs = ("proj_grad", "branch", "up_grad", "out_grad", "qkv_grad", "input_grad", "norm_grad")
+    t = TextBackward(backward_ins + outs + backward_scratch, refs)
+    parts = t.up_grad.shape[0]
+
+    def store_up(part, columns, value):
+        t.up_grad[part, :, columns] = value
+
+    def store_out(part, value):
+        t.out_grad[part] = value
+
+    def store_qkv(part, value):
+        t.qkv_grad[part] = value
+
+    t.proj_grad[...] = t.project()[0]
+    t.inner(parts, store_up)
+    t.middle()
+    t.output(parts, store_out)
+    t.attention()
+    t.heads_weights(parts, store_qkv)
+    t.input()
+
+
+class Place:
+    def __init__(self, z_count=4, y_count=2, x_count=2, k_count=2):
+        self.row, self.col = lax.axis_index("row"), lax.axis_index("col")
+        self.z, self.y = self.row // y_count, self.row % y_count
+        self.x, self.k = self.col // k_count, self.col % k_count
+        self.rows, self.cols = z_count * y_count, x_count * k_count
+        self.count = self.rows * self.cols
+        self.me = self.row * self.cols + self.col
+
+    def at(self, **moved):
+        z, y, x, k = (moved.get(name, getattr(self, name)) for name in "zyxk")
+        return z * 2 + y, x * 2 + k
+
+    def peer(self, distance):
+        other = (self.me + distance) % self.count
+        return other // self.cols, other % self.cols
+
+    def greet(self):
+        barrier = pltpu.get_barrier_semaphore()
+
+        @pl.loop(1, self.count)
+        def _(distance):
+            pl.semaphore_signal(barrier, inc=1, device_id=self.peer(distance), device_id_type=MESH)
+
+        pl.semaphore_wait(barrier, self.count - 1)
+
+
+def remote(src, dst, send, recv, to):
+    return pltpu.make_async_remote_copy(
+        src_ref=src, dst_ref=dst, send_sem=send, recv_sem=recv, device_id=to, device_id_type=MESH
+    )
+
+
+class Exchange:
+    def __init__(self, place, source, slots, sends, recvs):
+        self.place, self.source, self.slots, self.sends, self.recvs = place, source, slots, sends, recvs
+
+    def copy(self, distance):
+        to = self.place.peer(distance)
+        sems = self.sends.at[distance - 1], self.recvs.at[distance - 1]
+        return remote(self.source(to), self.slots.at[self.place.me], *sems, to)
+
+    def start(self):
+        pl.loop(1, self.place.count)(lambda distance: self.copy(distance).start())
+
+    def finish(self):
+        pl.loop(1, self.place.count)(lambda distance: self.copy(distance).wait())
+
+
+class GradientScatter:
+    def __init__(self, place, held, near, x1, y1, x2, y2, far, sends, recvs):
+        self.place, self.held, self.near, self.far = place, held, near, far
+        self.x1, self.y1, self.x2, self.y2 = x1, y1, x2, y2
+        self.sends, self.recvs = sends, recvs
+        half = held.shape[5] // 2
+        self.one, self.two = pl.ds(0, half), pl.ds(half, half)
+
+    def copy(self, n, src, dst, **moved):
+        return remote(src, dst, self.sends.at[n], self.recvs.at[n], self.place.at(**moved))
+
+    def copies(self, stage):
+        p, held = self.place, self.held
+        x, y, z, k = p.x, p.y, p.z, p.k
+        every = slice(None)
+        if stage == 0:
+            return [self.copy(0, held.at[:, 1 - k], self.near, k=1 - k)]
+        if stage == 1:
+            return [
+                self.copy(1, held.at[1 - x, k, :, :, :, self.one], self.x1, x=1 - x),
+                self.copy(2, held.at[:, k, :, 1 - y, :, self.two], self.y1, y=1 - y),
+            ]
+        if stage == 2:
+            return [
+                self.copy(3, held.at[x, k, :, 1 - y, :, self.one], self.y2, y=1 - y),
+                self.copy(4, held.at[1 - x, k, :, y, :, self.two], self.x2, x=1 - x),
+            ]
+        copies = []
+        for distance in range(1, held.shape[2]):
+            other = (z + distance) % held.shape[2]
+            copies.append(self.copy(4 + distance, held.at[x, k, other, y], self.far.at[distance - 1], z=other))
+        return copies
+
+    def start(self, stage):
+        for copy in self.copies(stage):
+            copy.start()
+
+    def finish(self, stage):
+        for copy in self.copies(stage):
+            copy.wait()
+        p, held = self.place, self.held
+        x, y, k = p.x, p.y, p.k
+        z_count = held.shape[2]
+
+        def add(target, source):
+            target[...] = (target[...].astype(f32) + source[...].astype(f32)).astype(bf16)
+
+        if stage == 0:
+            for i in range(2):
+                for j in range(2):
+                    pl.loop(0, z_count)(lambda z: add(held.at[i, k, z, j], self.near.at[i, z, j]))
+        if stage == 1:
+            for i in range(2):
+                pl.loop(0, z_count)(lambda z: add(held.at[x, k, z, i, :, self.one], self.x1.at[z, i]))
+                pl.loop(0, z_count)(lambda z: add(held.at[i, k, z, y, :, self.two], self.y1.at[i, z]))
+        if stage == 2:
+            pl.loop(0, z_count)(lambda z: add(held.at[x, k, z, y, :, self.one], self.y2.at[z]))
+            pl.loop(0, z_count)(lambda z: add(held.at[x, k, z, y, :, self.two], self.x2.at[z]))
+        if stage == 3:
+            total = held[x, k, p.z, y].astype(f32)
+            for i in range(z_count - 1):
+                total = total + self.far[i].astype(f32)
+            return total
+
+
+def scatter_scratch(rows, columns):
+    shapes = [
+        (2, 2, 4, 2, rows, columns), (2, 4, 2, rows, columns), (4, 2, rows, columns // 2), (2, 4, rows, columns // 2),
+        (4, rows, columns // 2), (4, rows, columns // 2), (3, rows, columns),
+    ]
+    return [pltpu.VMEM(shape, bf16) for shape in shapes] + [pltpu.SemaphoreType.DMA((8,))] * 2
+
+
+def text_backward_joined_kernel(*refs):
+    ins = backward_ins + ("factors", "loss")
+    outs = ("up_out", "out_out", "qkv_out", "down_out", "proj_out", "input_grad", "norm_out")
+    sets = tuple(name + tag for tag in ("_a", "_b") for name in scatter_names)
+    swaps = tuple(name + tag for tag in ("_factors", "_late", "_last") for name in exchange_names)
+    names = ins + outs + backward_scratch + sets + ("branch", "norm_grad") + swaps
+    t = TextBackward(names, refs)
+    place = Place()
+    width = t.width
+    scatter_a, scatter_b = (
+        GradientScatter(place, *(getattr(t, name + tag) for name in scatter_names)) for tag in ("_a", "_b")
+    )
+    factors = Exchange(
+        place, lambda to: t.own_factors.at[to[1]], t.all_factors, t.sends_factors, t.recvs_factors
+    )
+    late = Exchange(place, lambda to: t.own_late, t.all_late, t.sends_late, t.recvs_late)
+    last = Exchange(place, lambda to: t.own_last, t.all_last, t.sends_last, t.recvs_last)
+    cols = place.cols
+
+    def blocked(value):
+        return value.reshape(4, 2, value.shape[0] // 8, value.shape[1])
+
+    def store_up(part, columns, value):
+        t.held_a[part // 2, part % 2, :, :, :, columns] = blocked(value)
+
+    qkv_step, out_step = 3 * width // cols, width // cols
+
+    def store_out(part, value):
+        t.held_b[part // 2, part % 2, :, :, :, qkv_step:] = blocked(value)
+
+    def store_qkv(part, value):
+        t.held_b[part // 2, part % 2, :, :, :, :qkv_step] = blocked(value)
+
+    proj_grad, branch = t.project()
+    for part in range(cols):
+        columns = slice(part * out_step, (part + 1) * out_step)
+        t.own_factors[part] = jnp.concatenate([branch[:, columns], proj_grad[:, columns]], axis=1)
+    t.all_factors[place.me] = t.own_factors[place.col]
+    place.greet()
+    factors.start()
+    t.inner(cols, store_up)
+    scatter_a.start(0)
+    t.middle()
+    scatter_a.finish(0)
+    scatter_a.start(1)
+    t.own_late[...] = jnp.concatenate([t.norm_grad[2:3, :], t.norm_grad[3:4, :], t.loss[...]], axis=1)
+    t.all_late[place.me] = t.own_late[...]
+    late.start()
+    t.output(cols, store_out)
+    scatter_a.finish(1)
+    scatter_a.start(2)
+    t.attention()
+    t.heads_weights(cols, store_qkv)
+    scatter_b.start(0)
+    scatter_a.finish(2)
+    scatter_a.start(3)
+    scatter_b.finish(0)
+    scatter_b.start(1)
+    t.input()
+    t.own_last[...] = jnp.concatenate([t.norm_grad[0:1, :], t.norm_grad[1:2, :]], axis=1)
+    t.all_last[place.me] = t.own_last[...]
+    scatter_b.finish(1)
+    scatter_b.start(2)
+    last.start()
+    t.up_out[...] = scatter_a.finish(3)
+    factors.finish()
+    grown = dot_tn(
+        t.factors[...].reshape(-1, t.factors.shape[2]), t.all_factors[...].reshape(-1, t.all_factors.shape[2])
+    )
+    inner_step = t.wide // place.rows
+    t.down_out[...] = grown[:inner_step, :out_step]
+    t.proj_out[...] = grown[inner_step : inner_step + width // place.rows, out_step:]
+    late.finish()
+    scatter_b.finish(2)
+    scatter_b.start(3)
+    last.finish()
+    t.norm_out[:, : 2 * width] = jnp.sum(t.all_last[...], axis=0)
+    t.norm_out[:, 2 * width :] = jnp.sum(t.all_late[...], axis=0)
+    total = scatter_b.finish(3)
+    t.qkv_out[...] = total[:, :qkv_step]
+    t.out_out[...] = total[:, qkv_step:]
 
 
 def group_mean(images, rows):
@@ -579,37 +848,20 @@
     positives = logit_scale * jnp.sum(image_own * text_embed.astype(f32), axis=1)
     loss_part = 0.5 * jnp.sum(jnp.log(col_sums) - 2.0 * positives)
 
-    (proj_grad, branch, up_grad, out_grad, qkv_grad, input_grad, norm_grads) = plain(
-        text_backward_kernel,
-        (
-            array((captions, width), bf16),
-            array((captions, width), bf16),
-            array((col_count, width, wide // col_count), bf16),
-            array((col_count, width, width // col_count), bf16),
-            array((col_count, width, 3 * width // col_count), bf16),
-            array((tokens, width), bf16),
-            array((8, width), f32),
-        ),
-        [in_vmem] * 13 + [anywhere] * 5,
-        weight_scratch
-        + [
-            pltpu.VMEM((tokens, width), bf16),
-            pltpu.VMEM((tokens, wide), bf16),
-            pltpu.VMEM((tokens, width), f32),
-            pltpu.VMEM((tokens, width), f32),
-            pltpu.VMEM((tokens, width), bf16),
-            pltpu.VMEM((tokens, width), bf16),
-            pltpu.VMEM((tokens, 3 * width), bf16),
-            pltpu.SemaphoreType.DMA((5,)),
-        ],
-        "text_backward",
-    )(
+    backward_in = (
         text_tokens, lengths, key_bias, *vectors, embed_grad, projected, heads, mixed, mid, slope, *weights,
     )
-
-    def scattered(matrix):
-        blocks = matrix.reshape(col_count * row_count, width // row_count, matrix.shape[2])
-        return lax.psum_scatter(blocks, ("col", "row"), scatter_dimension=0, tiled=True)[0].astype(f32)
+    backward_specs = [in_vmem] * 13 + [anywhere] * 5
+    backward_buffers = weight_scratch + [
+        pltpu.VMEM((tokens, width), bf16),
+        pltpu.VMEM((tokens, wide), bf16),
+        pltpu.VMEM((tokens, width), f32),
+        pltpu.VMEM((tokens, width), f32),
+        pltpu.VMEM((tokens, width), bf16),
+        pltpu.VMEM((tokens, width), bf16),
+        pltpu.VMEM((tokens, 3 * width), bf16),
+        pltpu.SemaphoreType.DMA((5,)),
+    ]
 
     def by_row(x):
         x = lax.all_to_all(x, "row", split_axis=1, concat_axis=0, tiled=True)
@@ -619,13 +871,82 @@
         x = lax.all_gather(x, "row", axis=0, tiled=True)
         return lax.all_to_all(x, "col", split_axis=1, concat_axis=0, tiled=True)
 
-    grad_down = dot_tn(by_row(inner_sum), by_col(branch))
-    grad_proj = dot_tn(by_row(pooled), by_col(proj_grad))
-    loss_total, norm_total = lax.psum((loss_part, norm_grads), both)
+    count = row_count * col_count
+    if (row_count, col_count) == (8, 4):
+        row_blocks = [inner_sum.reshape(captions, row_count, -1), pooled.reshape(captions, row_count, -1)]
+        packed = jnp.concatenate(row_blocks, axis=2)
+        packed = jnp.pad(packed, ((0, 0), (0, 0), (0, -packed.shape[2] % 128))).transpose(1, 0, 2)
+        packed = lax.all_to_all(packed, "row", split_axis=0, concat_axis=0)
+        factors = lax.all_gather(packed, "col", axis=1).reshape(count, captions, -1)
+        out_step, inner_step = width // col_count, wide // row_count
+        rows = width // row_count
+        up_grad, out_grad, qkv_grad, grad_down, grad_proj, input_grad, norm_total = plain(
+            text_backward_joined_kernel,
+            (
+                array((rows, wide // col_count), f32),
+                array((rows, out_step), f32),
+                array((rows, 3 * out_step), f32),
+                array((inner_step, out_step), f32),
+                array((rows, out_step), f32),
+                array((tokens, width), bf16),
+                array((1, 4 * width + 128), f32),
+            ),
+            backward_specs + [in_vmem] * 2,
+            backward_buffers
+            + scatter_scratch(rows, wide // col_count)
+            + scatter_scratch(rows, 4 * out_step)
+            + [
+                pltpu.VMEM((captions, width), bf16),
+                pltpu.VMEM((8, width), f32),
+                pltpu.VMEM((col_count, captions, 2 * out_step), bf16),
+                pltpu.VMEM((count, captions, 2 * out_step), bf16),
+                pltpu.SemaphoreType.DMA((count - 1,)),
+                pltpu.SemaphoreType.DMA((count - 1,)),
+                pltpu.VMEM((1, 2 * width + 128), f32),
+                pltpu.VMEM((count, 1, 2 * width + 128), f32),
+                pltpu.SemaphoreType.DMA((count - 1,)),
+                pltpu.SemaphoreType.DMA((count - 1,)),
+                pltpu.VMEM((1, 2 * width), f32),
+                pltpu.VMEM((count, 1, 2 * width), f32),
+                pltpu.SemaphoreType.DMA((count - 1,)),
+                pltpu.SemaphoreType.DMA((count - 1,)),
+            ],
+            "text_backward_joined",
+            collective_id=3,
+            has_side_effects=True,
+        )(*backward_in, factors, jnp.full((1, 128), loss_part))
+        norm_total = norm_total[0]
+        norms = [norm_total[i * width : (i + 1) * width] for i in range(4)]
+        loss_total = norm_total[4 * width]
+    else:
+        (proj_grad, branch, up_grad, out_grad, qkv_grad, input_grad, norm_grads) = plain(
+            text_backward_kernel,
+            (
+                array((captions, width), bf16),
+                array((captions, width), bf16),
+                array((col_count, width, wide // col_count), bf16),
+                array((col_count, width, width // col_count), bf16),
+                array((col_count, width, 3 * width // col_count), bf16),
+                array((tokens, width), bf16),
+                array((8, width), f32),
+            ),
+            backward_specs,
+            backward_buffers,
+            "text_backward",
+        )(*backward_in)
+
+        def scattered(matrix):
+            blocks = matrix.reshape(count, width // row_count, matrix.shape[2])
+            return lax.psum_scatter(blocks, ("col", "row"), scatter_dimension=0, tiled=True)[0].astype(f32)
+
+        up_grad, out_grad, qkv_grad = scattered(up_grad), scattered(out_grad), scattered(qkv_grad)
+        grad_down = dot_tn(by_row(inner_sum), by_col(branch))
+        grad_proj = dot_tn(by_row(pooled), by_col(proj_grad))
+        loss_total, norm_total = lax.psum((loss_part, norm_grads), both)
+        norms = [norm_total[i] for i in range(4)]
     mean_loss = (loss_total + 0.5 * jnp.sum(jnp.log(row_sums))) / pair_total
     return (
-        mean_loss, hidden, input_grad, norm_total[0], norm_total[1], norm_total[2], norm_total[3],
-        scattered(qkv_grad), scattered(out_grad), scattered(up_grad), grad_down, grad_proj,
+        mean_loss, hidden, input_grad, *norms, qkv_grad, out_grad, up_grad, grad_down, grad_proj,
     )
 
 

time: 702 us -> 449 us (0.64)
  waiting for transfers between devices: 298 us -> 116 us
  blocking collectives: 162 us -> 54.6 us
  Pallas kernels: 176 us -> 230 us
  starting transfers between devices: 23.1 us -> 6.61 us
    reduce_scatter x3 -> x0, waiting for transfers between devices: 159 us -> none  [scattered(): lax.psum_scatter(blocks, ('col', 'row'), scatter_dimension=0, tiled=True)[0]]
    all_gather x4 -> x0, blocking collectives: 82.6 us -> none  [the longest x2 63.6 us: by_col(): x = lax.all_gather(x, 'row', axis=0, tiled=True)]
    pallas_call x1, Pallas kernels: 48.1 us -> 102 us  [body(): plain(text_backward_joined_kernel, (array((rows, wide // col_count), f32)...]
    psum x1 -> x0, blocking collectives: 40.5 us -> none  [body(): loss_total, norm_total = lax.psum((loss_part, norm_grads), both)]
    all_to_all x0 -> x1, blocking collectives: none -> 15.4 us  [body(): packed = lax.all_to_all(packed, 'row', split_axis=0, concat_axis=0)]
    all_gather x1, waiting for transfers between devices: 56.6 us -> 41.2 us  [body(): image_all = lax.all_gather(image_embed, both, axis=0, tiled=True)]
    all_to_all x4 -> x0, starting transfers between devices: 14.9 us -> none  [the longest x2 7.97 us: by_row(): x = lax.all_to_all(x, 'row', split_axis=1, concat_axis=0, tiled=True)]
  transfers between devices with their start and end apart: 20 -> 14, of which waited for: 6 -> 5; matrix products, arithmetic and copies ran while one was open for 3% -> 3% of each run, Pallas kernels for 13% -> 20%
where the time goes in v2:
time: 449 us; the launch traced here: 448 us
  Pallas kernels  230 us (51%)
  waiting for transfers between devices  116 us (26%)
  blocking collectives  54.6 us (12%)
  local copies, waits for them, and re-layouts  18 us (4%)
  between operations  17.4 us (4%)
  starting transfers between devices  6.61 us (1%)
    pallas_call x1, Pallas kernels, body(): plain(text_backward_joined_kernel, (array((rows, wide // col_count), f32)...  102 us
    ppermute x4, waiting for transfers between devices, partners(): far = lax.ppermute(x, 'col', order)  71.2 us
    pallas_call x1, Pallas kernels, body(): pl.pallas_call(functools.partial(image_mix_kernel, col_count), grid=(grou...  59.4 us
    all_gather x1, waiting for transfers between devices, body(): image_all = lax.all_gather(image_embed, both, axis=0, tiled=True)  41.2 us
    psum x1, blocking collectives, body(): row_sums = lax.psum(jnp.sum(lifted, axis=1), both)  39.2 us
    pallas_call x1, Pallas kernels, body(): pl.pallas_call(functools.partial(image_embed_kernel, col_count), grid=(gr...  38 us
    pallas_call x1, Pallas kernels, body(): plain(text_forward_kernel, (array((tokens, width), bf16), array((captions...  30.7 us
    all_to_all x1, blocking collectives, body(): packed = lax.all_to_all(packed, 'row', split_axis=0, concat_axis=0)  15.4 us
  transfers between devices with their start and end apart: 14, of which 5 were waited for; matrix products, arithmetic and copies ran while one was open for 3% of the time, Pallas kernels for 20%

profile of v2, /device:TPU:0, one launch (start us, length us, event | category | flops | bytes accessed | tf_op | source)
XLA Modules:
  0.0 448.1 jit_solution(886666087174310415)
XLA Ops:
  7.2 0.0 all-gather.4.cloned.1.call-start
  7.2 3.0 collective-permute-start.10
  10.2 0.1 collective-permute-start.7
  10.3 1.9 collective-permute-start.4
  12.3 0.1 collective-permute-start.1
  12.3 56.5 %collective-permute-done.4.refs_6_ = bf16[192,768]{1,0:T(8,128)(2,1)S(1)} collective-permute-done((bf16[192,768]{1,0:T(8,128)(2,1)}, bf16[192,768]{1,0:T(8,128)(2,1)S(1)}, u32[]{:S(2)}, u32[]{:S(2)}) %collective-permute-start.4) | collective-permute-done | bytes 294944 | tf_op jit(solution)/shard_map/ppermute | solution.py:745
  68.8 1.8 collective-permute-done.3.refs_5_
  70.6 0.1 collective-permute-start.5
  70.8 1.4 collective-permute-done.5.refs_7_
  72.2 0.1 collective-permute-start.6
  72.4 14.7 %collective-permute-done.1.refs_2_ = bf16[192,2304]{1,0:T(8,128)(2,1)} collective-permute-done((bf16[192,2304]{1,0:T(8,128)(2,1)}, bf16[192,2304]{1,0:T(8,128)(2,1)}, u32[]{:S(2)}, u32[]{:S(2)}) %collective-permute-start.1) | collective-permute-done | bytes 884768 | tf_op jit(solution)/shard_map/ppermute | solution.py:745
  87.1 0.5 collective-permute-start.11
  87.6 0.1 collective-permute-start.8
  87.7 0.5 collective-permute-start.2
  88.2 0.7 fusion.10
  89.0 0.6 select_n.15.key_bias_ref.refs_2_
  89.6 1.3 copy.38.len_ref.refs_1_
  91.0 1.3 reshape.87.gain1.refs_3_
  92.2 1.3 reshape.88.bias1.refs_4_
  93.5 1.3 reshape.89.gain2.refs_5_
  94.8 1.3 reshape.90.bias2.refs_6_
  96.0 30.7 %text_forward.1 = (bf16[512,768]{1,0:T(8,128)(2,1)}, bf16[32,768]{1,0:T(8,128)(2,1)}, f32[32,768]{1,0:T(8,128)}, bf16[32,768]{1,0:T(8,128)(2,1)}, bf16[32,3072]{...) custom-call(bf16[512,768]{1,0:T(8,128)(2,1)} %refs_0_.5, ...), custom_call_target="tpu_custom_call" | custom-call | tf_op jit(solution)/shard_map/text_forward/pallas_call | solution.py:775
  126.7 59.4 %image_mix.1 = (bf16[1600,768]{1,0:T(8,128)(2,1)}, f32[32,768]{1,0:T(8,128)}) custom-call(bf16[1600,768]{1,0:T(8,128)(2,1)} %tok_ref.2, f32[2,768]{1,0:T(2,128)} %gain_ref.1, f32[2,768]{1,0:T(2,128)} %bias_ref.1, bf16[192,2304]{1,0:T(8,128)(2,1)} %refs_0_.3, bf16[192,2304]{1,0:T(8,128)(2,1)} %collective-permute-done.refs_1_, ...), custom_call_target="tpu_custom_call" | custom-call | tf_op jit(solution)/shard_map/image_mix/pallas_call | solution.py:798
  186.1 1.0 copy-done.3
  187.2 38.0 %image_embed.1 = bf16[32,768]{1,0:T(8,128)(2,1)} custom-call(bf16[1600,768]{1,0:T(8,128)(2,1)} %get-tuple-element.34.normed_ref, f32[32,768]{1,0:T(8,128)} %get-tuple-element.35.mean_ref, bf16[192,3072]{1,0:T(8,128)(2,1)} %refs_0_.4, bf16[192,3072]{1,0:T(8,128)(2,1)} %copy-done.3, bf16[192,3072]{1,0:T(8,128)(2,1)} %copy-done.2, ...), custom_call_target="tpu_custom_call" | custom-call | tf_op jit(solution)/shard_map/image_embed/pallas_call | solution.py:823
  225.2 0.0 copy-start.4
  225.2 0.0 all-gather.4.cloned.1.call-update
  225.2 0.0 all-gather.6.cloned.1.call-start
  225.3 0.1 reshape.92
  225.5 15.4 %all_to_all.5 = bf16[8,32,512]{2,1,0:T(8,128)(2,1)} all-to-all(bf16[8,32,512]{2,1,0:T(8,128)(2,1)S(1)} %fusion.5), channel_id=1, replica_groups=mesh['row'=8,'col'=4] {'row'}, dimensions={0} | all-to-all | bytes 524288 | tf_op jit(solution)/shard_map/all_to_all | solution.py:879
  240.9 0.0 all-gather.6.cloned.1.call-update
  241.0 0.1 fusion.6
  241.1 41.2 %all-gather.4.cloned.1.call-done = bf16[1024,768]{1,0:T(8,128)(2,1)} async-done(((bf16[32,768]{1,0:T(8,128)(2,1)}), bf16[1024,768]{1,0:T(8,128)(2,1)}) %all-gather.4.cloned.1.call-update) | async-done | bytes 1572880 | tf_op jit(solution)/shard_map/all_gather | solution.py:840
  282.3 2.2 fusion.12
  284.5 0.6 subtract_reduce_fusion
  285.8 39.2 %psum.7 = f32[1024]{0:T(1024)S(1)} all-reduce(f32[1024]{0:T(1024)S(1)} %get-tuple-element.76), channel_id=1, replica_groups=mesh['row'=8,'col'=4] {'row','col'}, use_global_device_ids=true, to_apply=%region_1.2 | all-reduce | flops 1024 | bytes 8192 | tf_op jit(solution)/shard_map/psum | solution.py:843
  325.0 1.1 fusion.1.refs_7_
  326.1 0.5 broadcast_in_dim.15.refs_19_
  326.6 102.4 %text_backward_joined.1 = (f32[96,768]{1,0:T(8,128)}, f32[96,192]{1,0:T(8,128)}, f32[96,576]{1,0:T(8,128)}, f32[384,192]{1,0:T(8,128)}, f32[96,192]{1,0:T(8,128)...) custom-call(bf16[512,768]{1,0:T(8,128)(2,1)} %refs_0_.5, s32[32,1]{1,0:T(8,128)} %copy.38.len_ref.refs_1_, ...), custom_call_target="tpu_custom_call" | custom-call | tf_op jit(solution)/shard_map/text_backward_joined/pallas_call | solution.py:883
  429.0 1.4 slice_reduce_fusion
  430.4 1.2 slice.28
  431.6 0.6 log_reduce_fusion
  432.2 1.9 copy.39
  435.4 2.1 copy.48
  437.4 0.7 copy.49
  438.1 0.6 copy.50
  438.8 0.7 copy.51
  439.5 0.6 copy.52
  (43 shorter events, 0.1 us)
Async XLA Ops:
  7.2 275.2 %all-gather.4.cloned.1.call-start = ((), (), s32[]{:S(2)}) async-start(), calls=%async_computation.1 | async-start | bytes 1622016 | tf_op jit(solution)/shard_map/all_gather | solution.py:840
  7.2 79.9 %collective-permute-start.10 = (bf16[768,768]{1,0:T(8,128)(2,1)}, bf16[768,768]{1,0:T(8,128)(2,1)S(1)}, u32[]{:S(2)}, u32[]{:S(2)}) collective-permute-start(bf16[768,768]{1,0:T(8,128)(2,1)} %refs_4_.3), channel_id=1, source_target_pairs={{0,2},{1,3},{2,0},{3,1},{4,6},{5,7},{6,4},{7,5},{8,10},{9,11},{10,... | collective-permute-start | bytes 3538952 | tf_op jit(solution)/shard_map/ppermute | solution.py:745
  10.2 77.4 %collective-permute-start.7 = (bf16[192,3072]{1,0:T(8,128)(2,1)}, bf16[192,3072]{1,0:T(8,128)(2,1)S(1)}, u32[]{:S(2)}, u32[]{:S(2)}) collective-permute-start(bf16[192,3072]{1,0:T(8,128)(2,1)} %refs_0_.4), channel_id=1, source_target_pairs={{0,2},{1,3},{2,0},{3,1},{4,6},{5,7},{6,4},{7,5},{8,10},{9,11},{10,... | collective-permute-start | bytes 3538952 | tf_op jit(solution)/shard_map/ppermute | solution.py:745
  10.3 58.5 %collective-permute-start.4 = (bf16[192,768]{1,0:T(8,128)(2,1)}, bf16[192,768]{1,0:T(8,128)(2,1)S(1)}, u32[]{:S(2)}, u32[]{:S(2)}) collective-permute-start(bf16[192,768]{1,0:T(8,128)(2,1)} %refs_4_.2), channel_id=1, source_target_pairs={{0,2},{1,3},{2,0},{3,1},{4,6},{5,7},{6,4},{7,5},{8,10},{9,11},{10,... | collective-permute-start | bytes 884744 | tf_op jit(solution)/shard_map/ppermute | solution.py:745
  12.3 74.8 %collective-permute-start.1 = (bf16[192,2304]{1,0:T(8,128)(2,1)}, bf16[192,2304]{1,0:T(8,128)(2,1)}, u32[]{:S(2)}, u32[]{:S(2)}) collective-permute-start(bf16[192,2304]{1,0:T(8,128)(2,1)} %refs_0_.3), channel_id=1, source_target_pairs={{0,2},{1,3},{2,0},{3,1},{4,6},{5,7},{6,4},{7,5},{8,10},{9,11},{10,... | collective-permute-start | bytes 2654216 | tf_op jit(solution)/shard_map/ppermute | solution.py:745
  12.3 75.4 %collective-permute-start = (bf16[192,2304]{1,0:T(8,128)(2,1)}, bf16[192,2304]{1,0:T(8,128)(2,1)}, u32[]{:S(2)}, u32[]{:S(2)}) collective-permute-start(bf16[192,2304]{1,0:T(8,128)(2,1)} %refs_0_.3), channel_id=1, source_target_pairs={{0,1},{1,0},{2,3},{3,2},{4,5},{5,4},{6,7},{7,6},{8,9},{9,8},{10,11... | collective-permute-start | bytes 2654216 | tf_op jit(solution)/shard_map/ppermute | solution.py:746
  68.8 18.8 %copy-start.6 = (bf16[192,768]{1,0:T(8,128)(2,1)}, bf16[192,768]{1,0:T(8,128)(2,1)S(1)}, u32[]{:S(2)}) copy-start(bf16[192,768]{1,0:T(8,128)(2,1)S(1)} %collective-permute-done.4.refs_6_) | copy-start | bytes 884740
  68.8 1.8 collective-permute-start.3
  70.6 17.1 %copy-start.7 = (bf16[192,768]{1,0:T(8,128)(2,1)}, bf16[192,768]{1,0:T(8,128)(2,1)S(1)}, u32[]{:S(2)}) copy-start(bf16[192,768]{1,0:T(8,128)(2,1)S(1)} %collective-permute-done.3.refs_5_) | copy-start | bytes 884740
  70.6 1.6 collective-permute-start.5
  72.2 15.5 %copy-start.8 = (bf16[192,768]{1,0:T(8,128)(2,1)}, bf16[192,768]{1,0:T(8,128)(2,1)S(1)}, u32[]{:S(2)}) copy-start(bf16[192,768]{1,0:T(8,128)(2,1)S(1)} %collective-permute-done.5.refs_7_) | copy-start | bytes 884740
  72.2 113.9 %collective-permute-start.6 = (bf16[192,3072]{1,0:T(8,128)(2,1)}, bf16[192,3072]{1,0:T(8,128)(2,1)S(1)}, u32[]{:S(2)}, u32[]{:S(2)}) collective-permute-start(bf16[192,3072]{1,0:T(8,128)(2,1)} %refs_0_.4), channel_id=1, source_target_pairs={{0,1},{1,0},{2,3},{3,2},{4,5},{5,4},{6,7},{7,6},{8,9},{9,8},{10,11... | collective-permute-start | bytes 3538952 | tf_op jit(solution)/shard_map/ppermute | solution.py:746
  87.1 99.0 %collective-permute-start.9 = (bf16[768,768]{1,0:T(8,128)(2,1)}, bf16[768,768]{1,0:T(8,128)(2,1)}, u32[]{:S(2)}, u32[]{:S(2)}) collective-permute-start(bf16[768,768]{1,0:T(8,128)(2,1)} %refs_4_.3), channel_id=1, source_target_pairs={{0,1},{1,0},{2,3},{3,2},{4,5},{5,4},{6,7},{7,6},{8,9},{9,8},{10,11... | collective-permute-start | bytes 3538952 | tf_op jit(solution)/shard_map/ppermute | solution.py:746
  87.1 39.6 %copy-start.1 = (bf16[768,768]{1,0:T(8,128)(2,1)}, bf16[768,768]{1,0:T(8,128)(2,1)S(1)}, u32[]{:S(2)}) copy-start(bf16[768,768]{1,0:T(8,128)(2,1)S(1)} %collective-permute-done.10.refs_6_) | copy-start | bytes 3538948
  87.1 99.0 %collective-permute-start.11 = (bf16[768,768]{1,0:T(8,128)(2,1)S(1)}, bf16[768,768]{1,0:T(8,128)(2,1)}, u32[]{:S(2)}, u32[]{:S(2)}) collective-permute-start(bf16[768,768]{1,0:T(8,128)(2,1)S(1)} %collective-permute-done.10.refs_6_), channel_id=1, source_target_pairs={{0,1},{1,0},{2,3},{3,2},{4,5},{5,4},{6,7},{7,6},{8,9},{9,8},{10,11... | collective-permute-start | bytes 3538952 | tf_op jit(solution)/shard_map/ppermute | solution.py:746
  87.6 39.1 %copy-start.2 = (bf16[192,3072]{1,0:T(8,128)(2,1)}, bf16[192,3072]{1,0:T(8,128)(2,1)S(1)}, u32[]{:S(2)}) copy-start(bf16[192,3072]{1,0:T(8,128)(2,1)S(1)} %collective-permute-done.7.refs_2_) | copy-start | bytes 3538948
  87.6 98.5 %collective-permute-start.8 = (bf16[192,3072]{1,0:T(8,128)(2,1)S(1)}, bf16[192,3072]{1,0:T(8,128)(2,1)}, u32[]{:S(2)}, u32[]{:S(2)}) collective-permute-start(bf16[192,3072]{1,0:T(8,128)(2,1)S(1)} %collective-permute-done.7.refs_2_), channel_id=1, source_target_pairs={{0,1},{1,0},{2,3},{3,2},{4,5},{5,4},{6,7},{7,6},{8,9},{9,8},{10,11... | collective-permute-start | bytes 3538952 | tf_op jit(solution)/shard_map/ppermute | solution.py:746
  87.7 39.0 %collective-permute-start.2 = (bf16[192,2304]{1,0:T(8,128)(2,1)}, bf16[192,2304]{1,0:T(8,128)(2,1)}, u32[]{:S(2)}, u32[]{:S(2)}) collective-permute-start(bf16[192,2304]{1,0:T(8,128)(2,1)} %collective-permute-done.1.refs_2_), channel_id=1, source_target_pairs={{0,1},{1,0},{2,3},{3,2},{4,5},{5,4},{6,7},{7,6},{8,9},{9,8},{10,11... | collective-permute-start | bytes 2654216 | tf_op jit(solution)/shard_map/ppermute | solution.py:746
  186.1 1.1 copy-start.3
  187.2 38.1 %copy-start.10 = (bf16[32,3072]{1,0:T(8,128)(2,1)S(1)}, bf16[32,3072]{1,0:T(8,128)(2,1)}, u32[]{:S(2)}) copy-start(bf16[32,3072]{1,0:T(8,128)(2,1)} %get-tuple-element.42) | copy-start | bytes 589828
  187.2 38.2 %copy-start.14 = (bf16[32,768]{1,0:T(8,128)(2,1)S(1)}, bf16[32,768]{1,0:T(8,128)(2,1)}, u32[]{:S(2)}) copy-start(bf16[32,768]{1,0:T(8,128)(2,1)} %get-tuple-element.43) | copy-start | bytes 147460
  225.2 15.8 %copy-start.4 = (bf16[32,768]{1,0:T(8,128)(2,1)S(1)}, bf16[32,768]{1,0:T(8,128)(2,1)}, u32[]{:S(2)}) copy-start(bf16[32,768]{1,0:T(8,128)(2,1)} %image_embed.1) | copy-start | bytes 147460
  225.2 15.8 %copy-start.11 = (bf16[32,768]{1,0:T(8,128)(2,1)S(1)}, bf16[32,768]{1,0:T(8,128)(2,1)}, u32[]{:S(2)}) copy-start(bf16[32,768]{1,0:T(8,128)(2,1)} %get-tuple-element.36) | copy-start | bytes 147460
  225.2 100.8 %all-gather.6.cloned.1.call-start = ((), (), s32[]{:S(2)}) async-start(), calls=%async_computation.2 | async-start | bytes 1310720 | tf_op jit(solution)/shard_map/all_gather | solution.py:880
  282.3 42.7 %copy-start = (bf16[1024,768]{1,0:T(8,128)(2,1)S(1)}, bf16[1024,768]{1,0:T(8,128)(2,1)}, u32[]{:S(2)}) copy-start(bf16[1024,768]{1,0:T(8,128)(2,1)} %all-gather.4.cloned.1.call-done) | copy-start | bytes 4718596
  428.9 8.5 %copy-start.9 = (f32[96,576]{1,0:T(8,128)S(1)}, f32[96,576]{1,0:T(8,128)}, u32[]{:S(2)}) copy-start(f32[96,576]{1,0:T(8,128)} %get-tuple-element.102) | copy-start | bytes 663556
  429.0 9.2 %copy-start.13 = (f32[96,192]{1,0:T(8,128)S(1)}, f32[96,192]{1,0:T(8,128)}, u32[]{:S(2)}) copy-start(f32[96,192]{1,0:T(8,128)} %get-tuple-element.103) | copy-start | bytes 221188
  429.0 9.8 %copy-start.5 = (f32[96,768]{1,0:T(8,128)S(1)}, f32[96,768]{1,0:T(8,128)}, u32[]{:S(2)}) copy-start(f32[96,768]{1,0:T(8,128)} %get-tuple-element.104) | copy-start | bytes 884740
  434.0 5.5 %copy-start.12 = (f32[96,192]{1,0:T(8,128)S(1)}, f32[96,192]{1,0:T(8,128)}, u32[]{:S(2)}) copy-start(f32[96,192]{1,0:T(8,128)} %get-tuple-element.106) | copy-start | bytes 221188
Sparse Core Ops, SparseCore 0:
  225.3 56.9 all-gather.3
  283.9 16.0 all-gather.5

commit v3 on v2

--- a/solution.py
+++ b/solution.py
@@ -1,5 +1,6 @@
 import functools
 import math
+from types import SimpleNamespace
 
 import jax
 import jax.numpy as jnp
@@ -91,6 +92,23 @@
     return weights, 1.0 / jnp.sum(weights, axis=-1, keepdims=True)
 
 
+def set_lengths(lengths_ref, lens_ref, key_bias_ref):
+    captions, tokens = lens_ref.shape[0], key_bias_ref.shape[1]
+    length = tokens // captions
+    caption = lax.broadcasted_iota(jnp.int32, (captions, 1), 0)
+    token = lax.broadcasted_iota(jnp.int32, (1, tokens), 1)
+    column, row = jnp.zeros((captions, 1), jnp.int32), jnp.zeros((1, tokens), jnp.int32)
+    for n in range(captions):
+        column = jnp.where(caption == n, lengths_ref[n], column)
+        row = jnp.where(token // length == n, lengths_ref[n], row)
+    lens_ref[...] = column
+    key_bias_ref[...] = jnp.where(token % length < row, 0.0, masked_score)
+
+
+def as_row(ref):
+    return ref[...].reshape(1, ref.shape[0])
+
+
 def text_bias(key_bias_ref, block, rows, length):
     near = lax.broadcasted_iota(jnp.int32, (rows, rows), 0) // length
     far = lax.broadcasted_iota(jnp.int32, (rows, rows), 1) // length
@@ -111,12 +129,13 @@
     return jnp.broadcast_to(x[:, None, :], (rows, length, width)).reshape(rows * length, width)
 
 
-def text_forward_kernel(
-    tok_ref, len_ref, key_bias_ref, gain1, bias1, gain2, bias2, qkv_hbm, out_hbm, up_hbm, down_hbm, proj_hbm,
+def text_forward(
+    after_up, tok_ref, lengths_ref, gain1, bias1, gain2, bias2, qkv_hbm, out_hbm, up_hbm, down_hbm, proj_hbm,
     hidden_ref, embed_ref, projected_ref, pooled_ref, inner_sum_ref, heads_ref, mixed_ref, mid_ref, slope_ref,
-    w_qkv, w_out, w_up, w_down, w_proj, norm_ref, inner_ref, sems,
+    w_qkv, w_out, w_up, w_down, w_proj, norm_ref, inner_ref, len_ref, key_bias_ref, sems,
 ):
     tokens, width = tok_ref.shape
+    set_lengths(lengths_ref, len_ref, key_bias_ref)
     captions = len_ref.shape[0]
     length = tokens // captions
     wide = w_up.shape[1]
@@ -130,7 +149,7 @@
     @pl.loop(0, tokens // band)
     def _(i):
         rows = pl.ds(pl.multiple_of(i * band, band), band)
-        norm_ref[rows, :] = layer_norm(tok_ref[rows, :].astype(f32), gain1[...], bias1[...]).astype(bf16)
+        norm_ref[rows, :] = layer_norm(tok_ref[rows, :].astype(f32), as_row(gain1), as_row(bias1)).astype(bf16)
 
     loads[0].wait()
 
@@ -161,7 +180,7 @@
         rows = pl.ds(pl.multiple_of(i * band, band), band)
         mid = tok_ref[rows, :].astype(f32) + dot_nn(mixed_ref[rows, :], w_out[...])
         mid_ref[rows, :] = mid
-        norm_ref[rows, :] = layer_norm(mid, gain2[...], bias2[...]).astype(bf16)
+        norm_ref[rows, :] = layer_norm(mid, as_row(gain2), as_row(bias2)).astype(bf16)
 
     loads[2].wait()
     chosen = member(len_ref, captions, tokens)
@@ -178,6 +197,7 @@
         slope_ref[:, columns] = (slope * valid).astype(bf16)
         inner_sum_ref[:, columns] = dot_nn(chosen_low, value).astype(bf16)
 
+    after_up()
     loads[3].wait()
     inverse = 1.0 / len_ref[...].astype(f32)
 
@@ -197,6 +217,24 @@
     ).astype(bf16)
 
 
+def text_forward_kernel(*refs):
+    text_forward(lambda: None, *refs)
+
+
+def text_forward_joined_kernel(*refs):
+    ins, shards, outs, wholes = refs[:11], refs[11:13], refs[13:22], refs[22:24]
+    scratch, sems = refs[24:-3], refs[-3:]
+    place = Place()
+    place.greet_near()
+    gathers = [Gather(place, *pair, *(sem.at[i] for sem in sems)) for i, pair in enumerate(zip(shards, wholes))]
+    for gather in gathers:
+        gather.start()
+    text_forward(gathers[0].relay, *ins, *outs, *scratch)
+    gathers[1].relay()
+    for gather in gathers:
+        gather.finish()
+
+
 def load_weights(pairs, sems):
     loads = [pltpu.make_async_copy(s, d, sems.at[i]) for i, (s, d) in enumerate(pairs)]
     for load in loads:
@@ -222,6 +260,7 @@
             setattr(self, name, ref)
         self.tokens, self.width = self.tok.shape
         self.captions = self.lens.shape[0]
+        set_lengths(self.lengths, self.lens, self.key_bias)
         self.length = self.tokens // self.captions
         self.wide = self.w_up.shape[1]
         pairs = (
@@ -238,7 +277,7 @@
 
     def project(self):
         def renorm(rows):
-            self.norm[rows, :] = layer_norm(self.mid[rows, :], self.gain2[...], self.bias2[...]).astype(bf16)
+            self.norm[rows, :] = layer_norm(self.mid[rows, :], as_row(self.gain2), as_row(self.bias2)).astype(bf16)
 
         self.bands(renorm)
         projected = self.projected[...]
@@ -285,7 +324,7 @@
             outer = self.outer[rows, :]
             self.norm_grad[2:3, :] += jnp.sum(outer * unit, axis=0, keepdims=True)
             self.norm_grad[3:4, :] += jnp.sum(outer, axis=0, keepdims=True)
-            mid_grad = self.mid_grad[rows, :] + norm_backward(outer, unit, spread, self.gain2[...])
+            mid_grad = self.mid_grad[rows, :] + norm_backward(outer, unit, spread, as_row(self.gain2))
             self.mid_grad[rows, :] = mid_grad
             self.low_grad[rows, :] = mid_grad.astype(bf16)
 
@@ -299,7 +338,7 @@
 
         def through_out(rows):
             self.mixed_grad[rows, :] = dot_nt(self.low_grad[rows, :], self.w_out[...]).astype(bf16)
-            norm = layer_norm(self.tok[rows, :].astype(f32), self.gain1[...], self.bias1[...])
+            norm = layer_norm(self.tok[rows, :].astype(f32), as_row(self.gain1), as_row(self.bias1))
             self.norm[rows, :] = norm.astype(bf16)
 
         self.bands(through_out)
@@ -351,19 +390,20 @@
             outer = self.outer[rows, :]
             self.norm_grad[0:1, :] += jnp.sum(outer * unit, axis=0, keepdims=True)
             self.norm_grad[1:2, :] += jnp.sum(outer, axis=0, keepdims=True)
-            inner = norm_backward(outer, unit, spread, self.gain1[...])
+            inner = norm_backward(outer, unit, spread, as_row(self.gain1))
             self.input_grad[rows, :] = (self.mid_grad[rows, :] + inner).astype(bf16)
 
         self.bands(through_norm)
 
 
 backward_ins = (
-    "tok", "lens", "key_bias", "gain1", "bias1", "gain2", "bias2", "embed_grad", "projected", "heads",
+    "tok", "lengths", "gain1", "bias1", "gain2", "bias2", "embed_grad", "projected", "heads",
     "mixed", "mid", "slope", "qkv_hbm", "out_hbm", "up_hbm", "down_hbm", "proj_hbm",
 )
 backward_scratch = (
     "w_qkv", "w_out", "w_up", "w_down", "w_proj", "norm", "pre_grad", "outer", "mid_grad", "low_grad",
-    "mixed_grad", "heads_grad", "sems",
+    "mixed_grad", "heads_grad",
+    "lens", "key_bias", "sems",
 )
 scatter_names = (
     "held", "near", "x1", "y1", "x2", "y2", "far", "sends", "recvs",
@@ -422,11 +462,46 @@
 
         pl.semaphore_wait(barrier, self.count - 1)
 
+    def greet_near(self):
+        barrier = pltpu.get_barrier_semaphore()
+        for other in (self.at(k=1 - self.k), self.at(x=1 - self.x)):
+            pl.semaphore_signal(barrier, inc=1, device_id=other, device_id_type=MESH)
+        pl.semaphore_wait(barrier, 2)
+
 
 def remote(src, dst, send, recv, to):
     return pltpu.make_async_remote_copy(
         src_ref=src, dst_ref=dst, send_sem=send, recv_sem=recv, device_id=to, device_id_type=MESH
     )
+
+
+class Gather:
+    def __init__(self, place, shard, whole, local, sends, recvs):
+        depth = shard.shape[0]
+
+        def block(col):
+            return whole.at[pl.ds(pl.multiple_of(col * depth, depth), depth)]
+
+        own, across = block(place.col), block(place.at(x=1 - place.x)[1])
+        mate, next_chip = place.at(k=1 - place.k), place.at(x=1 - place.x)
+        self.local = pltpu.make_async_copy(shard, own, local)
+        self.near = remote(shard, own, sends.at[0], recvs.at[0], mate)
+        self.far = remote(shard, own, sends.at[1], recvs.at[1], next_chip)
+        self.passed = remote(across, across, sends.at[2], recvs.at[2], mate)
+
+    def start(self):
+        self.far.start()
+        self.near.start()
+        self.local.start()
+
+    def relay(self):
+        self.far.wait()
+        self.passed.start()
+
+    def finish(self):
+        self.local.wait()
+        self.near.wait()
+        self.passed.wait()
 
 
 class Exchange:
@@ -617,26 +692,10 @@
     return copies
 
 
-def image_mix_kernel(
-    col_count, tok_ref, gain_ref, bias_ref, *refs,
-):
-    qkv_parts, out_parts = refs[:col_count], refs[col_count : 2 * col_count]
-    normed_ref, mean_ref, w_qkv, w_out, norm_ref, heads_ref, mixed_ref, sems = refs[2 * col_count :]
-    rows, width = tok_ref.shape
+def image_mix(tokens, gain_ref, bias_ref, w_qkv, w_out, norm_ref, heads_ref, mixed_ref):
+    rows, width = tokens.shape
     images = rows // IMG_TOK
-    step = pl.program_id(0)
-    col = lax.axis_index("col")
-
-    @pl.when(step == 0)
-    def _():
-        copies = load_parts(qkv_parts, w_qkv, sems.at[0], col, col_count)
-        copies += load_parts(out_parts, w_out, sems.at[1], col, col_count)
-        for copy in copies:
-            copy.start()
-        for copy in copies:
-            copy.wait()
-
-    norm_ref[...] = layer_norm(tok_ref[...].astype(f32), gain_ref[0:1, :], bias_ref[0:1, :]).astype(bf16)
+    norm_ref[...] = layer_norm(tokens.astype(f32), gain_ref[0:1, :], bias_ref[0:1, :]).astype(bf16)
 
     @pl.loop(0, 3 * width // 256)
     def _(j):
@@ -671,11 +730,28 @@
                 mixed_ref[low : low + 16, pl.ds(at, 128)] = jnp.where(keep, former, mixed[:16]).astype(bf16)
                 mixed_ref[low + 16 : low + window, pl.ds(at, 128)] = mixed[16:].astype(bf16)
 
-    mid = tok_ref[...].astype(f32) + dot_nn(mixed_ref[...], w_out[...])
-    normed_ref[...] = layer_norm(mid, gain_ref[1:2, :], bias_ref[1:2, :]).astype(bf16)
+    mid = tokens.astype(f32) + dot_nn(mixed_ref[...], w_out[...])
     high, low = split_low(mid)
     select = group_mean(images, rows)
-    mean_ref[...] = (dot_nn(select, high) + dot_nn(select, low)) * (1.0 / IMG_TOK)
+    mean = (dot_nn(select, high) + dot_nn(select, low)) * (1.0 / IMG_TOK)
+    return layer_norm(mid, gain_ref[1:2, :], bias_ref[1:2, :]).astype(bf16), mean
+
+
+def image_mix_kernel(col_count, tok_ref, gain_ref, bias_ref, *refs):
+    qkv_parts, out_parts = refs[:col_count], refs[col_count : 2 * col_count]
+    normed_ref, mean_ref, w_qkv, w_out, *buffers, sems = refs[2 * col_count :]
+    col = lax.axis_index("col")
+
+    @pl.when(pl.program_id(0) == 0)
+    def _():
+        copies = load_parts(qkv_parts, w_qkv, sems.at[0], col, col_count)
+        copies += load_parts(out_parts, w_out, sems.at[1], col, col_count)
+        for copy in copies:
+            copy.start()
+        for copy in copies:
+            copy.wait()
+
+    normed_ref[...], mean_ref[...] = image_mix(tok_ref[...], gain_ref, bias_ref, w_qkv, w_out, *buffers)
 
 
 def image_embed_kernel(col_count, normed_ref, mean_ref, *refs):
@@ -715,20 +791,136 @@
         ).astype(bf16)
 
 
+image_names = (
+    "tok", "gain", "bias", "qkv_hbm", "out_hbm", "up_hbm", "down_hbm", "text_embed", "own_factors",
+    "embed_grad", "all_factors", "loss",
+    "w_qkv", "w_out", "w_up", "w_down", "norm", "heads", "mixed", "normed", "mean", "sums", "own", "images",
+    "own_sums", "all_sums", "loads", "local", "sends", "recvs", "factor_sends", "factor_recvs", "factor_local",
+    "image_sends", "image_recvs", "pass_sends", "pass_recvs", "sum_sends", "sum_recvs",
+)
+
+
+def image_joined_kernel(*refs):
+    t = SimpleNamespace(**dict(zip(image_names, refs, strict=True)))
+    place = Place()
+    loads = load_weights(((t.qkv_hbm, t.w_qkv), (t.out_hbm, t.w_out)), t.loads)
+    place.greet()
+    up, down = (
+        Gather(place, shard, target, t.local.at[i], t.sends.at[i], t.recvs.at[i])
+        for i, (shard, target) in enumerate(((t.up_hbm, t.w_up), (t.down_hbm, t.w_down)))
+    )
+    up.start()
+    rows, width = t.tok.shape
+    group_rows = t.norm.shape[0]
+    groups = rows // group_rows
+    group_images = group_rows // IMG_TOK
+    for load in loads:
+        load.wait()
+
+    @pl.loop(0, groups)
+    def _(group):
+        span = pl.ds(pl.multiple_of(group * group_rows, 16), group_rows)
+        normed2, mean = image_mix(
+            t.tok[span, :], t.gain, t.bias, t.w_qkv, t.w_out, t.norm, t.heads, t.mixed
+        )
+        t.normed[span, :] = normed2
+        t.mean[pl.ds(pl.multiple_of(group * group_images, 8), group_images), :] = mean
+
+        @pl.when(group == groups // 2)
+        def _():
+            up.relay()
+            down.start()
+
+    factors = Exchange(
+        place, lambda to: t.own_factors.at[to[0]], t.all_factors, t.factor_sends, t.factor_recvs
+    )
+    own_factor = pltpu.make_async_copy(
+        t.own_factors.at[place.row], t.all_factors.at[place.me], t.factor_local.at[0]
+    )
+    own_factor.start()
+    factors.start()
+    up.finish()
+
+    halves, _, chips, half_images, _ = t.images.shape
+    half_rows = half_images * IMG_TOK
+    wide = t.w_up.shape[1]
+    select = group_mean(half_images, half_rows)
+    chip = place.row * 2 + place.x
+
+    def image_copy(half, distance):
+        other = (chip + distance) % chips
+        mine = t.images.at[half, place.k, chip]
+        sems = t.image_sends.at[half, distance - 1], t.image_recvs.at[half, distance - 1]
+        return remote(mine, mine, *sems, (other // 2, other % 2 * 2 + place.k))
+
+    def pass_copy(half):
+        held = t.images.at[half, place.k]
+        return remote(held, held, t.pass_sends.at[half], t.pass_recvs.at[half], place.at(k=1 - place.k))
+
+    for half in range(halves):
+        span = slice(half * half_rows, (half + 1) * half_rows)
+
+        @pl.loop(0, wide // 256)
+        def _(j):
+            columns = pl.ds(pl.multiple_of(j * 256, 256), 256)
+            inner = gelu(dot_nn(t.normed[span, :], t.w_up[:, columns])).astype(bf16)
+            t.sums[:, columns] = dot_nn(select, inner)
+
+        if half == 0:
+            down.relay()
+            down.finish()
+        else:
+            pl.loop(1, chips)(lambda distance: image_copy(half - 1, distance).wait())
+            pass_copy(half - 1).start()
+        high, low = split_low(t.sums[...] * (1.0 / IMG_TOK))
+        pooled = dot_nn(jnp.concatenate([high, low], axis=0), t.w_down[...])
+        part = slice(half * half_images, (half + 1) * half_images)
+        pooled = t.mean[part, :] + pooled[:half_images] + pooled[half_images:]
+        embed = pooled * lax.rsqrt(jnp.sum(pooled * pooled, axis=-1, keepdims=True) + norm_eps)
+        t.own[part, :] = embed.astype(bf16)
+        t.images[half, place.k, chip] = embed.astype(bf16)
+        pl.loop(1, chips)(lambda distance: image_copy(half, distance).start())
+
+    pl.loop(1, chips)(lambda distance: image_copy(halves - 1, distance).wait())
+    pass_copy(halves - 1).start()
+    for half in range(halves):
+        pass_copy(half).wait()
+
+    images = t.images[...].reshape(-1, width)
+    own = t.own[...].astype(f32)
+    lifted = jnp.exp2(dot_nt(t.text_embed[...], images) * (logit_scale * log2e))
+    col_sums = jnp.sum(lifted, axis=1, keepdims=True)
+    t.own_sums[...] = jnp.sum(lifted, axis=0, keepdims=True)
+    t.all_sums[place.me] = t.own_sums[...]
+    sums = Exchange(place, lambda to: t.own_sums, t.all_sums, t.sum_sends, t.sum_recvs)
+    sums.start()
+    positives = logit_scale * jnp.sum(own * t.text_embed[...].astype(f32), axis=(0, 1), keepdims=True)
+    sums.finish()
+    row_sums = jnp.sum(t.all_sums[...], axis=0)
+    sim_grad = (0.5 * (lifted * (1.0 / row_sums) + lifted * (1.0 / col_sums))).astype(bf16)
+    t.embed_grad[...] = logit_scale * (dot_nn(sim_grad, images) - own)
+    logs = jnp.sum(jnp.log(col_sums), axis=(0, 1), keepdims=True)
+    logs = logs + jnp.sum(jnp.log(row_sums), axis=(0, 1), keepdims=True) * (1.0 / place.count)
+    t.loss[...] = jnp.broadcast_to(0.5 * logs - positives, t.loss.shape)
+    own_factor.wait()
+    factors.finish()
+
+
 def whole(shape):
     return pl.BlockSpec(shape, lambda *_: (0,) * len(shape))
 
 
 in_vmem = pl.BlockSpec(memory_space=pltpu.VMEM)
+in_smem = pl.BlockSpec(memory_space=pltpu.SMEM)
 anywhere = pl.BlockSpec(memory_space=pl.ANY)
 
 
-def plain(kernel, outs, ins, scratch, name, **settings):
+def plain(kernel, outs, ins, scratch, name, out_specs=None, **settings):
     return pl.pallas_call(
         kernel,
         out_shape=outs,
         in_specs=ins,
-        out_specs=[in_vmem] * len(outs),
+        out_specs=out_specs or [in_vmem] * len(outs),
         scratch_shapes=scratch,
         compiler_params=pltpu.CompilerParams(vmem_limit_bytes=VMEM_LIMIT, **settings),
         name=name,
@@ -760,98 +952,150 @@
     pair_total = captions * row_count * col_count
     image_rows, images = image_tokens.shape[0], image_tokens.shape[0] // IMG_TOK
 
-    qkv_parts = partners(image_qkv, col_count)
-    out_parts = partners(image_out, col_count)
-    up_parts = partners(image_up, col_count)
-    down_parts = partners(image_down, col_count)
-
-    lengths = text_lengths.reshape(captions, 1)
-    place = lax.broadcasted_iota(jnp.int32, (captions, length), 1)
-    key_bias = jnp.where(place < lengths, 0.0, masked_score).reshape(1, tokens)
-    vectors = [v.reshape(1, width) for v in (norm1_gain, norm1_bias, norm2_gain, norm2_bias)]
+    count = row_count * col_count
+    joined = (row_count, col_count) == (8, 4)
+    vectors = (norm1_gain, norm1_bias, norm2_gain, norm2_bias)
     weights = (text_qkv, text_out, text_up, text_down, text_proj)
     weight_scratch = [pltpu.VMEM(w.shape, bf16) for w in weights]
 
-    (hidden, text_embed, projected, pooled, inner_sum, heads, mixed, mid, slope) = plain(
-        text_forward_kernel,
-        (
-            array((tokens, width), bf16),
-            array((captions, width), bf16),
-            array((captions, width), f32),
-            array((captions, width), bf16),
-            array((captions, wide), bf16),
-            array((tokens, 3 * width), bf16),
-            array((tokens, width), bf16),
-            array((tokens, width), f32),
-            array((tokens, wide), bf16),
-        ),
-        [in_vmem] * 7 + [anywhere] * 5,
-        weight_scratch
-        + [pltpu.VMEM((tokens, width), bf16), pltpu.VMEM((tokens, wide), bf16), pltpu.SemaphoreType.DMA((5,))],
-        "text_forward",
-    )(text_tokens, lengths, key_bias, *vectors, *weights)
-
+    text_outs = (
+        array((tokens, width), bf16),
+        array((captions, width), bf16),
+        array((captions, width), f32),
+        array((captions, width), bf16),
+        array((captions, wide), bf16),
+        array((tokens, 3 * width), bf16),
+        array((tokens, width), bf16),
+        array((tokens, width), f32),
+        array((tokens, wide), bf16),
+    )
+    text_specs = [in_vmem, in_smem] + [in_vmem] * 4 + [anywhere] * 5
+    text_buffers = weight_scratch + [
+        pltpu.VMEM((tokens, width), bf16),
+        pltpu.VMEM((tokens, wide), bf16),
+        pltpu.VMEM((captions, 1), jnp.int32),
+        pltpu.VMEM((1, tokens), f32),
+        pltpu.SemaphoreType.DMA((5,)),
+    ]
+    text_in = (text_tokens, text_lengths, *vectors, *weights)
     groups = 4
     group_rows, group_images = image_rows // groups, images // groups
-    parts = [anywhere] * (2 * col_count)
-    image_tokens, text_embed = lax.optimization_barrier((image_tokens, text_embed))
-    image_normed, image_mean = pl.pallas_call(
-        functools.partial(image_mix_kernel, col_count),
-        grid=(groups,),
-        out_shape=(array((image_rows, width), bf16), array((images, width), f32)),
-        in_specs=[
-            pl.BlockSpec((group_rows, width), lambda i: (i, 0)),
-            whole(image_norm_gain.shape),
-            whole(image_norm_bias.shape),
-        ]
-        + parts,
-        out_specs=(
-            pl.BlockSpec((group_rows, width), lambda i: (i, 0)),
-            pl.BlockSpec((group_images, width), lambda i: (i, 0)),
-        ),
-        scratch_shapes=[
-            pltpu.VMEM((width, 3 * width), bf16),
-            pltpu.VMEM((width, width), bf16),
-            pltpu.VMEM((group_rows, width), bf16),
-            pltpu.VMEM((group_rows, 3 * width), bf16),
-            pltpu.VMEM((group_rows, width), bf16),
-            pltpu.SemaphoreType.DMA((2, col_count)),
-        ],
-        compiler_params=pltpu.CompilerParams(vmem_limit_bytes=VMEM_LIMIT),
-        name="image_mix",
-    )(image_tokens, image_norm_gain, image_norm_bias, *qkv_parts, *out_parts)
-    image_embed = pl.pallas_call(
-        functools.partial(image_embed_kernel, col_count),
-        grid=(groups,),
-        out_shape=array((images, width), bf16),
-        in_specs=[pl.BlockSpec((group_rows, width), lambda i: (i, 0)), whole((images, width))] + parts,
-        out_specs=whole((images, width)),
-        scratch_shapes=[
-            pltpu.VMEM((width, wide), bf16),
-            pltpu.VMEM((wide, width), bf16),
-            pltpu.VMEM((images, wide), f32),
-            pltpu.SemaphoreType.DMA((2, col_count)),
-        ],
-        compiler_params=pltpu.CompilerParams(vmem_limit_bytes=VMEM_LIMIT),
-        name="image_embed",
-    )(image_normed, image_mean, *up_parts, *down_parts)
-
+    mix_buffers = [
+        pltpu.VMEM((group_rows, width), bf16),
+        pltpu.VMEM((group_rows, 3 * width), bf16),
+        pltpu.VMEM((group_rows, width), bf16),
+    ]
+    mix_weights = [pltpu.VMEM((width, 3 * width), bf16), pltpu.VMEM((width, width), bf16)]
+    embed_weights = [pltpu.VMEM((width, wide), bf16), pltpu.VMEM((wide, width), bf16)]
     both = ("row", "col")
-    image_all = lax.all_gather(image_embed, both, axis=0, tiled=True)
-    sims = logit_scale * dot_nt(image_all, text_embed)
-    lifted = jnp.exp(sims)
-    row_sums = lax.psum(jnp.sum(lifted, axis=1), both)
-    col_sums = jnp.sum(lifted, axis=0)
-    sim_grad = (0.5 * (lifted / row_sums[:, None] + lifted / col_sums[None, :])).astype(bf16)
-    image_own = image_embed.astype(f32)
-    embed_grad = logit_scale * (dot_tn(sim_grad, image_all) - image_own)
-    positives = logit_scale * jnp.sum(image_own * text_embed.astype(f32), axis=1)
-    loss_part = 0.5 * jnp.sum(jnp.log(col_sums) - 2.0 * positives)
+
+    if joined:
+        *text_results, whole_qkv, whole_out = plain(
+            text_forward_joined_kernel,
+            text_outs + (array((width, 3 * width), bf16), array((width, width), bf16)),
+            text_specs + [anywhere] * 2,
+            text_buffers + [pltpu.SemaphoreType.DMA((2,))] + [pltpu.SemaphoreType.DMA((2, 3))] * 2,
+            "text_forward_joined",
+            out_specs=[in_vmem] * len(text_outs) + [anywhere] * 2,
+            collective_id=1,
+            has_side_effects=True,
+        )(*text_in, image_qkv, image_out)
+        (hidden, text_embed, projected, pooled, inner_sum, heads, mixed, mid, slope) = text_results
+        row_blocks = [inner_sum.reshape(captions, row_count, -1), pooled.reshape(captions, row_count, -1)]
+        packed = jnp.concatenate(row_blocks, axis=2)
+        packed = jnp.pad(packed, ((0, 0), (0, 0), (0, -packed.shape[2] % 128))).transpose(1, 0, 2)
+        chips, halves = count // 2, 2
+        embed_grad, factors, loss_part = plain(
+            image_joined_kernel,
+            (array((captions, width), f32), array((count, *packed.shape[1:]), bf16), array((1, 128), f32)),
+            [in_vmem] * 3 + [anywhere] * 4 + [in_vmem] * 2,
+            mix_weights
+            + embed_weights
+            + mix_buffers
+            + [
+                pltpu.VMEM((image_rows, width), bf16),
+                pltpu.VMEM((images, width), f32),
+                pltpu.VMEM((images // halves, wide), f32),
+                pltpu.VMEM((images, width), bf16),
+                pltpu.VMEM((halves, 2, chips, images // halves, width), bf16),
+                pltpu.VMEM((1, pair_total), f32),
+                pltpu.VMEM((count, 1, pair_total), f32),
+                pltpu.SemaphoreType.DMA((2,)),
+                pltpu.SemaphoreType.DMA((2,)),
+                pltpu.SemaphoreType.DMA((2, 3)),
+                pltpu.SemaphoreType.DMA((2, 3)),
+                pltpu.SemaphoreType.DMA((count - 1,)),
+                pltpu.SemaphoreType.DMA((count - 1,)),
+                pltpu.SemaphoreType.DMA((1,)),
+                pltpu.SemaphoreType.DMA((halves, chips - 1)),
+                pltpu.SemaphoreType.DMA((halves, chips - 1)),
+                pltpu.SemaphoreType.DMA((halves,)),
+                pltpu.SemaphoreType.DMA((halves,)),
+                pltpu.SemaphoreType.DMA((count - 1,)),
+                pltpu.SemaphoreType.DMA((count - 1,)),
+            ],
+            "image_joined",
+            out_specs=[in_vmem, anywhere, in_vmem],
+            collective_id=2,
+            has_side_effects=True,
+        )(
+            image_tokens, image_norm_gain, image_norm_bias, whole_qkv, whole_out, image_up, image_down,
+            text_embed, packed,
+        )
+    else:
+        (hidden, text_embed, projected, pooled, inner_sum, heads, mixed, mid, slope) = plain(
+            text_forward_kernel, text_outs, text_specs, text_buffers, "text_forward"
+        )(*text_in)
+        qkv_parts = partners(image_qkv, col_count)
+        out_parts = partners(image_out, col_count)
+        up_parts = partners(image_up, col_count)
+        down_parts = partners(image_down, col_count)
+        parts = [anywhere] * (2 * col_count)
+        image_normed, image_mean = pl.pallas_call(
+            functools.partial(image_mix_kernel, col_count),
+            grid=(groups,),
+            out_shape=(array((image_rows, width), bf16), array((images, width), f32)),
+            in_specs=[
+                pl.BlockSpec((group_rows, width), lambda i: (i, 0)),
+                whole(image_norm_gain.shape),
+                whole(image_norm_bias.shape),
+            ]
+            + parts,
+            out_specs=(
+                pl.BlockSpec((group_rows, width), lambda i: (i, 0)),
+                pl.BlockSpec((group_images, width), lambda i: (i, 0)),
+            ),
+            scratch_shapes=mix_weights + mix_buffers + [pltpu.SemaphoreType.DMA((2, col_count))],
+            compiler_params=pltpu.CompilerParams(vmem_limit_bytes=VMEM_LIMIT),
+            name="image_mix",
+        )(image_tokens, image_norm_gain, image_norm_bias, *qkv_parts, *out_parts)
+        image_embed = pl.pallas_call(
+            functools.partial(image_embed_kernel, col_count),
+            grid=(groups,),
+            out_shape=array((images, width), bf16),
+            in_specs=[pl.BlockSpec((group_rows, width), lambda i: (i, 0)), whole((images, width))] + parts,
+            out_specs=whole((images, width)),
+            scratch_shapes=embed_weights
+            + [pltpu.VMEM((images, wide), f32), pltpu.SemaphoreType.DMA((2, col_count))],
+            compiler_params=pltpu.CompilerParams(vmem_limit_bytes=VMEM_LIMIT),
+            name="image_embed",
+        )(image_normed, image_mean, *up_parts, *down_parts)
+
+        image_all = lax.all_gather(image_embed, both, axis=0, tiled=True)
+        lifted = jnp.exp(logit_scale * dot_nt(image_all, text_embed))
+        row_sums = lax.psum(jnp.sum(lifted, axis=1), both)
+        col_sums = jnp.sum(lifted, axis=0)
+        sim_grad = (0.5 * (lifted / row_sums[:, None] + lifted / col_sums[None, :])).astype(bf16)
+        image_own = image_embed.astype(f32)
+        embed_grad = logit_scale * (dot_tn(sim_grad, image_all) - image_own)
+        positives = logit_scale * jnp.sum(image_own * text_embed.astype(f32), axis=1)
+        loss_part = 0.5 * jnp.sum(jnp.log(col_sums) - 2.0 * positives)
+        loss_part = loss_part + 0.5 * jnp.sum(jnp.log(row_sums)) / count
 
     backward_in = (
-        text_tokens, lengths, key_bias, *vectors, embed_grad, projected, heads, mixed, mid, slope, *weights,
+        text_tokens, text_lengths, *vectors, embed_grad, projected, heads, mixed, mid, slope, *weights,
     )
-    backward_specs = [in_vmem] * 13 + [anywhere] * 5
+    backward_specs = [in_vmem, in_smem] + [in_vmem] * 10 + [anywhere] * 5
     backward_buffers = weight_scratch + [
         pltpu.VMEM((tokens, width), bf16),
         pltpu.VMEM((tokens, wide), bf16),
@@ -860,6 +1104,8 @@
         pltpu.VMEM((tokens, width), bf16),
         pltpu.VMEM((tokens, width), bf16),
         pltpu.VMEM((tokens, 3 * width), bf16),
+        pltpu.VMEM((captions, 1), jnp.int32),
+        pltpu.VMEM((1, tokens), f32),
         pltpu.SemaphoreType.DMA((5,)),
     ]
 
@@ -871,13 +1117,7 @@
         x = lax.all_gather(x, "row", axis=0, tiled=True)
         return lax.all_to_all(x, "col", split_axis=1, concat_axis=0, tiled=True)
 
-    count = row_count * col_count
-    if (row_count, col_count) == (8, 4):
-        row_blocks = [inner_sum.reshape(captions, row_count, -1), pooled.reshape(captions, row_count, -1)]
-        packed = jnp.concatenate(row_blocks, axis=2)
-        packed = jnp.pad(packed, ((0, 0), (0, 0), (0, -packed.shape[2] % 128))).transpose(1, 0, 2)
-        packed = lax.all_to_all(packed, "row", split_axis=0, concat_axis=0)
-        factors = lax.all_gather(packed, "col", axis=1).reshape(count, captions, -1)
+    if joined:
         out_step, inner_step = width // col_count, wide // row_count
         rows = width // row_count
         up_grad, out_grad, qkv_grad, grad_down, grad_proj, input_grad, norm_total = plain(
@@ -914,7 +1154,7 @@
             "text_backward_joined",
             collective_id=3,
             has_side_effects=True,
-        )(*backward_in, factors, jnp.full((1, 128), loss_part))
+        )(*backward_in, factors, loss_part)
         norm_total = norm_total[0]
         norms = [norm_total[i * width : (i + 1) * width] for i in range(4)]
         loss_total = norm_total[4 * width]
@@ -944,7 +1184,7 @@
         grad_proj = dot_tn(by_row(pooled), by_col(proj_grad))
         loss_total, norm_total = lax.psum((loss_part, norm_grads), both)
         norms = [norm_total[i] for i in range(4)]
-    mean_loss = (loss_total + 0.5 * jnp.sum(jnp.log(row_sums))) / pair_total
+    mean_loss = loss_total / pair_total
     return (
         mean_loss, hidden, input_grad, *norms, qkv_grad, out_grad, up_grad, grad_down, grad_proj,
     )

time: 449 us -> 283 us (0.63)
  waiting for transfers between devices: 116 us -> 0 us
  blocking collectives: 54.6 us -> 0 us
  Pallas kernels: 230 us -> 268 us
  between operations: 17.4 us -> 2.52 us
  local copies, waits for them, and re-layouts: 18 us -> 10.8 us
  starting transfers between devices: 6.61 us -> 0 us
    ppermute x12 -> x0, waiting for transfers between devices: 74.5 us -> none  [the longest x4 71.2 us: partners(): far = lax.ppermute(x, 'col', order)]
    all_gather x2 -> x0, waiting for transfers between devices: 41.2 us -> none  [the longest x1 41.2 us: body(): image_all = lax.all_gather(image_embed, both, axis=0, tiled=True)]
    psum x1 -> x0, blocking collectives: 39.2 us -> none  [body(): row_sums = lax.psum(jnp.sum(lifted, axis=1), both)]
    pallas_call x3 -> x2, Pallas kernels: 128 us -> 167 us  [the longest x1 122 us: body(): plain(image_joined_kernel, (array((captions, width), f32), array((count,...]
    all_to_all x1 -> x0, blocking collectives: 15.4 us -> none  [body(): packed = lax.all_to_all(packed, 'row', split_axis=0, concat_axis=0)]
    ppermute x12 -> x0, starting transfers between devices: 6.53 us -> none  [the longest x4 5.11 us: partners(): far = lax.ppermute(x, 'col', order)]
    reshape x5 -> x0, local copies, waits for them, and re-layouts: 6.4 us -> none  [the longest x4 5.07 us: body(): v.reshape(1, width)]
  transfers between devices with their start and end apart: 14 -> 0, of which waited for: 5 -> 0; matrix products, arithmetic and copies ran while one was open for 3% -> 0% of each run, Pallas kernels for 20% -> 0%
where the time goes in v3:
time: 283 us; the launch traced here: 282 us
  Pallas kernels  268 us (95%)
  local copies, waits for them, and re-layouts  10.8 us (4%)
    pallas_call x1, Pallas kernels, body(): plain(image_joined_kernel, (array((captions, width), f32), array((count,...  122 us
    pallas_call x1, Pallas kernels, body(): plain(text_backward_joined_kernel, (array((rows, wide // col_count), f32)...  101 us
    pallas_call x1, Pallas kernels, body(): plain(text_forward_joined_kernel, text_outs + (array((width, 3 * width),...  44.6 us
    unnamed x19, local copies, waits for them, and re-layouts  6.33 us

profile of v3, /device:TPU:0, one launch (start us, length us, event | category | flops | bytes accessed | tf_op | source)
XLA Modules:
  0.0 281.8 jit_solution(17426513703408011498)
XLA Ops:
  0.6 44.6 %text_forward_joined.1 = (bf16[512,768]{1,0:T(8,128)(2,1)}, bf16[32,768]{1,0:T(8,128)(2,1)}, f32[32,768]{1,0:T(8,128)}, bf16[32,768]{1,0:T(8,128)(2,1)}, bf16[32...) custom-call(bf16[512,768]{1,0:T(8,128)(2,1)} %refs_0_.5, ...), custom_call_target="tpu_custom_call" | custom-call | tf_op jit(solution)/shard_map/text_forward_joined/pallas_call | solution.py:993
  45.3 0.9 reshape.39
  46.2 0.9 copy.36
  47.2 0.7 fusion.3.refs_8_
  47.9 122.1 %image_joined.1 = (f32[32,768]{1,0:T(8,128)}, bf16[32,32,512]{2,1,0:T(8,128)(2,1)}, f32[1,128]{1,0:T(1,128)}) custom-call(bf16[1600,768]{1,0:T(8,128)(2,1)} %refs_0_.4, f32[2,768]{1,0:T(2,128)} %refs_1_.4, f32[2,768]{1,0:T(2,128)} %refs_2_.4, bf16[768,2304]{1,0:T(8,128)(2,1)} %get-tuple-element.33.refs_3_, bf16[768,768]{1,0:T(8,128)(2,1)} %get-tuple-element.34.refs_4_, ...), custom_call_target="tpu_custom_call" | custom-call | tf_op jit(solution)/shard_map/image_joined/pallas_call | solution.py:1008
  170.0 0.0 copy-start
  170.0 101.1 %text_backward_joined.1 = (f32[96,768]{1,0:T(8,128)}, f32[96,192]{1,0:T(8,128)}, f32[96,576]{1,0:T(8,128)}, f32[384,192]{1,0:T(8,128)}, f32[96,192]{1,0:T(8,128)...) custom-call(bf16[512,768]{1,0:T(8,128)(2,1)} %refs_0_.5, s32[32]{0:T(128)} %refs_1_.5, f32[768]{0:T(1024)} %refs_2_.5, ...), custom_call_target="tpu_custom_call" | custom-call | tf_op jit(solution)/shard_map/text_backward_joined/pallas_call | solution.py:1123
  271.1 0.0 copy-start.1
  271.1 0.0 copy-start.3
  271.2 0.0 copy-start.5
  271.2 0.0 copy-start.2
  271.2 1.2 slice.28
  273.1 1.3 slice_reduce_fusion
  274.4 1.9 copy.33
  276.2 0.0 copy-done
  276.2 0.0 copy-start.4
  276.3 0.9 copy.43
  277.1 0.0 copy-done.1
  277.1 0.9 copy.44
  278.0 0.0 copy-done.3
  278.0 0.7 copy.45
  278.7 0.0 copy-done.5
  278.7 0.6 copy.46
  279.4 0.0 copy-done.2
  279.4 0.7 copy.47
  280.1 0.0 copy-done.4
  280.1 0.6 copy.48
  (1 shorter events, 0.0 us)
Async XLA Ops:
  170.0 106.2 %copy-start = (bf16[512,768]{1,0:T(8,128)(2,1)S(1)}, bf16[512,768]{1,0:T(8,128)(2,1)}, u32[]{:S(2)}) copy-start(bf16[512,768]{1,0:T(8,128)(2,1)} %get-tuple-element.95) | copy-start | bytes 2359300
  271.1 6.0 %copy-start.1 = (bf16[512,768]{1,0:T(8,128)(2,1)S(1)}, bf16[512,768]{1,0:T(8,128)(2,1)}, u32[]{:S(2)}) copy-start(bf16[512,768]{1,0:T(8,128)(2,1)} %get-tuple-element.96) | copy-start | bytes 2359300
  271.1 6.9 %copy-start.3 = (f32[96,576]{1,0:T(8,128)S(1)}, f32[96,576]{1,0:T(8,128)}, u32[]{:S(2)}) copy-start(f32[96,576]{1,0:T(8,128)} %get-tuple-element.101) | copy-start | bytes 663556
  271.2 7.6 %copy-start.5 = (f32[96,192]{1,0:T(8,128)S(1)}, f32[96,192]{1,0:T(8,128)}, u32[]{:S(2)}) copy-start(f32[96,192]{1,0:T(8,128)} %get-tuple-element.102) | copy-start | bytes 221188
  271.2 8.2 %copy-start.2 = (f32[96,768]{1,0:T(8,128)S(1)}, f32[96,768]{1,0:T(8,128)}, u32[]{:S(2)}) copy-start(f32[96,768]{1,0:T(8,128)} %get-tuple-element.103) | copy-start | bytes 884740
  276.2 3.8 %copy-start.4 = (f32[96,192]{1,0:T(8,128)S(1)}, f32[96,192]{1,0:T(8,128)}, u32[]{:S(2)}) copy-start(f32[96,192]{1,0:T(8,128)} %get-tuple-element.105) | copy-start | bytes 221188

commit v4 on v3

v4 whole, which is shorter than its diff:
```python
import functools
import math
from types import SimpleNamespace

import jax
import jax.numpy as jnp
from jax import lax
from jax.experimental import pallas as pl
from jax.experimental.pallas import tpu as pltpu
from jax.sharding import PartitionSpec as P

HEADS = 12
IMG_TOK = 50
norm_eps = 1e-06
logit_scale = 50.0
masked_score = -1e30
log2e = math.log2(math.e)
f32 = jnp.float32
bf16 = jnp.bfloat16
VMEM_LIMIT = 60 * 2**20
MESH = pl.DeviceIdType.MESH


def dot_nn(a, b):
    return lax.dot_general(a, b, (((1,), (0,)), ((), ())), preferred_element_type=f32)


def dot_nt(a, b):
    return lax.dot_general(a, b, (((1,), (1,)), ((), ())), preferred_element_type=f32)


def dot_tn(a, b):
    return lax.dot_general(a, b, (((0,), (0,)), ((), ())), preferred_element_type=f32)


def split_low(x):
    high = x.astype(bf16)
    return high, (x - high.astype(f32)).astype(bf16)


def normed(x):
    centered = x - jnp.mean(x, axis=-1, keepdims=True)
    spread = lax.rsqrt(jnp.mean(centered * centered, axis=-1, keepdims=True) + norm_eps)
    return centered * spread, spread


def layer_norm(x, gain, bias):
    return normed(x)[0] * gain + bias


def gelu(x):
    return x * (0.5 + 0.5 * lax.erf(x * math.sqrt(0.5)))


def gelu_and_slope(x):
    below = 0.5 + 0.5 * lax.erf(x * math.sqrt(0.5))
    bell = jnp.exp2((-0.5 * log2e) * (x * x))
    return x * below, below + x * (bell * (1.0 / math.sqrt(2.0 * math.pi)))


def lane_halves(width):
    lane = lax.broadcasted_iota(jnp.int32, (1, width), 1)
    first = (lane < width // 2).astype(f32)
    return first.astype(bf16), (1.0 - first).astype(bf16)


def stack_heads(x, first, second):
    return jnp.concatenate([x * first, x * second], axis=0)


def join_heads(stacked):
    rows, width = stacked.shape[0] // 2, stacked.shape[1]
    lane = lax.broadcasted_iota(jnp.int32, (rows, width), 1)
    return jnp.where(lane < width // 2, stacked[:rows], stacked[rows:])


def soft_weights(query, key, bias, factor):
    scores = dot_nt(query, key) * (factor * log2e) + bias
    weights = jnp.exp2(scores - jnp.max(scores, axis=-1, keepdims=True))
    return weights, 1.0 / jnp.sum(weights, axis=-1, keepdims=True)


def set_lengths(lengths_ref, lens_ref, key_bias_ref):
    captions, tokens = lens_ref.shape[0], key_bias_ref.shape[1]
    length = tokens // captions
    caption = lax.broadcasted_iota(jnp.int32, (captions, 1), 0)
    token = lax.broadcasted_iota(jnp.int32, (1, tokens), 1)
    column, row = jnp.zeros((captions, 1), jnp.int32), jnp.zeros((1, tokens), jnp.int32)
    for n in range(captions):
        column = jnp.where(caption == n, lengths_ref[n], column)
        row = jnp.where(token // length == n, lengths_ref[n], row)
    lens_ref[...] = column
    key_bias_ref[...] = jnp.where(token % length < row, 0.0, masked_score)


def as_row(ref):
    return ref[...].reshape(1, ref.shape[0])


def text_bias(key_bias_ref, block, rows, length):
    near = lax.broadcasted_iota(jnp.int32, (rows, rows), 0) // length
    far = lax.broadcasted_iota(jnp.int32, (rows, rows), 1) // length
    columns = pl.ds(pl.multiple_of(block * rows, rows), rows)
    bias = jnp.where(near == far, key_bias_ref[:, columns], masked_score)
    return jnp.concatenate([bias, bias], axis=0)


def member(len_ref, captions, tokens):
    length = tokens // captions
    token = lax.broadcasted_iota(jnp.int32, (captions, tokens), 1)
    caption = lax.broadcasted_iota(jnp.int32, (captions, tokens), 0)
    return ((token // length == caption) & (token % length < len_ref[...])).astype(f32)


def spread_rows(x, length):
    rows, width = x.shape
    return jnp.broadcast_to(x[:, None, :], (rows, length, width)).reshape(rows * length, width)


def wide_steps(total, most=768):
    step = math.gcd(total, most)

    def loop(body):
        @pl.loop(0, total // step)
        def _(j):
            body(pl.ds(pl.multiple_of(j * step, 128), step))

    return loop


class TextForward:
    band = 128

    def __init__(self, names, refs):
        for name, ref in zip(names, refs, strict=True):
            setattr(self, name, ref)
        self.tokens, self.width = self.tok.shape
        self.captions = self.lens.shape[0]
        self.length = self.tokens // self.captions
        self.wide = self.w_up.shape[1]
        pairs = (
            (self.qkv_hbm, self.w_qkv), (self.out_hbm, self.w_out), (self.up_hbm, self.w_up),
            (self.down_hbm, self.w_down), (self.proj_hbm, self.w_proj),
        )
        self.loads = load_weights(pairs, self.sems)

    def bands(self, step):
        pl.loop(0, self.tokens // self.band)(
            lambda i: step(pl.ds(pl.multiple_of(i * self.band, self.band), self.band))
        )

    def prepare(self):
        set_lengths(self.lengths, self.lens, self.key_bias)

        def first_norm(rows):
            norm = layer_norm(self.tok[rows, :].astype(f32), as_row(self.gain1), as_row(self.bias1))
            self.norm[rows, :] = norm.astype(bf16)

        self.bands(first_norm)

    def attention(self):
        width = self.width
        self.loads[0].wait()

        @wide_steps(3 * width)
        def _(columns):
            self.heads[:, columns] = dot_nn(self.norm[...], self.w_qkv[:, columns]).astype(bf16)

        first, second = lane_halves(128)
        factor = (width // HEADS) ** -0.5

        @pl.loop(0, self.tokens // self.band)
        def _(block):
            rows = pl.ds(pl.multiple_of(block * self.band, self.band), self.band)
            bias = text_bias(self.key_bias, block, self.band, self.length)
            for at in range(0, width, 128):
                query = stack_heads(self.heads[rows, at : at + 128], first, second)
                key = self.heads[rows, width + at : width + at + 128]
                weights, scale = soft_weights(query, key, bias, factor)
                value = self.heads[rows, 2 * width + at : 2 * width + at + 128]
                mixed = dot_nn(weights.astype(bf16), value) * scale
                self.mixed[rows, at : at + 128] = join_heads(mixed).astype(bf16)

    def middle(self):
        self.loads[1].wait()

        def second_norm(rows):
            mid = self.tok[rows, :].astype(f32) + dot_nn(self.mixed[rows, :], self.w_out[...])
            self.mid[rows, :] = mid
            self.norm[rows, :] = layer_norm(mid, as_row(self.gain2), as_row(self.bias2)).astype(bf16)

        self.bands(second_norm)

    def feed(self):
        self.loads[2].wait()
        self.chosen = member(self.lens, self.captions, self.tokens).astype(bf16)
        place = lax.broadcasted_iota(jnp.int32, (self.captions, self.length, 1), 1)
        valid = (place < self.lens[...].reshape(self.captions, 1, 1)).astype(f32).reshape(self.tokens, 1)

        @wide_steps(self.wide)
        def _(columns):
            value, slope = gelu_and_slope(dot_nn(self.norm[...], self.w_up[:, columns]))
            value = value.astype(bf16)
            self.inner[:, columns] = value
            self.slope[:, columns] = (slope * valid).astype(bf16)
            self.inner_sum[:, columns] = dot_nn(self.chosen, value).astype(bf16)

    def finish(self):
        self.loads[3].wait()
        inverse = 1.0 / self.lens[...].astype(f32)

        @wide_steps(self.width)
        def _(columns):
            state = self.mid[:, columns] + dot_nn(self.inner[...], self.w_down[:, columns])
            self.hidden[:, columns] = state.astype(bf16)
            high, low = split_low(state)
            pooled = (dot_nn(self.chosen, high) + dot_nn(self.chosen, low)) * inverse
            self.pooled[:, columns] = pooled.astype(bf16)

        self.loads[4].wait()
        projected = dot_nn(self.pooled[...], self.w_proj[...])
        self.projected[...] = projected
        scale = lax.rsqrt(jnp.sum(projected * projected, axis=-1, keepdims=True) + norm_eps)
        self.text_embed[...] = (projected * scale).astype(bf16)


text_ins = (
    "tok", "lengths", "gain1", "bias1", "gain2", "bias2", "qkv_hbm", "out_hbm", "up_hbm", "down_hbm", "proj_hbm",
)
text_names = ("hidden", "text_embed", "projected", "pooled", "inner_sum", "heads", "mixed", "mid", "slope")
text_scratch = ("w_qkv", "w_out", "w_up", "w_down", "w_proj", "norm", "inner", "lens", "key_bias", "sems")


def text_forward_kernel(*refs):
    t = TextForward(text_ins + text_names + text_scratch, refs)
    t.prepare()
    t.attention()
    t.middle()
    t.feed()
    t.finish()


def load_weights(pairs, sems):
    loads = [pltpu.make_async_copy(s, d, sems.at[i]) for i, (s, d) in enumerate(pairs)]
    for load in loads:
        load.start()
    return loads


def spans(count, size):
    return lambda i: pl.ds(pl.multiple_of(i * size, size), size)


def norm_backward(outer, unit, spread, gain):
    outer = outer * gain
    inner = outer - jnp.mean(outer, axis=-1, keepdims=True)
    return spread * (inner - unit * jnp.mean(outer * unit, axis=-1, keepdims=True))


class TextBackward:
    band = 128

    def __init__(self, names, refs):
        for name, ref in zip(names, refs, strict=True):
            setattr(self, name, ref)
        self.tokens, self.width = self.tok.shape
        self.captions = self.lens.shape[0]
        self.length = self.tokens // self.captions
        self.wide = self.w_up.shape[1]
        order = ("w_proj", "mid", "w_down", "slope", "w_up", "mixed", "w_out", "tok", "heads", "w_qkv")
        pairs = [(getattr(self, name + "_hbm"), getattr(self, name)) for name in order]
        self.loads = dict(zip(order, load_weights(pairs, self.sems)))
        self.pre_grad = self.slope

    def rows(self, i):
        return pl.ds(pl.multiple_of(i * self.band, self.band), self.band)

    def bands(self, step):
        pl.loop(0, self.tokens // self.band)(lambda i: step(self.rows(i)))

    def valid(self):
        place = lax.broadcasted_iota(jnp.int32, (self.captions, self.length, 1), 1)
        valid = place < self.lens[...].reshape(self.captions, 1, 1)
        return valid.astype(f32).reshape(self.tokens, 1)

    def project(self):
        set_lengths(self.lengths, self.lens, self.key_bias)
        projected = self.projected[...]
        embed_grad = self.embed_grad[...]
        r = lax.rsqrt(jnp.sum(projected * projected, axis=-1, keepdims=True) + norm_eps)
        along = jnp.sum(projected * embed_grad, axis=-1, keepdims=True)
        proj_grad = (r * embed_grad - (r * r * r) * projected * along).astype(bf16)
        self.loads["w_proj"].wait()
        state_grad = dot_nt(proj_grad, self.w_proj[...]) * (1.0 / self.lens[...].astype(f32))
        self.branch[...] = state_grad.astype(bf16)
        self.mid_grad[...] = spread_rows(state_grad, self.length) * self.valid()
        return proj_grad, self.branch[...]

    def inner(self):
        self.loads["w_down"].wait()
        self.loads["slope"].wait()
        branch = self.branch[...]

        @wide_steps(self.wide)
        def _(columns):
            inner_grad = dot_nt(branch, self.w_down[columns, :])
            pre_grad = spread_rows(inner_grad, self.length) * self.slope[:, columns].astype(f32)
            self.pre_grad[:, columns] = pre_grad.astype(bf16)

        self.loads["mid"].wait()

        def second_norm(rows):
            self.norm[rows, :] = layer_norm(
                self.mid[rows, :], as_row(self.gain2), as_row(self.bias2)
            ).astype(bf16)

        self.bands(second_norm)
        self.turned[...] = self.norm[...].T

    def up_block(self, columns):
        return dot_nn(self.turned[...], self.pre_grad[:, columns]).astype(bf16)

    def to_middle(self):
        self.loads["w_up"].wait()

        @wide_steps(self.width)
        def _(columns):
            self.outer[:, columns] = dot_nt(self.pre_grad[...], self.w_up[columns, :])

    def middle(self):
        self.norm_grad[...] = jnp.zeros_like(self.norm_grad)

        def through_norm(rows):
            unit, spread = normed(self.mid[rows, :])
            outer = self.outer[rows, :]
            self.norm_grad[2:3, :] += jnp.sum(outer * unit, axis=0, keepdims=True)
            self.norm_grad[3:4, :] += jnp.sum(outer, axis=0, keepdims=True)
            mid_grad = self.mid_grad[rows, :] + norm_backward(outer, unit, spread, as_row(self.gain2))
            self.mid_grad[rows, :] = mid_grad
            self.low_grad[rows, :] = mid_grad.astype(bf16)

        self.bands(through_norm)

    def out_block(self, columns):
        return dot_tn(self.mixed[...], self.low_grad[:, columns]).astype(bf16)

    def to_heads(self):
        self.loads["w_out"].wait()
        self.loads["tok"].wait()

        def through_out(rows):
            self.mixed_grad[rows, :] = dot_nt(self.low_grad[rows, :], self.w_out[...]).astype(bf16)
            norm = layer_norm(self.tok[rows, :].astype(f32), as_row(self.gain1), as_row(self.bias1))
            self.norm[rows, :] = norm.astype(bf16)

        self.bands(through_out)

    def attention(self, after=lambda block: None):
        first, second = lane_halves(128)
        width = self.width
        factor = (width // HEADS) ** -0.5
        self.loads["heads"].wait()
        self.key_column[...] = (1.0 - self.valid()) * masked_score

        @pl.loop(0, self.tokens // self.band)
        def _(block):
            rows = self.rows(block)
            near = lax.broadcasted_iota(jnp.int32, (self.band, self.band), 0) // self.length
            far = lax.broadcasted_iota(jnp.int32, (self.band, self.band), 1) // self.length
            bias = jnp.where(near == far, self.key_column[rows, :], masked_score)
            bias = jnp.concatenate([bias, bias], axis=1)
            for at in range(0, width, 128):
                query = stack_heads(self.heads[rows, at : at + 128], first, second)
                key = self.heads[rows, width + at : width + at + 128]
                value = self.heads[rows, 2 * width + at : 2 * width + at + 128]
                grad = stack_heads(self.mixed_grad[rows, at : at + 128], first, second)
                scores = dot_nt(key, query) * (factor * log2e) + bias
                weights = jnp.exp2(scores - jnp.max(scores, axis=0, keepdims=True))
                probs = weights * (1.0 / jnp.sum(weights, axis=0, keepdims=True))
                prob_grad = dot_nt(value, grad)
                total = jnp.sum(prob_grad * probs, axis=0, keepdims=True)
                score_grad = (probs * (prob_grad - total)).astype(bf16)
                query_grad = join_heads(dot_tn(score_grad, key)) * factor
                self.heads_grad[rows, at : at + 128] = query_grad.astype(bf16)
                key_grad = dot_nn(score_grad, query) * factor
                self.heads_grad[rows, width + at : width + at + 128] = key_grad.astype(bf16)
                value_grad = dot_nn(probs.astype(bf16), grad)
                self.heads_grad[rows, 2 * width + at : 2 * width + at + 128] = value_grad.astype(bf16)
            after(block)

    def qkv_block(self, columns):
        return dot_tn(self.norm[...], self.heads_grad[:, columns]).astype(bf16)

    def input(self):
        self.loads["w_qkv"].wait()

        @wide_steps(self.width)
        def _(columns):
            self.outer[:, columns] = dot_nt(self.heads_grad[...], self.w_qkv[columns, :])

        def through_norm(rows):
            unit, spread = normed(self.tok[rows, :].astype(f32))
            outer = self.outer[rows, :]
            self.norm_grad[0:1, :] += jnp.sum(outer * unit, axis=0, keepdims=True)
            self.norm_grad[1:2, :] += jnp.sum(outer, axis=0, keepdims=True)
            inner = norm_backward(outer, unit, spread, as_row(self.gain1))
            self.input_grad[rows, :] = (self.mid_grad[rows, :] + inner).astype(bf16)

        self.bands(through_norm)


backward_ins = (
    "lengths", "gain1", "bias1", "gain2", "bias2", "embed_grad", "projected", "tok_hbm", "heads_hbm", "mixed_hbm",
    "mid_hbm", "slope_hbm", "w_qkv_hbm", "w_out_hbm", "w_up_hbm", "w_down_hbm", "w_proj_hbm",
)
backward_scratch = (
    "tok", "heads", "mixed", "mid", "slope", "w_qkv", "w_out", "w_up", "w_down", "w_proj", "norm", "turned",
    "outer", "mid_grad", "low_grad", "mixed_grad", "heads_grad", "lens", "key_bias", "key_column",
    "sems",
)


def text_backward_kernel(*refs):
    outs = ("proj_grad", "branch", "up_grad", "out_grad", "qkv_grad", "input_grad", "norm_grad")
    t = TextBackward(backward_ins + outs + backward_scratch, refs)
    parts = t.up_grad.shape[0]

    def blocks(target, block):
        step = target.shape[2]
        for part in range(parts):
            target[part] = block(slice(part * step, (part + 1) * step))

    t.proj_grad[...] = t.project()[0]
    t.inner()
    blocks(t.up_grad, t.up_block)
    t.to_middle()
    t.middle()
    t.loads["mixed"].wait()
    blocks(t.out_grad, t.out_block)
    t.to_heads()
    t.attention()
    blocks(t.qkv_grad, t.qkv_block)
    t.input()


class Place:
    def __init__(self, z_count=4, y_count=2, x_count=2, k_count=2):
        self.row, self.col = lax.axis_index("row"), lax.axis_index("col")
        self.z, self.y = self.row // y_count, self.row % y_count
        self.x, self.k = self.col // k_count, self.col % k_count
        self.rows, self.cols = z_count * y_count, x_count * k_count
        self.count = self.rows * self.cols
        self.me = self.row * self.cols + self.col
        self.slot = self.col * self.rows + self.row

    def at(self, **moved):
        z, y, x, k = (moved.get(name, getattr(self, name)) for name in "zyxk")
        return z * 2 + y, x * 2 + k

    def peer(self, distance):
        other = (self.me + distance) % self.count
        return other // self.cols, other % self.cols

    def greet(self):
        barrier = pltpu.get_barrier_semaphore()

        @pl.loop(1, self.count)
        def _(distance):
            pl.semaphore_signal(barrier, inc=1, device_id=self.peer(distance), device_id_type=MESH)

    def meet(self):
        pl.semaphore_wait(pltpu.get_barrier_semaphore(), self.count - 1)


def remote(src, dst, send, recv, to):
    return pltpu.make_async_remote_copy(
        src_ref=src, dst_ref=dst, send_sem=send, recv_sem=recv, device_id=to, device_id_type=MESH
    )


class Gather:
    def __init__(self, place, shard, whole, local, sends, recvs):
        depth = shard.shape[0]
        half = depth // 2
        y = place.y
        mate, next_x, next_y = place.at(k=1 - place.k), place.at(x=1 - place.x), place.at(y=1 - y)

        def block(col, part):
            return whole.at[pl.ds(pl.multiple_of(col * depth + part * half, 16), half)]

        own = whole.at[pl.ds(pl.multiple_of(place.col * depth, 16), depth)]
        across = next_x[1]
        shard_half = shard.at[pl.ds(pl.multiple_of(y * half, 16), half)]
        self.local = pltpu.make_async_copy(shard, own, local)
        self.near = remote(shard, own, sends.at[0], recvs.at[0], mate)
        self.far = remote(shard_half, block(place.col, y), sends.at[1], recvs.at[1], next_x)
        self.along = remote(block(across, y), block(across, y), sends.at[2], recvs.at[2], next_y)
        self.first = remote(block(across, y), block(across, y), sends.at[3], recvs.at[3], mate)
        self.second = remote(block(across, 1 - y), block(across, 1 - y), sends.at[4], recvs.at[4], mate)

    def start(self):
        self.far.start()
        self.near.start()
        self.local.start()

    def share(self):
        self.far.wait()
        self.along.start()
        self.first.start()

    def relay(self):
        self.along.wait()
        self.second.start()

    def finish(self):
        self.local.wait()
        self.near.wait()
        self.first.wait()
        self.second.wait()


class RowFactors:
    def __init__(self, place, own, held, local, sends, recvs):
        self.place, self.own, self.held, self.sends, self.recvs = place, own, held, sends, recvs
        self.local = pltpu.make_async_copy(own.at[place.row], held.at[place.col, place.row], local)
        mine, across = held.at[place.col], held.at[place.at(x=1 - place.x)[1]]
        mate, next_x = place.at(k=1 - place.k), place.at(x=1 - place.x)
        n = place.rows - 1
        self.far = remote(mine, mine, sends.at[n], recvs.at[n], next_x)
        self.near = remote(mine, mine, sends.at[n + 1], recvs.at[n + 1], mate)
        self.passed = remote(across, across, sends.at[n + 2], recvs.at[n + 2], mate)

    def copy(self, distance):
        p = self.place
        row = (p.row + distance) % p.rows
        sems = self.sends.at[distance - 1], self.recvs.at[distance - 1]
        return remote(self.own.at[row], self.held.at[p.col, p.row], *sems, (row, p.col))

    def start(self):
        self.local.start()
        pl.loop(1, self.place.rows)(lambda distance: self.copy(distance).start())

    def share(self):
        self.local.wait()
        pl.loop(1, self.place.rows)(lambda distance: self.copy(distance).wait())
        self.far.start()
        self.near.start()

    def relay(self):
        self.far.wait()
        self.passed.start()

    def finish(self):
        self.near.wait()
        self.passed.wait()


class Exchange:
    def __init__(self, place, source, slots, sends, recvs):
        self.place, self.source, self.slots, self.sends, self.recvs = place, source, slots, sends, recvs

    def copy(self, distance):
        to = self.place.peer(distance)
        sems = self.sends.at[distance - 1], self.recvs.at[distance - 1]
        return remote(self.source(to), self.slots.at[self.place.slot], *sems, to)

    def start(self):
        pl.loop(1, self.place.count)(lambda distance: self.copy(distance).start())

    def finish(self):
        pl.loop(1, self.place.count)(lambda distance: self.copy(distance).wait())


class GradientScatter:
    chunks = 3

    def __init__(self, place, held, near, x1, y1, x2, y2, far, sends, recvs):
        self.place, self.held, self.near, self.far = place, held, near, far
        self.x1, self.y1, self.x2, self.y2 = x1, y1, x2, y2
        self.sends, self.recvs = sends, recvs
        self.step = held.shape[5] // self.chunks

    def lanes(self, chunk):
        step, half = self.step, self.step // 2
        at = chunk * step
        return pl.ds(at, step), pl.ds(at, half), pl.ds(at + half, half), pl.ds(chunk * half, half)

    def copies(self, chunk, stage):
        p, held = self.place, self.held
        x, y, z, k = p.x, p.y, p.z, p.k
        whole, one, two, part = self.lanes(chunk)

        def copy(n, src, dst, **moved):
            return remote(src, dst, self.sends.at[chunk, n], self.recvs.at[chunk, n], p.at(**moved))

        if stage == 0:
            return [copy(0, held.at[:, 1 - k, :, :, :, whole], self.near.at[:, :, :, :, whole], k=1 - k)]
        if stage == 1:
            return [
                copy(1, held.at[1 - x, k, :, :, :, one], self.x1.at[:, :, :, part], x=1 - x),
                copy(2, held.at[:, k, :, 1 - y, :, two], self.y1.at[:, :, :, part], y=1 - y),
            ]
        if stage == 2:
            return [
                copy(3, held.at[x, k, :, 1 - y, :, one], self.y2.at[:, :, part], y=1 - y),
                copy(4, held.at[1 - x, k, :, y, :, two], self.x2.at[:, :, part], x=1 - x),
            ]
        copies = []
        for distance in range(1, held.shape[2]):
            other = (z + distance) % held.shape[2]
            copies.append(
                copy(4 + distance, held.at[x, k, other, y, :, whole], self.far.at[distance - 1, :, whole], z=other)
            )
        return copies

    def start(self, chunk, stage):
        for copy in self.copies(chunk, stage):
            copy.start()

    def finish(self, chunk, stage):
        for copy in self.copies(chunk, stage):
            copy.wait()
        p, held = self.place, self.held
        x, y, k = p.x, p.y, p.k
        z_count = held.shape[2]
        whole, one, two, part = self.lanes(chunk)

        def add(target, source):
            target[...] = (target[...].astype(f32) + source[...].astype(f32)).astype(bf16)

        if stage == 0:

            @pl.loop(0, z_count)
            def _(z):
                for i in range(2):
                    for j in range(2):
                        add(held.at[i, k, z, j, :, whole], self.near.at[i, z, j, :, whole])

        if stage == 1:

            @pl.loop(0, z_count)
            def _(z):
                for i in range(2):
                    add(held.at[x, k, z, i, :, one], self.x1.at[z, i, :, part])
                    add(held.at[i, k, z, y, :, two], self.y1.at[i, z, :, part])

        if stage == 2:

            @pl.loop(0, z_count)
            def _(z):
                add(held.at[x, k, z, y, :, one], self.y2.at[z, :, part])
                add(held.at[x, k, z, y, :, two], self.x2.at[z, :, part])

    def step_on(self, chunk, stage):
        self.finish(chunk, stage - 1)
        self.start(chunk, stage)

    def total(self):
        p = self.place
        total = self.held[p.x, p.k, p.z, p.y].astype(f32)
        for i in range(self.far.shape[0]):
            total = total + self.far[i].astype(f32)
        return total


def scatter_scratch(rows, columns):
    shapes = [
        (2, 2, 4, 2, rows, columns), (2, 4, 2, rows, columns), (4, 2, rows, columns // 2), (2, 4, rows, columns // 2),
        (4, rows, columns // 2), (4, rows, columns // 2), (3, rows, columns),
    ]
    return [pltpu.VMEM(shape, bf16) for shape in shapes] + [pltpu.SemaphoreType.DMA((GradientScatter.chunks, 8))] * 2


scatter_names = ("held", "near", "x1", "y1", "x2", "y2", "far", "sends", "recvs")
exchange_names = ("own", "all", "sends", "recvs")


def text_backward_joined_kernel(*refs):
    ins = backward_ins + ("factors", "loss")
    outs = ("up_out", "out_out", "qkv_out", "down_out", "proj_out", "input_grad", "norm_out")
    sets = tuple(name + tag for tag in ("_a", "_b") for name in scatter_names)
    swaps = tuple(name + tag for tag in ("_factors", "_late", "_last") for name in exchange_names)
    names = ins + outs + backward_scratch + sets + ("branch", "norm_grad") + swaps
    t = TextBackward(names, refs)
    place = Place()
    place.greet()
    width = t.width
    a, b = (GradientScatter(place, *(getattr(t, name + tag) for name in scatter_names)) for tag in ("_a", "_b"))
    factors = Exchange(
        place, lambda to: t.own_factors.at[to[1]], t.all_factors, t.sends_factors, t.recvs_factors
    )
    late = Exchange(place, lambda to: t.own_late, t.all_late, t.sends_late, t.recvs_late)
    last = Exchange(place, lambda to: t.own_last, t.all_last, t.sends_last, t.recvs_last)
    cols = place.cols
    up_step, qkv_step, out_step = t.wide // cols, 3 * width // cols, width // cols

    def blocked(value):
        return value.reshape(4, 2, value.shape[0] // 8, value.shape[1])

    proj_grad, branch = t.project()
    for part in range(cols):
        columns = slice(part * out_step, (part + 1) * out_step)
        t.own_factors[part] = jnp.concatenate([branch[:, columns], proj_grad[:, columns]], axis=1)
    t.all_factors[place.slot] = t.own_factors[place.col]
    place.meet()
    factors.start()
    t.inner()
    for chunk in range(a.chunks):
        for part in range(cols):
            at = part * up_step + chunk * a.step
            t.held_a[part // 2, part % 2, :, :, :, chunk * a.step : (chunk + 1) * a.step] = blocked(
                t.up_block(slice(at, at + a.step))
            )
        a.start(chunk, 0)
        if chunk > 0:
            a.step_on(chunk - 1, 1)
    t.to_middle()
    a.step_on(2, 1)
    t.middle()
    t.own_late[...] = jnp.concatenate([t.norm_grad[2:3, :], t.norm_grad[3:4, :], t.loss[...]], axis=1)
    t.all_late[place.slot] = t.own_late[...]
    late.start()
    a.step_on(0, 2)
    t.loads["mixed"].wait()
    for part in range(cols):
        t.held_b[part // 2, part % 2, :, :, :, qkv_step:] = blocked(
            t.out_block(slice(part * out_step, (part + 1) * out_step))
        )
    t.to_heads()

    def after(block):
        @pl.when(block == 0)
        def _():
            a.step_on(1, 2)
            a.step_on(0, 3)

        @pl.when(block == 1)
        def _():
            a.step_on(2, 2)

        @pl.when(block == 2)
        def _():
            a.step_on(1, 3)

    t.attention(after)
    for part in range(cols):
        t.held_b[part // 2, part % 2, :, :, :, :qkv_step] = blocked(
            t.qkv_block(slice(part * qkv_step, (part + 1) * qkv_step))
        )
    for chunk in range(b.chunks):
        b.start(chunk, 0)
    a.step_on(2, 3)
    for chunk in range(b.chunks):
        b.step_on(chunk, 1)
    t.input()
    t.own_last[...] = jnp.concatenate([t.norm_grad[0:1, :], t.norm_grad[1:2, :]], axis=1)
    t.all_last[place.slot] = t.own_last[...]
    last.start()
    b.step_on(0, 2)
    for chunk in range(a.chunks):
        a.finish(chunk, 3)
    t.up_out[...] = a.total()
    factors.finish()
    b.step_on(1, 2)
    b.step_on(0, 3)
    grown = dot_tn(
        t.factors[...].reshape(-1, t.factors.shape[3]), t.all_factors[...].reshape(-1, t.all_factors.shape[2])
    )
    inner_step = t.wide // place.rows
    t.down_out[...] = grown[:inner_step, :out_step]
    t.proj_out[...] = grown[inner_step : inner_step + width // place.rows, out_step:]
    b.step_on(2, 2)
    b.step_on(1, 3)
    late.finish()
    last.finish()
    t.norm_out[:, : 2 * width] = jnp.sum(t.all_last[...], axis=0)
    t.norm_out[:, 2 * width :] = jnp.sum(t.all_late[...], axis=0)
    b.step_on(2, 3)
    for chunk in range(b.chunks):
        b.finish(chunk, 3)
    total = b.total()
    t.qkv_out[...] = total[:, :qkv_step]
    t.out_out[...] = total[:, qkv_step:]


def group_mean(images, rows):
    token = lax.broadcasted_iota(jnp.int32, (images, rows), 1)
    image = lax.broadcasted_iota(jnp.int32, (images, rows), 0)
    inside = (token >= image * IMG_TOK) & (token < (image + 1) * IMG_TOK)
    return inside.astype(f32).astype(bf16)


def load_parts(parts, target, sems, col, col_count):
    depth = target.shape[0] // col_count
    copies = []
    for k, part in enumerate(parts):
        place = pl.multiple_of((col ^ k) * depth, depth)
        copies.append(pltpu.make_async_copy(part, target.at[pl.ds(place, depth)], sems.at[k]))
    return copies


def image_mix(tokens, gain_ref, bias_ref, w_qkv, w_out, norm_ref, heads_ref, mixed_ref):
    rows, width = tokens.shape
    images = rows // IMG_TOK
    norm_ref[...] = layer_norm(tokens.astype(f32), gain_ref[0:1, :], bias_ref[0:1, :]).astype(bf16)

    @wide_steps(3 * width)
    def _(columns):
        heads_ref[:, columns] = dot_nn(norm_ref[...], w_qkv[:, columns]).astype(bf16)

    first, second = lane_halves(128)
    factor = (width // HEADS) ** -0.5
    window = 112

    @pl.loop(0, images // 2)
    def _(pair):
        start = pair * (2 * IMG_TOK)
        low = pl.multiple_of(start // 16 * 16, 16)
        near = lax.broadcasted_iota(jnp.int32, (window, window), 0) + low
        far = lax.broadcasted_iota(jnp.int32, (window, window), 1) + low
        same = (near >= start) & (near < start + 2 * IMG_TOK) & (far >= start) & (far < start + 2 * IMG_TOK)
        same = same & ((near >= start + IMG_TOK) == (far >= start + IMG_TOK))
        bias = jnp.where(same, 0.0, masked_score)
        bias = jnp.concatenate([bias, bias], axis=0)
        keep = lax.broadcasted_iota(jnp.int32, (16, 128), 0) + low < start
        span, head, tail = pl.ds(low, window), pl.ds(low, 16), pl.ds(low + 16, window - 16)
        for at in range(0, width, 128):
            query = stack_heads(heads_ref[span, at : at + 128], first, second)
            key = heads_ref[span, width + at : width + at + 128]
            weights, scale = soft_weights(query, key, bias, factor)
            value = heads_ref[span, 2 * width + at : 2 * width + at + 128]
            mixed = join_heads(dot_nn(weights.astype(bf16), value) * scale)
            former = mixed_ref[head, at : at + 128].astype(f32)
            mixed_ref[head, at : at + 128] = jnp.where(keep, former, mixed[:16]).astype(bf16)
            mixed_ref[tail, at : at + 128] = mixed[16:].astype(bf16)

    mid = tokens.astype(f32) + dot_nn(mixed_ref[...], w_out[...])
    high, low = split_low(mid)
    select = group_mean(images, rows)
    mean = (dot_nn(select, high) + dot_nn(select, low)) * (1.0 / IMG_TOK)
    return layer_norm(mid, gain_ref[1:2, :], bias_ref[1:2, :]).astype(bf16), mean


def image_mix_kernel(col_count, tok_ref, gain_ref, bias_ref, *refs):
    qkv_parts, out_parts = refs[:col_count], refs[col_count : 2 * col_count]
    normed_ref, mean_ref, w_qkv, w_out, *buffers, sems = refs[2 * col_count :]
    col = lax.axis_index("col")

    @pl.when(pl.program_id(0) == 0)
    def _():
        copies = load_parts(qkv_parts, w_qkv, sems.at[0], col, col_count)
        copies += load_parts(out_parts, w_out, sems.at[1], col, col_count)
        for copy in copies:
            copy.start()
        for copy in copies:
            copy.wait()

    normed_ref[...], mean_ref[...] = image_mix(tok_ref[...], gain_ref, bias_ref, w_qkv, w_out, *buffers)


def image_embed_kernel(col_count, normed_ref, mean_ref, *refs):
    up_parts, down_parts = refs[:col_count], refs[col_count : 2 * col_count]
    embed_ref, w_up, w_down, sum_ref, sems = refs[2 * col_count :]
    rows, width = normed_ref.shape
    images = rows // IMG_TOK
    wide = w_up.shape[1]
    step = pl.program_id(0)
    col = lax.axis_index("col")
    downs = load_parts(down_parts, w_down, sems.at[1], col, col_count)

    @pl.when(step == 0)
    def _():
        ups = load_parts(up_parts, w_up, sems.at[0], col, col_count)
        for copy in ups + downs:
            copy.start()
        for copy in ups:
            copy.wait()

    select = group_mean(images, rows)

    @wide_steps(wide)
    def _(columns):
        inner = gelu(dot_nn(normed_ref[...], w_up[:, columns])).astype(bf16)
        sum_ref[pl.ds(pl.multiple_of(step * images, images), images), columns] = dot_nn(select, inner)

    @pl.when(step == pl.num_programs(0) - 1)
    def _():
        for copy in downs:
            copy.wait()
        high, low = split_low(sum_ref[...] * (1.0 / IMG_TOK))
        pooled = mean_ref[...] + dot_nn(high, w_down[...]) + dot_nn(low, w_down[...])
        embed_ref[...] = (
            pooled * lax.rsqrt(jnp.sum(pooled * pooled, axis=-1, keepdims=True) + norm_eps)
        ).astype(bf16)


image_ins = (
    "image_hbm", "image_gain", "image_bias", "image_qkv_hbm", "image_out_hbm", "image_up_hbm", "image_down_hbm",
)
saved_names = ("hidden", "projected", "heads", "mixed", "mid", "slope", "held_factors")
image_scratch = (
    "image_tok", "iw_qkv", "iw_out", "iw_up", "iw_down", "image_norm", "image_heads", "image_mixed", "image_normed",
    "image_mean", "sums", "own", "images", "own_factors", "held_factors", "own_sums", "all_sums", "save_sems",
    "tok_sem", "local", "sends", "recvs", "factor_local", "factor_sends", "factor_recvs", "image_sends",
    "image_recvs", "pass_sends", "pass_recvs", "sum_sends", "sum_recvs",
)


def forward_joined_kernel(*refs):
    saves = tuple(name + "_out" for name in saved_names)
    names = text_ins + image_ins + saves + ("embed_grad", "loss") + text_names + text_scratch + image_scratch
    t = TextForward(names, refs)
    place = Place()
    place.greet()
    load_images = pltpu.make_async_copy(t.image_hbm, t.image_tok, t.tok_sem.at[0])
    load_images.start()
    save = {
        name: pltpu.make_async_copy(getattr(t, name), getattr(t, name + "_out"), t.save_sems.at[i])
        for i, name in enumerate(saved_names)
    }
    shards = (
        (t.image_qkv_hbm, t.iw_qkv), (t.image_out_hbm, t.iw_out), (t.image_up_hbm, t.iw_up),
        (t.image_down_hbm, t.iw_down),
    )
    qkv, out, up, down = (
        Gather(place, *pair, t.local.at[i], t.sends.at[i], t.recvs.at[i]) for i, pair in enumerate(shards)
    )
    factors = RowFactors(
        place, t.own_factors, t.held_factors, t.factor_local.at[0], t.factor_sends, t.factor_recvs
    )
    t.prepare()
    place.meet()
    qkv.start()
    out.start()
    t.attention()
    save["heads"].start()
    save["mixed"].start()
    qkv.share()
    out.share()
    up.start()
    t.middle()
    save["mid"].start()
    t.feed()
    save["slope"].start()
    t.finish()
    save["hidden"].start()
    save["projected"].start()
    inner_step, width_step = t.wide // place.rows, t.width // place.rows
    pooled = t.pooled[...]
    for row in range(place.rows):
        block = pooled[:, row * width_step : (row + 1) * width_step]
        spare = t.own_factors.shape[2] - inner_step - width_step
        t.own_factors[row, :, :inner_step] = t.inner_sum[:, row * inner_step : (row + 1) * inner_step]
        t.own_factors[row, :, inner_step:] = jnp.concatenate([block, jnp.zeros((t.captions, spare), bf16)], axis=1)
    factors.start()
    qkv.relay()
    out.relay()
    qkv.finish()
    out.finish()
    load_images.wait()

    rows, width = t.image_tok.shape
    group_rows = t.image_norm.shape[0]
    groups = rows // group_rows
    group_images = group_rows // IMG_TOK

    @pl.loop(0, groups)
    def _(group):
        span = pl.ds(pl.multiple_of(group * group_rows, 16), group_rows)
        normed2, mean = image_mix(
            t.image_tok[span, :], t.image_gain, t.image_bias, t.iw_qkv, t.iw_out,
            t.image_norm, t.image_heads, t.image_mixed,
        )
        t.image_normed[span, :] = normed2
        t.image_mean[pl.ds(pl.multiple_of(group * group_images, 8), group_images), :] = mean

        @pl.when(group == 0)
        def _():
            up.share()
            down.start()

        @pl.when(group == 2)
        def _():
            up.relay()
            down.share()

    factors.share()
    up.finish()

    halves, _, chips, half_images, _ = t.images.shape
    half_rows = half_images * IMG_TOK
    chip = place.row * 2 + place.x

    def image_copy(half, distance):
        other = (chip + distance) % chips
        mine = t.images.at[half, place.k, chip]
        sems = t.image_sends.at[half, distance - 1], t.image_recvs.at[half, distance - 1]
        return remote(mine, mine, *sems, (other // 2, other % 2 * 2 + place.k))

    def pass_copy(half):
        held = t.images.at[half, place.k]
        return remote(held, held, t.pass_sends.at[half], t.pass_recvs.at[half], place.at(k=1 - place.k))

    select = group_mean(half_images, half_rows)
    for half in range(halves):

        @wide_steps(t.wide)
        def _(columns):
            total = 0.0
            for group in range(half_rows // group_rows):
                local = slice(group * group_rows, (group + 1) * group_rows)
                at = half * half_rows + group * group_rows
                inner = gelu(dot_nn(t.image_normed[at : at + group_rows, :], t.iw_up[:, columns])).astype(bf16)
                total = total + dot_nn(select[:, local], inner)
            t.sums[:, columns] = total

        if half == 0:
            down.relay()
            factors.relay()
            down.finish()
        else:
            pl.loop(1, chips)(lambda distance: image_copy(half - 1, distance).wait())
            pass_copy(half - 1).start()
        high, low = split_low(t.sums[...] * (1.0 / IMG_TOK))
        pooled = dot_nn(jnp.concatenate([high, low], axis=0), t.iw_down[...])
        part = slice(half * half_images, (half + 1) * half_images)
        pooled = t.image_mean[part, :] + pooled[:half_images] + pooled[half_images:]
        embed = pooled * lax.rsqrt(jnp.sum(pooled * pooled, axis=-1, keepdims=True) + norm_eps)
        t.own[part, :] = embed.astype(bf16)
        t.images[half, place.k, chip] = embed.astype(bf16)
        pl.loop(1, chips)(lambda distance: image_copy(half, distance).start())

    factors.finish()
    save["held_factors"].start()
    pl.loop(1, chips)(lambda distance: image_copy(halves - 1, distance).wait())
    pass_copy(halves - 1).start()
    for half in range(halves):
        pass_copy(half).wait()

    images = t.images[...].reshape(-1, width)
    own = t.own[...].astype(f32)
    lifted = jnp.exp2(dot_nt(t.text_embed[...], images) * (logit_scale * log2e))
    t.own_sums[...] = jnp.sum(lifted, axis=0, keepdims=True)
    t.all_sums[place.slot] = t.own_sums[...]
    sums = Exchange(place, lambda to: t.own_sums, t.all_sums, t.sum_sends, t.sum_recvs)
    sums.start()
    col_sums = jnp.sum(lifted, axis=1, keepdims=True)
    positives = logit_scale * jnp.sum(own * t.text_embed[...].astype(f32), axis=(0, 1), keepdims=True)
    sums.finish()
    row_sums = jnp.sum(t.all_sums[...], axis=0)
    sim_grad = (0.5 * (lifted * (1.0 / row_sums) + lifted * (1.0 / col_sums))).astype(bf16)
    t.embed_grad[...] = logit_scale * (dot_nn(sim_grad, images) - own)
    logs = jnp.sum(jnp.log(col_sums), axis=(0, 1), keepdims=True)
    logs = logs + jnp.sum(jnp.log(row_sums), axis=(0, 1), keepdims=True) * (1.0 / place.count)
    t.loss[...] = jnp.broadcast_to(0.5 * logs - positives, t.loss.shape)
    for copy in save.values():
        copy.wait()


def whole(shape):
    return pl.BlockSpec(shape, lambda *_: (0,) * len(shape))


in_vmem = pl.BlockSpec(memory_space=pltpu.VMEM)
in_smem = pl.BlockSpec(memory_space=pltpu.SMEM)
anywhere = pl.BlockSpec(memory_space=pl.ANY)


def plain(kernel, outs, ins, scratch, name, out_specs=None, **settings):
    return pl.pallas_call(
        kernel,
        out_shape=outs,
        in_specs=ins,
        out_specs=out_specs or [in_vmem] * len(outs),
        scratch_shapes=scratch,
        compiler_params=pltpu.CompilerParams(vmem_limit_bytes=VMEM_LIMIT, **settings),
        name=name,
    )


def array(shape, dtype):
    return jax.ShapeDtypeStruct(shape, dtype)


def partners(x, col_count):
    order = [(i, i ^ 2) for i in range(col_count)]
    near = [(i, i ^ 1) for i in range(col_count)]
    far = lax.ppermute(x, "col", order)
    return [x, lax.ppermute(x, "col", near), far, lax.ppermute(far, "col", near)]


def body(
    image_tokens, image_norm_gain, image_norm_bias, image_qkv, image_out, image_up, image_down,
    text_tokens, text_lengths, norm1_gain, norm1_bias, norm2_gain, norm2_bias,
    text_qkv, text_out, text_up, text_down, text_proj,
):
    tokens, width = text_tokens.shape
    captions = text_lengths.shape[0]
    length = tokens // captions
    wide = text_up.shape[1]
    row_count, col_count = lax.axis_size("row"), lax.axis_size("col")
    row, col = lax.axis_index("row"), lax.axis_index("col")
    pair_total = captions * row_count * col_count
    image_rows, images = image_tokens.shape[0], image_tokens.shape[0] // IMG_TOK

    count = row_count * col_count
    joined = (row_count, col_count) == (8, 4)
    vectors = (norm1_gain, norm1_bias, norm2_gain, norm2_bias)
    weights = (text_qkv, text_out, text_up, text_down, text_proj)
    weight_scratch = [pltpu.VMEM(w.shape, bf16) for w in weights]

    text_shapes = (
        array((tokens, width), bf16),
        array((captions, width), bf16),
        array((captions, width), f32),
        array((captions, width), bf16),
        array((captions, wide), bf16),
        array((tokens, 3 * width), bf16),
        array((tokens, width), bf16),
        array((tokens, width), f32),
        array((tokens, wide), bf16),
    )
    text_specs = [in_vmem, in_smem] + [in_vmem] * 4 + [anywhere] * 5
    text_buffers = weight_scratch + [
        pltpu.VMEM((tokens, width), bf16),
        pltpu.VMEM((tokens, wide), bf16),
        pltpu.VMEM((captions, 1), jnp.int32),
        pltpu.VMEM((1, tokens), f32),
        pltpu.SemaphoreType.DMA((5,)),
    ]
    text_in = (text_tokens, text_lengths, *vectors, *weights)
    groups = 4
    group_rows, group_images = image_rows // groups, images // groups
    mix_buffers = [
        pltpu.VMEM((group_rows, width), bf16),
        pltpu.VMEM((group_rows, 3 * width), bf16),
        pltpu.VMEM((group_rows, width), bf16),
    ]
    mix_weights = [pltpu.VMEM((width, 3 * width), bf16), pltpu.VMEM((width, width), bf16)]
    embed_weights = [pltpu.VMEM((width, wide), bf16), pltpu.VMEM((wide, width), bf16)]
    both = ("row", "col")

    if joined:
        chips, halves = count // 2, 2
        packed = -(-(wide // row_count + width // row_count) // 128) * 128
        shapes = dict(zip(text_names, text_shapes))
        shapes["held_factors"] = array((col_count, row_count, captions, packed), bf16)
        dma = pltpu.SemaphoreType.DMA
        hidden, projected, heads, mixed, mid, slope, factors, embed_grad, loss_part = plain(
            forward_joined_kernel,
            tuple(shapes[name] for name in saved_names) + (array((captions, width), f32), array((1, 128), f32)),
            text_specs + [anywhere, in_vmem, in_vmem] + [anywhere] * 4,
            [pltpu.VMEM(shape.shape, shape.dtype) for shape in text_shapes]
            + text_buffers
            + [pltpu.VMEM((image_rows, width), bf16)]
            + mix_weights
            + embed_weights
            + mix_buffers
            + [
                pltpu.VMEM((image_rows, width), bf16),
                pltpu.VMEM((images, width), f32),
                pltpu.VMEM((images // halves, wide), f32),
                pltpu.VMEM((images, width), bf16),
                pltpu.VMEM((halves, 2, chips, images // halves, width), bf16),
                pltpu.VMEM((row_count, captions, packed), bf16),
                pltpu.VMEM((col_count, row_count, captions, packed), bf16),
                pltpu.VMEM((1, pair_total), f32),
                pltpu.VMEM((count, 1, pair_total), f32),
                dma((len(saved_names),)),
                dma((1,)),
                dma((4,)),
                dma((4, 5)),
                dma((4, 5)),
                dma((1,)),
                dma((row_count + 2,)),
                dma((row_count + 2,)),
                dma((halves, chips - 1)),
                dma((halves, chips - 1)),
                dma((halves,)),
                dma((halves,)),
                dma((count - 1,)),
                dma((count - 1,)),
            ],
            "forward_joined",
            out_specs=[anywhere] * len(saved_names) + [in_vmem] * 2,
            collective_id=1,
            has_side_effects=True,
        )(*text_in, image_tokens, image_norm_gain, image_norm_bias, image_qkv, image_out, image_up, image_down)
    else:
        (hidden, text_embed, projected, pooled, inner_sum, heads, mixed, mid, slope) = plain(
            text_forward_kernel, text_shapes, text_specs, text_buffers, "text_forward"
        )(*text_in)
        qkv_parts = partners(image_qkv, col_count)
        out_parts = partners(image_out, col_count)
        up_parts = partners(image_up, col_count)
        down_parts = partners(image_down, col_count)
        parts = [anywhere] * (2 * col_count)
        image_normed, image_mean = pl.pallas_call(
            functools.partial(image_mix_kernel, col_count),
            grid=(groups,),
            out_shape=(array((image_rows, width), bf16), array((images, width), f32)),
            in_specs=[
                pl.BlockSpec((group_rows, width), lambda i: (i, 0)),
                whole(image_norm_gain.shape),
                whole(image_norm_bias.shape),
            ]
            + parts,
            out_specs=(
                pl.BlockSpec((group_rows, width), lambda i: (i, 0)),
                pl.BlockSpec((group_images, width), lambda i: (i, 0)),
            ),
            scratch_shapes=mix_weights + mix_buffers + [pltpu.SemaphoreType.DMA((2, col_count))],
            compiler_params=pltpu.CompilerParams(vmem_limit_bytes=VMEM_LIMIT),
            name="image_mix",
        )(image_tokens, image_norm_gain, image_norm_bias, *qkv_parts, *out_parts)
        image_embed = pl.pallas_call(
            functools.partial(image_embed_kernel, col_count),
            grid=(groups,),
            out_shape=array((images, width), bf16),
            in_specs=[pl.BlockSpec((group_rows, width), lambda i: (i, 0)), whole((images, width))] + parts,
            out_specs=whole((images, width)),
            scratch_shapes=embed_weights
            + [pltpu.VMEM((images, wide), f32), pltpu.SemaphoreType.DMA((2, col_count))],
            compiler_params=pltpu.CompilerParams(vmem_limit_bytes=VMEM_LIMIT),
            name="image_embed",
        )(image_normed, image_mean, *up_parts, *down_parts)

        image_all = lax.all_gather(image_embed, both, axis=0, tiled=True)
        lifted = jnp.exp(logit_scale * dot_nt(image_all, text_embed))
        row_sums = lax.psum(jnp.sum(lifted, axis=1), both)
        col_sums = jnp.sum(lifted, axis=0)
        sim_grad = (0.5 * (lifted / row_sums[:, None] + lifted / col_sums[None, :])).astype(bf16)
        image_own = image_embed.astype(f32)
        embed_grad = logit_scale * (dot_tn(sim_grad, image_all) - image_own)
        positives = logit_scale * jnp.sum(image_own * text_embed.astype(f32), axis=1)
        loss_part = 0.5 * jnp.sum(jnp.log(col_sums) - 2.0 * positives)
        loss_part = loss_part + 0.5 * jnp.sum(jnp.log(row_sums)) / count

    backward_in = (text_lengths, *vectors, embed_grad, projected, text_tokens, heads, mixed, mid, slope, *weights)
    backward_specs = [in_smem] + [in_vmem] * 6 + [anywhere] * 10
    backward_buffers = (
        [
            pltpu.VMEM((tokens, width), bf16),
            pltpu.VMEM((tokens, 3 * width), bf16),
            pltpu.VMEM((tokens, width), bf16),
            pltpu.VMEM((tokens, width), f32),
            pltpu.VMEM((tokens, wide), bf16),
        ]
        + weight_scratch
        + [
            pltpu.VMEM((tokens, width), bf16),
            pltpu.VMEM((width, tokens), bf16),
            pltpu.VMEM((tokens, width), f32),
            pltpu.VMEM((tokens, width), f32),
            pltpu.VMEM((tokens, width), bf16),
            pltpu.VMEM((tokens, width), bf16),
            pltpu.VMEM((tokens, 3 * width), bf16),
            pltpu.VMEM((captions, 1), jnp.int32),
            pltpu.VMEM((1, tokens), f32),
            pltpu.VMEM((tokens, 1), f32),
            pltpu.SemaphoreType.DMA((10,)),
        ]
    )

    def by_row(x):
        x = lax.all_to_all(x, "row", split_axis=1, concat_axis=0, tiled=True)
        return lax.all_gather(x, "col", axis=0, tiled=True)

    def by_col(x):
        x = lax.all_gather(x, "row", axis=0, tiled=True)
        return lax.all_to_all(x, "col", split_axis=1, concat_axis=0, tiled=True)

    if joined:
        out_step, inner_step = width // col_count, wide // row_count
        rows = width // row_count
        up_grad, out_grad, qkv_grad, grad_down, grad_proj, input_grad, norm_total = plain(
            text_backward_joined_kernel,
            (
                array((rows, wide // col_count), f32),
                array((rows, out_step), f32),
                array((rows, 3 * out_step), f32),
                array((inner_step, out_step), f32),
                array((rows, out_step), f32),
                array((tokens, width), bf16),
                array((1, 4 * width + 128), f32),
            ),
            backward_specs + [in_vmem] * 2,
            backward_buffers
            + scatter_scratch(rows, wide // col_count)
            + scatter_scratch(rows, 4 * out_step)
            + [
                pltpu.VMEM((captions, width), bf16),
                pltpu.VMEM((8, width), f32),
                pltpu.VMEM((col_count, captions, 2 * out_step), bf16),
                pltpu.VMEM((count, captions, 2 * out_step), bf16),
                pltpu.SemaphoreType.DMA((count - 1,)),
                pltpu.SemaphoreType.DMA((count - 1,)),
                pltpu.VMEM((1, 2 * width + 128), f32),
                pltpu.VMEM((count, 1, 2 * width + 128), f32),
                pltpu.SemaphoreType.DMA((count - 1,)),
                pltpu.SemaphoreType.DMA((count - 1,)),
                pltpu.VMEM((1, 2 * width), f32),
                pltpu.VMEM((count, 1, 2 * width), f32),
                pltpu.SemaphoreType.DMA((count - 1,)),
                pltpu.SemaphoreType.DMA((count - 1,)),
            ],
            "text_backward_joined",
            collective_id=3,
            has_side_effects=True,
        )(*backward_in, factors, loss_part)
        norm_total = norm_total[0]
        norms = [norm_total[i * width : (i + 1) * width] for i in range(4)]
        loss_total = norm_total[4 * width]
    else:
        (proj_grad, branch, up_grad, out_grad, qkv_grad, input_grad, norm_grads) = plain(
            text_backward_kernel,
            (
                array((captions, width), bf16),
                array((captions, width), bf16),
                array((col_count, width, wide // col_count), bf16),
                array((col_count, width, width // col_count), bf16),
                array((col_count, width, 3 * width // col_count), bf16),
                array((tokens, width), bf16),
                array((8, width), f32),
            ),
            backward_specs,
            backward_buffers,
            "text_backward",
        )(*backward_in)

        def scattered(matrix):
            blocks = matrix.reshape(count, width // row_count, matrix.shape[2])
            return lax.psum_scatter(blocks, ("col", "row"), scatter_dimension=0, tiled=True)[0].astype(f32)

        up_grad, out_grad, qkv_grad = scattered(up_grad), scattered(out_grad), scattered(qkv_grad)
        grad_down = dot_tn(by_row(inner_sum), by_col(branch))
        grad_proj = dot_tn(by_row(pooled), by_col(proj_grad))
        loss_total, norm_total = lax.psum((loss_part, norm_grads), both)
        norms = [norm_total[i] for i in range(4)]
    mean_loss = loss_total / pair_total
    return (
        mean_loss, hidden, input_grad, *norms, qkv_grad, out_grad, up_grad, grad_down, grad_proj,
    )


def solution(mesh):
    split = P(("row", "col"), None)
    grid = P("row", "col")
    in_specs = (
        split, P(), P(), P("col", None), P("col", None), P("col", None), P("col", None), split, P(("row", "col")),
    ) + (P(),) * 9
    out_specs = (P(), split, split, P(), P(), P(), P(), grid, grid, grid, grid, grid)
    return jax.shard_map(body, mesh=mesh, in_specs=in_specs, out_specs=out_specs, check_vma=False)
```

time: 283 us -> 203 us (0.72)
  Pallas kernels: 268 us -> 192 us
    pallas_call x2 -> x1, Pallas kernels: 167 us -> 108 us  [body(): plain(forward_joined_kernel, tuple((shapes[name] for name in saved_names)...]
    pallas_call x1, Pallas kernels: 101 us -> 83.6 us  [body(): plain(text_backward_joined_kernel, (array((rows, wide // col_count), f32)...]
where the time goes in v4:
time: 203 us
  Pallas kernels  192 us (95%)
  local copies, waits for them, and re-layouts  8.9 us (4%)
  between operations  2.49 us (1%)
    pallas_call x1, Pallas kernels, body(): plain(forward_joined_kernel, tuple((shapes[name] for name in saved_names)...  108 us
    pallas_call x1, Pallas kernels, body(): plain(text_backward_joined_kernel, (array((rows, wide // col_count), f32)...  83.6 us
    unnamed x19, local copies, waits for them, and re-layouts  6.33 us

profile of v4, /device:TPU:0, one launch (start us, length us, event | category | flops | bytes accessed | tf_op | source)
XLA Modules:
  0.0 203.0 jit_solution(15300331077624877740)
XLA Ops:
  0.6 108.0 %forward_joined.1 = (bf16[512,768]{1,0:T(8,128)(2,1)}, f32[32,768]{1,0:T(8,128)}, bf16[512,2304]{1,0:T(8,128)(2,1)}, bf16[512,768]{1,0:T(8,128)(2,1)}, f32[512,7...) custom-call(bf16[512,768]{1,0:T(8,128)(2,1)} %refs_7_.3, ...), custom_call_target="tpu_custom_call" | custom-call | tf_op jit(solution)/shard_map/forward_joined/pallas_call | solution.py:1149
  108.6 0.0 copy-start
  108.6 83.6 %text_backward_joined.1 = (f32[96,768]{1,0:T(8,128)}, f32[96,192]{1,0:T(8,128)}, f32[96,576]{1,0:T(8,128)}, f32[384,192]{1,0:T(8,128)}, f32[96,192]{1,0:T(8,128)...) custom-call(s32[32]{0:T(128)} %refs_0_.3, f32[768]{0:T(1024)} %refs_1_.3, f32[768]{0:T(1024)} %refs_2_.3, f32[768]{0:T(1024)} %refs_3_.3, ...), custom_call_target="tpu_custom_call" | custom-call | tf_op jit(solution)/shard_map/text_backward_joined/pallas_call | solution.py:1276
  192.3 0.0 copy-start.1
  192.3 0.0 copy-start.3
  192.3 0.0 copy-start.5
  192.3 0.0 copy-start.2
  192.3 1.2 slice.28
  194.2 1.3 slice_reduce_fusion
  195.5 1.9 copy.30
  197.4 0.0 copy-done
  197.4 0.0 copy-start.4
  197.4 0.9 copy.37
  198.3 0.0 copy-done.1
  198.3 0.9 copy.38
  199.2 0.0 copy-done.3
  199.2 0.7 copy.39
  199.8 0.0 copy-done.5
  199.8 0.6 copy.40
  200.5 0.0 copy-done.2
  200.5 0.7 copy.41
  201.2 0.0 copy-done.4
  201.2 0.6 copy.42
Async XLA Ops:
  108.6 88.8 %copy-start = (bf16[512,768]{1,0:T(8,128)(2,1)S(1)}, bf16[512,768]{1,0:T(8,128)(2,1)}, u32[]{:S(2)}) copy-start(bf16[512,768]{1,0:T(8,128)(2,1)} %get-tuple-element.73) | copy-start | bytes 2359300
  192.3 6.0 %copy-start.1 = (bf16[512,768]{1,0:T(8,128)(2,1)S(1)}, bf16[512,768]{1,0:T(8,128)(2,1)}, u32[]{:S(2)}) copy-start(bf16[512,768]{1,0:T(8,128)(2,1)} %get-tuple-element.74) | copy-start | bytes 2359300
  192.3 6.9 %copy-start.3 = (f32[96,576]{1,0:T(8,128)S(1)}, f32[96,576]{1,0:T(8,128)}, u32[]{:S(2)}) copy-start(f32[96,576]{1,0:T(8,128)} %get-tuple-element.79) | copy-start | bytes 663556
  192.3 7.6 %copy-start.5 = (f32[96,192]{1,0:T(8,128)S(1)}, f32[96,192]{1,0:T(8,128)}, u32[]{:S(2)}) copy-start(f32[96,192]{1,0:T(8,128)} %get-tuple-element.80) | copy-start | bytes 221188
  192.3 8.2 %copy-start.2 = (f32[96,768]{1,0:T(8,128)S(1)}, f32[96,768]{1,0:T(8,128)}, u32[]{:S(2)}) copy-start(f32[96,768]{1,0:T(8,128)} %get-tuple-element.81) | copy-start | bytes 884740
  197.4 3.8 %copy-start.4 = (f32[96,192]{1,0:T(8,128)S(1)}, f32[96,192]{1,0:T(8,128)}, u32[]{:S(2)}) copy-start(f32[96,192]{1,0:T(8,128)} %get-tuple-element.83) | copy-start | bytes 221188
